TPU v7x, 32 devices: a whole 2x2x4 slice. The times are simulated.
32 devices in a mesh: dp: 4 (over y, x), seq: 8 (over z, core).
Axes of the slice: x: 2, y: 2, z: 4, core: 2. Of those that a mesh axis runs over, the one named last changes fastest.
Arguments:
- tokens: bfloat16 [8192, 1024], P(('dp', 'seq')), may hold values from -6 to 6
- lengths: int32 [4, 4], P('dp'), may hold values from 1 to 1793, 2048 in all within a row
- attn_gain: float32 [1024], replicated, may hold values from 0.5 to 1.5
- w_query: bfloat16 [1024, 1024], replicated, may hold values from -0.1875 to 0.1875
- w_key: bfloat16 [1024, 512], replicated, may hold values from -0.1875 to 0.1875
- w_value: bfloat16 [1024, 512], replicated, may hold values from -0.1875 to 0.1875
- query_gain: float32 [64], replicated, may hold values from 1 to 2
- key_gain: float32 [64], replicated, may hold values from 1 to 2
- w_out: bfloat16 [1024, 1024], replicated, may hold values from -0.75 to 0.75
- ffn_gain: float32 [1024], replicated, may hold values from 0.5 to 1.5
- w_gate: bfloat16 [1024, 4608], replicated, may hold values from -0.1875 to 0.1875
- w_up: bfloat16 [1024, 4608], replicated, may hold values from -0.1875 to 0.1875
- w_down: bfloat16 [4608, 1024], replicated, may hold values from -0.09375 to 0.09375
- cotangent: bfloat16 [8192, 1024], P(('dp', 'seq')), may hold values from -6 to 6
Outputs:
- mixed: bfloat16 [8192, 1024], P(('dp', 'seq'))
- grad_tokens: float32 [8192, 1024], P(('dp', 'seq'))
- grad_attn_gain: float32 [1024], replicated
- grad_w_query: float32 [1024, 1024], P(('dp', 'seq'))
- grad_w_key: float32 [1024, 512], P(('dp', 'seq'))
- grad_w_value: float32 [1024, 512], P(('dp', 'seq'))
- grad_query_gain: float32 [64], replicated
- grad_key_gain: float32 [64], replicated
- grad_w_out: float32 [1024, 1024], P(('dp', 'seq'))
- grad_ffn_gain: float32 [1024], replicated
- grad_w_gate: float32 [1024, 4608], P(('dp', 'seq'))
- grad_w_up: float32 [1024, 4608], P(('dp', 'seq'))
- grad_w_down: float32 [4608, 1024], P(('dp', 'seq'))
Inputs may be any that keep to these rules, and one draw needn't show every extreme that they name: Each row holds the lengths of the 4 sequences packed in slot order into one data position's 2048 tokens; they sum to 2048 and the largest is exactly 1793.
All inputs are finite; a program needn't handle non-finite values.
Results may differ from a plain program's by a relative error of at most 0.015.
Values may be sent and summed in bfloat16 or wider, within the bound.
No kernel may reach another device: no remote copies, remote signals or barrier semaphores. Data moves between devices by JAX's collectives and lax.ppermute only.
A program may use at most 256 MiB of HBM per device.

v0:
```python
import jax
import jax.numpy as jnp
from jax import lax
from jax.sharding import PartitionSpec as P

EPSILON = 1e-05
ROPE_BASE = 1000000.0


def rms_scale(field, gain_vec):
    return field * lax.rsqrt(jnp.mean(field * field, axis=-1, keepdims=True) + EPSILON) * gain_vec


def seg_info(tok_index, seq_lengths):
    seq_ends = jnp.cumsum(seq_lengths)
    seq_starts = seq_ends - seq_lengths
    inside = (tok_index[:, None] >= seq_starts[None, :]) & (tok_index[:, None] < seq_ends[None, :])
    slot_ids = jnp.arange(seq_lengths.shape[0], dtype=jnp.int32)
    segment = jnp.sum(jnp.where(inside, slot_ids[None, :], 0), axis=1)
    offset = jnp.sum(jnp.where(inside, seq_starts[None, :], 0), axis=1)
    return (segment, tok_index - offset)


def rope_tables(position, head_size):
    half_size = head_size // 2
    freqs = ROPE_BASE ** (-2.0 * jnp.arange(half_size, dtype=jnp.float32) / head_size)
    angles = position.astype(jnp.float32)[:, None] * freqs[None, :]
    angles = jnp.concatenate([angles, angles], axis=1)
    return (jnp.cos(angles), jnp.sin(angles))


def rotate(field, cosine, sine):
    half_size = field.shape[-1] // 2
    turned = jnp.concatenate([-field[..., half_size:], field[..., :half_size]], axis=-1)
    return field * cosine[:, None, :] + turned * sine[:, None, :]


def normed_rotated(query_raw, key_raw, query_scale, key_scale, cosine, sine):
    head_size = query_scale.shape[0]
    tok_rows = query_raw.shape[0]
    queries = rms_scale(query_raw.reshape(tok_rows, -1, head_size), query_scale)
    key_rows = rms_scale(key_raw.reshape(tok_rows, -1, head_size), key_scale)
    return (
        rotate(queries, cosine, sine).reshape(tok_rows, -1),
        rotate(key_rows, cosine, sine).reshape(tok_rows, -1),
    )


def tokens_dot(left, right):
    return lax.dot_general(
        left, right, (((0,), (0,)), ((), ())), preferred_element_type=jnp.float32
    )


def back_dot(grad_rows, weight):
    return lax.dot_general(
        grad_rows, weight, (((1,), (1,)), ((), ())), preferred_element_type=jnp.float32
    )


def block_count(group_rows):
    block_total = max(1, group_rows // 512)
    while group_rows % block_total:
        block_total = block_total - 1
    return block_total


def block_mask(segment, tok_index, row_start, block_rows):
    row_ids = lax.dynamic_slice_in_dim(tok_index, row_start, block_rows, 0)
    row_segments = lax.dynamic_slice_in_dim(segment, row_start, block_rows, 0)
    return (row_segments[:, None] == segment[None, :]) & (tok_index[None, :] <= row_ids[:, None])


def block_scores(query_block, key_rows, keep_mask, score_scale):
    raw_scores = (
        jnp.einsum("qgrd,kgd->grqk", query_block, key_rows, preferred_element_type=jnp.float32)
        * score_scale
    )
    return jnp.where(keep_mask[None, None], raw_scores, -1e30)


def attend_forward(queries, key_rows, value_rows, segment, tok_index, score_scale, block_total):
    group_rows = key_rows.shape[0]
    block_rows = group_rows // block_total

    def one_block(block_id):
        row_start = block_id * block_rows
        query_block = lax.dynamic_slice_in_dim(queries, row_start, block_rows, 0)
        scores = block_scores(
            query_block,
            key_rows,
            block_mask(segment, tok_index, row_start, block_rows),
            score_scale,
        )
        row_max = jnp.max(scores, axis=-1, keepdims=True)
        exp_terms = jnp.exp(scores - row_max)
        row_total = jnp.sum(exp_terms, axis=-1, keepdims=True)
        weights = (exp_terms / row_total).astype(jnp.bfloat16)
        attended = jnp.einsum(
            "grqk,kgd->qgrd", weights, value_rows, preferred_element_type=jnp.float32
        )
        return (attended.astype(jnp.bfloat16), (row_max + jnp.log(row_total))[..., 0])

    blocks_out, log_totals = lax.map(one_block, jnp.arange(block_total, dtype=jnp.int32))
    return (blocks_out.reshape(queries.shape), log_totals)


def attend_backward(
    queries,
    key_rows,
    value_rows,
    grad_out,
    log_totals,
    segment,
    tok_index,
    score_scale,
    block_total,
):
    group_rows = key_rows.shape[0]
    block_rows = group_rows // block_total

    def one_block(run_sums, inputs):
        grad_keys, grad_values = run_sums
        block_id, log_total = inputs
        row_start = block_id * block_rows
        query_block = lax.dynamic_slice_in_dim(queries, row_start, block_rows, 0)
        grad_block = lax.dynamic_slice_in_dim(grad_out, row_start, block_rows, 0)
        scores = block_scores(
            query_block,
            key_rows,
            block_mask(segment, tok_index, row_start, block_rows),
            score_scale,
        )
        weights = jnp.exp(scores - log_total[..., None])
        low_weights = weights.astype(jnp.bfloat16)
        grad_values = grad_values + jnp.einsum(
            "grqk,qgrd->kgd", low_weights, grad_block, preferred_element_type=jnp.float32
        )
        grad_weights = jnp.einsum(
            "qgrd,kgd->grqk", grad_block, value_rows, preferred_element_type=jnp.float32
        )
        row_inner = jnp.sum(weights * grad_weights, axis=-1, keepdims=True)
        grad_scores = (weights * (grad_weights - row_inner)).astype(jnp.bfloat16)
        grad_query = (
            jnp.einsum("grqk,kgd->qgrd", grad_scores, key_rows, preferred_element_type=jnp.float32)
            * score_scale
        )
        grad_keys = (
            grad_keys
            + jnp.einsum(
                "grqk,qgrd->kgd", grad_scores, query_block, preferred_element_type=jnp.float32
            )
            * score_scale
        )
        return ((grad_keys, grad_values), grad_query)

    empty_sums = jnp.zeros(key_rows.shape, jnp.float32)
    (grad_keys, grad_values), grad_queries = lax.scan(
        one_block, (empty_sums, empty_sums), (jnp.arange(block_total, dtype=jnp.int32), log_totals)
    )
    return (grad_queries.reshape(queries.shape), grad_keys, grad_values)


def plain_pick():

    def picker(left):
        return left

    return picker


def split_columns(joined, widths):
    pieces = []
    begin = 0
    for width in widths:
        pieces.append(joined[:, begin : begin + width])
        begin = begin + width
    return pieces


def body(
    tokens,
    lengths,
    attn_gain,
    w_query,
    w_key,
    w_value,
    query_gain,
    key_gain,
    w_out,
    ffn_gain,
    w_gate,
    w_up,
    w_down,
    cotangent,
):
    tok_rows = tokens.shape[0]
    head_size = query_gain.shape[0]
    kv_total = w_key.shape[1] // head_size
    seq_parts = lax.axis_size("seq")
    group_rows = tok_rows * seq_parts
    local_groups = kv_total // seq_parts
    score_scale = head_size ** (-0.5)
    tok_index = jnp.arange(group_rows, dtype=jnp.int32)
    segment, position = seg_info(tok_index, lengths[0])
    own_position = lax.dynamic_slice_in_dim(position, lax.axis_index("seq") * tok_rows, tok_rows, 0)
    cosine, sine = rope_tables(own_position, head_size)
    block_total = block_count(group_rows)
    inputs = tokens.astype(jnp.float32)
    normed, first_back = jax.vjp(rms_scale, inputs, attn_gain)
    low_normed = normed.astype(jnp.bfloat16)
    query_raw = jnp.dot(low_normed, w_query, preferred_element_type=jnp.float32)
    key_raw = jnp.dot(low_normed, w_key, preferred_element_type=jnp.float32)
    value_low = jnp.dot(low_normed, w_value, preferred_element_type=jnp.float32).astype(
        jnp.bfloat16
    )

    def rotate_pair(query_in, key_in, query_scale, key_scale):
        return normed_rotated(query_in, key_in, query_scale, key_scale, cosine, sine)

    (query_turned, key_turned), turn_back = jax.vjp(
        rotate_pair, query_raw, key_raw, query_gain, key_gain
    )
    packed = jnp.concatenate(
        [
            query_turned.astype(jnp.bfloat16).reshape(tok_rows, kv_total, 2 * head_size),
            key_turned.astype(jnp.bfloat16).reshape(tok_rows, kv_total, head_size),
            value_low.reshape(tok_rows, kv_total, head_size),
        ],
        axis=2,
    )
    by_head = lax.all_to_all(packed, "seq", split_axis=1, concat_axis=0, tiled=True)
    query_heads = by_head[:, :, : 2 * head_size].reshape(group_rows, local_groups, 2, head_size)
    key_heads = by_head[:, :, 2 * head_size : 3 * head_size]
    value_heads = by_head[:, :, 3 * head_size :]
    attended, log_totals = attend_forward(
        query_heads, key_heads, value_heads, segment, tok_index, score_scale, block_total
    )
    by_token = lax.all_to_all(
        attended.reshape(group_rows, local_groups, 2 * head_size),
        "seq",
        split_axis=0,
        concat_axis=1,
        tiled=True,
    )
    heads_low = by_token.reshape(tok_rows, -1)
    middle = inputs + jnp.dot(heads_low, w_out, preferred_element_type=jnp.float32)
    normed_two, second_back = jax.vjp(rms_scale, middle, ffn_gain)
    low_two = normed_two.astype(jnp.bfloat16)
    gate = jnp.dot(low_two, w_gate, preferred_element_type=jnp.float32)
    up_proj = jnp.dot(low_two, w_up, preferred_element_type=jnp.float32)
    sigmoid_gate = jax.nn.sigmoid(gate)
    activated = (gate * sigmoid_gate * up_proj).astype(jnp.bfloat16)
    mixed = (middle + jnp.dot(activated, w_down, preferred_element_type=jnp.float32)).astype(
        jnp.bfloat16
    )
    grad_act = back_dot(cotangent, w_down)
    grad_gate = (grad_act * up_proj * sigmoid_gate * (1.0 + gate * (1.0 - sigmoid_gate))).astype(
        jnp.bfloat16
    )
    grad_up = (grad_act * gate * sigmoid_gate).astype(jnp.bfloat16)
    grad_normed_two = back_dot(grad_gate, w_gate) + back_dot(grad_up, w_up)
    grad_middle_part, grad_fgain = second_back(grad_normed_two)
    grad_middle = cotangent.astype(jnp.float32) + grad_middle_part
    grad_attn_low = grad_middle.astype(jnp.bfloat16)
    grad_heads = back_dot(grad_attn_low, w_out).astype(jnp.bfloat16)
    grad_by_head = lax.all_to_all(
        grad_heads.reshape(tok_rows, kv_total, 2 * head_size),
        "seq",
        split_axis=1,
        concat_axis=0,
        tiled=True,
    )
    grad_queries, grad_keys, grad_values = attend_backward(
        query_heads,
        key_heads,
        value_heads,
        grad_by_head.reshape(group_rows, local_groups, 2, head_size),
        log_totals,
        segment,
        tok_index,
        score_scale,
        block_total,
    )
    grad_packed = jnp.concatenate(
        [
            grad_queries.astype(jnp.bfloat16).reshape(group_rows, local_groups, 2 * head_size),
            grad_keys.astype(jnp.bfloat16),
            grad_values.astype(jnp.bfloat16),
        ],
        axis=2,
    )
    grad_by_token = lax.all_to_all(grad_packed, "seq", split_axis=0, concat_axis=1, tiled=True)
    grad_turned_query = (
        grad_by_token[:, :, : 2 * head_size].reshape(tok_rows, -1).astype(jnp.float32)
    )
    grad_turned_key = (
        grad_by_token[:, :, 2 * head_size : 3 * head_size].reshape(tok_rows, -1).astype(jnp.float32)
    )
    grad_value_low = grad_by_token[:, :, 3 * head_size :].reshape(tok_rows, -1)
    grad_query_raw, grad_key_raw, grad_qgain, grad_kgain = turn_back(
        (grad_turned_query, grad_turned_key)
    )
    grad_query_low = grad_query_raw.astype(jnp.bfloat16)
    grad_key_low = grad_key_raw.astype(jnp.bfloat16)
    grad_normed = (
        back_dot(grad_query_low, w_query)
        + back_dot(grad_key_low, w_key)
        + back_dot(grad_value_low, w_value)
    )
    grad_input_part, grad_again = first_back(grad_normed)
    grad_inputs = grad_middle + grad_input_part
    gain_totals = lax.psum((grad_again, grad_qgain, grad_kgain, grad_fgain), ("dp", "seq"))
    right_inputs = jnp.concatenate([grad_query_low, grad_key_low, grad_value_low], axis=1)
    right_ffn = jnp.concatenate([grad_gate, grad_up], axis=1)
    picker = plain_pick()
    inside = lax.psum_scatter(
        jnp.concatenate(
            [
                tokens_dot(picker(low_normed), right_inputs),
                tokens_dot(picker(low_two), right_ffn),
                tokens_dot(picker(heads_low), grad_attn_low),
            ],
            axis=1,
        ),
        ("dp", "seq"),
        scatter_dimension=0,
        tiled=True,
    )
    down_share = lax.psum_scatter(
        tokens_dot(plain_pick()(activated), cotangent),
        ("dp", "seq"),
        scatter_dimension=0,
        tiled=True,
    )
    widths = [
        w_query.shape[1],
        w_key.shape[1],
        w_value.shape[1],
        w_gate.shape[1],
        w_up.shape[1],
        w_out.shape[1],
    ]
    share_q, share_k, share_v, share_g, share_u, share_o = split_columns(inside, widths)
    return (
        mixed,
        grad_inputs,
        gain_totals[0],
        share_q,
        share_k,
        share_v,
        gain_totals[1],
        gain_totals[2],
        share_o,
        gain_totals[3],
        share_g,
        share_u,
        down_share,
    )


def solution(mesh):
    in_specs = (
        P(("dp", "seq"), None),
        P("dp", None),
        P(),
        P(),
        P(),
        P(),
        P(),
        P(),
        P(),
        P(),
        P(),
        P(),
        P(),
        P(("dp", "seq"), None),
    )
    out_specs = (
        P(("dp", "seq"), None),
        P(("dp", "seq"), None),
        P(),
        P(("dp", "seq"), None),
        P(("dp", "seq"), None),
        P(("dp", "seq"), None),
        P(),
        P(),
        P(("dp", "seq"), None),
        P(),
        P(("dp", "seq"), None),
        P(("dp", "seq"), None),
        P(("dp", "seq"), None),
    )
    return jax.shard_map(body, mesh=mesh, in_specs=in_specs, out_specs=out_specs, check_vma=False)
```

profile of v0, /device:TPU:0, one launch (start us, length us, event | category | flops | bytes accessed | tf_op | source)
XLA Modules:
  0.0 1037.2 jit_solution(17899464785107545421)
XLA Ops:
  24.6 3.3 fusion.107
  44.4 6.9 all-to-all-start
  51.4 26.5 %all-to-all-done = bf16[256,8,256]{2,0,1:T(8,128)(2,1)S(1)} async-done(((bf16[256,8,256]{2,0,1:T(8,128)(2,1)}), bf16[256,8,256]{2,0,1:T(8,128)(2,1)S(1)}, u32[]{:S(2)}, u32[]{:S(2)}) %all-to-all-start) | async-done | bytes 1048608 | tf_op jit(solution)/shard_map/all_to_all | solution.py:232
  83.7 40.2 %while.29 = (s32[]{:T(128)}, bf16[4,512,1,2,64]{1,4,3,2,0:T(8,128)(2,1)}, f32[4,1,2,512]{3,2,1,0:T(2,128)S(1)}, s32[4]{0:T(128)S(1)}, s32[2048]{0:T(1024)S(1)}, ...) while((s32[]{:T(128)}, ...), condition=%wide.region_9.10_spmd.clone, body=%wide.region_6.9_spmd.clone.sunk | while | flops 565246976 | bytes 30208212 | solution.py:104
  90.4 3.3 fusion.174
  100.4 3.3 fusion.174
  110.5 3.3 fusion.174
  120.6 3.3 fusion.174
  124.8 3.6 copy.129
  128.3 5.1 reshape.492
  133.9 12.6 %reduce.3 = bf16[2048,128]{1,0:T(8,128)(2,1)S(1)} reduce(bf16[2048,1,128]{2,1,0:T(2,128)(2,1)} %reshape.492, bf16[]{:T(256)} %broadcast.355), dimensions={1}, to_apply=%reshape.492.reduce_sub_computation | reduce | bytes 1048578 | tf_op jit(solution)/shard_map/reshape;reshape | solution.py:240
  147.4 19.1 %all_to_all.66 = bf16[8,2,16384]{2,1,0:T(2,128)(2,1)S(1)} all-to-all(bf16[8,2,16384]{2,1,0:T(2,128)(2,1)} %reshape.493), channel_id=1, replica_groups=mesh['dp'=4,'seq'=8] {'seq'}, dimensions={0} | all-to-all | bytes 1048576 | tf_op jit(solution)/shard_map/all_to_all | solution.py:239
  172.7 8.4 fusion.116
  181.1 8.1 fusion.115
  189.2 14.2 %multiply_convert_fusion = (bf16[256,4608]{1,0:T(8,128)(2,1)S(1)}, bf16[256,4608]{1,0:T(8,128)(2,1)}, bf16[256,4608]{1,0:T(8,128)(2,1)}) fusion(f32[256,4608]{1,0:T(8,128)} %fusion.115, f32[256,4608]{1,0:T(8,128)} %fusion.116, bf16[256,1024]{1,0:T(8,128)(2,1)S(1)} %copy-done.27, bf16[4608,1024]{1,0:T(8,128)(2,1)} %param.30), kind=kOutput, calls=%fused_computation.68 | convolution fusion | flops 2434793472 | bytes 26476544 | tf_op jit(solution)/shard_map/dot_general | solution.py:56
  203.4 5.1 fusion.117
  208.6 6.1 multiply_reduce_fusion
  216.6 3.8 all-to-all-start.2
  220.5 3.7 fusion.89
  224.2 11.5 %all-to-all-done.2 = bf16[256,8,128]{2,0,1:T(8,128)(2,1)S(1)} async-done(((bf16[256,8,128]{2,0,1:T(8,128)(2,1)}), bf16[256,8,128]{2,0,1:T(8,128)(2,1)S(1)}, u32[]{:S(2)}, u32[]{:S(2)}) %all-to-all-start.2) | async-done | bytes 524320 | tf_op jit(solution)/shard_map/all_to_all | solution.py:267
  236.4 66.3 %while.30 = (s32[]{:T(128)}, f32[2048,1,64]{0,2,1:T(8,128)S(1)}, f32[2048,1,64]{0,2,1:T(8,128)}, bf16[4,512,1,2,64]{1,4,3,2,0:T(8,128)(2,1)}, s32[4]{0:T(128)S(1...) while((s32[]{:T(128)}, f32[2048,1,64]{0,2,1:T(8,128)S(1)}, ...), condition=%wide.region_14.15_spmd.clone.clone, body=%wide.region_12.14_spmd.clone.clone.sunk | while | flops 1377500160 | bytes 79225200 | solution.py:158
  308.9 3.6 all-to-all-start.3
  312.5 17.1 %fusion.62 = f32[1024,9216]{1,0:T(8,128)} fusion(bf16[256,1024]{1,0:T(8,128)(2,1)S(1)} %copy-done.16, bf16[256,4608]{1,0:T(8,128)(2,1)} %copy-done.24, bf16[256,4608]{1,0:T(8,128)(2,1)} %get-tuple-element.298), kind=kOutput, calls=%fused_computation.64 | convolution fusion | flops 4841275392 | bytes 42991616 | tf_op jit(solution)/shard_map/dot_general | solution.py:50
  329.6 9.4 all-to-all-done.3
  339.0 3.4 reshape.496
  348.8 4.7 fusion.79
  353.5 33.4 %pad_maximum_fusion = f32[1024,12288]{1,0:T(8,128)} fusion(f32[1024,1024]{1,0:T(8,128)} %fusion.89, f32[1024,9216]{1,0:T(8,128)} %fusion.62, f32[1024,2048]{1,0:T(8,128)} %fusion.79), kind=kLoop, calls=%fused_computation.63 | loop fusion | flops 25165824 | bytes 100663296 | tf_op jit(solution)/shard_map/concatenate | solution.py:318
  387.9 12.7 %fusion.119 = f32[4608,1024]{1,0:T(8,128)} fusion(bf16[256,4608]{1,0:T(8,128)(2,1)} %get-tuple-element.299, bf16[256,1024]{1,0:T(8,128)(2,1)S(1)} %copy-done.28), kind=kOutput, calls=%fused_computation.181 | convolution fusion | flops 2415919104 | bytes 21757952 | tf_op jit(solution)/shard_map/dot_general | solution.py:50
  402.1 10.2 fusion.66
  415.3 38.6 %all-reduce.4 = (f32[1024]{0:T(1024)}, f32[64]{0:T(128)}, f32[64]{0:T(128)}, f32[1024]{0:T(1024)}) all-reduce(f32[1024]{0:T(1024)S(1)} %get-tuple-element.243, f32[64]{0:T(128)S(1)} %get-tuple-element.241, f32[64]{0:T(128)S(1)} %copy-done.57, f32[1024]{0:T(1024)S(1)} %copy-done.56), channel_id=1, replica_groups=mesh['dp'=4,'seq'=8] {'dp','seq'}, use_global_device_ids=true, to_apply=%region_19.20 | all-reduce | flops 2176 | bytes 17408 | tf_op jit(solution)/shard_map/psum | solution.py:313
  456.8 360.6 %reduce-scatter.3.cloned.1.call-done = f32[32,12288]{1,0:T(8,128)} async-done(((f32[1024,12288]{1,0:T(8,128)}), f32[32,12288]{1,0:T(8,128)}) %reduce-scatter.3.cloned.1.call-update) | async-done | bytes 1572880 | tf_op jit(solution)/shard_map/reduce_scatter | solution.py:317
  823.0 207.1 %reduce-scatter.5.cloned.1.call-done = f32[144,1024]{1,0:T(8,128)} async-done(((f32[4608,1024]{1,0:T(8,128)}), f32[144,1024]{1,0:T(8,128)}) %reduce-scatter.5.cloned.1.call-update) | async-done | bytes 589840 | tf_op jit(solution)/shard_map/reduce_scatter | solution.py:330
  (325 shorter events, 163.9 us)
Async XLA Ops:
  7.2 164.4 %copy-start = (bf16[1024,1024]{1,0:T(8,128)(2,1)S(1)}, bf16[1024,1024]{1,0:T(8,128)(2,1)}, u32[]{:S(2)}) copy-start(bf16[1024,1024]{1,0:T(8,128)(2,1)} %param.26) | copy-start | bytes 6291460
  7.2 11.1 %copy-start.53 = (f32[64]{0:T(128)S(1)}, f32[64]{0:T(128)}, u32[]{:S(2)}) copy-start(f32[64]{0:T(128)} %param.25) | copy-start | bytes 772
  10.6 14.0 %copy-start.46 = (f32[256]{0:T(256)}, f32[256]{0:T(256)S(1)}, u32[]{:S(2)}) copy-start(f32[256]{0:T(256)S(1)} %fusion.98) | copy-start | bytes 3076
  12.5 17.5 %copy-start.30 = (f32[256,64]{0,1:T(8,128)}, f32[256,64]{0,1:T(8,128)S(1)}, u32[]{:S(2)}) copy-start(f32[256,64]{0,1:T(8,128)S(1)} %get-tuple-element.317) | copy-start | bytes 196612
  12.5 24.8 %copy-start.20 = (f32[256,64]{0,1:T(8,128)}, f32[256,64]{0,1:T(8,128)S(1)}, u32[]{:S(2)}) copy-start(f32[256,64]{0,1:T(8,128)S(1)} %get-tuple-element.316) | copy-start | bytes 196612
  18.6 6.1 copy-start.4
  18.6 6.1 copy-start.40
  21.7 8.0 copy-start.54
  34.7 6.2 copy-start.14
  44.4 33.4 %all-to-all-start = ((bf16[256,8,256]{2,0,1:T(8,128)(2,1)}), bf16[256,8,256]{2,0,1:T(8,128)(2,1)S(1)}, u32[]{:S(2)}, u32[]{:S(2)}) async-start(bf16[256,8,256]{2,0,1:T(8,128)(2,1)} %pad_maximum_fusion.1), calls=%async_computation | async-start | bytes 2097152 | tf_op jit(solution)/shard_map/all_to_all | solution.py:232
  128.3 43.3 %copy-start.5 = (bf16[256,1024]{1,0:T(8,128)(2,1)S(1)}, bf16[256,1024]{1,0:T(8,128)(2,1)}, u32[]{:S(2)}) copy-start(bf16[256,1024]{1,0:T(8,128)(2,1)} %param.18) | copy-start | bytes 1572868
  147.4 25.1 %copy-start.50 = (f32[1024]{0:T(1024)S(1)}, f32[1024]{0:T(1024)}, u32[]{:S(2)}) copy-start(f32[1024]{0:T(1024)} %param.27) | copy-start | bytes 12292
  171.6 9.4 copy-start.19
  172.4 42.2 %copy-start.12 = (f32[256,1024]{1,0:T(8,128)}, f32[256,1024]{1,0:T(8,128)S(1)}, u32[]{:S(2)}) copy-start(f32[256,1024]{1,0:T(8,128)S(1)} %get-tuple-element.319) | copy-start | bytes 3145732
  172.6 8.4 copy-start.15
  181.0 8.2 copy-start.27
  181.0 22.3 %slice-start = ((s8[9437184]{0:T(1024)(128)(4,1)}), s8[4194304]{0:T(1024)(128)(4,1)S(1)}, s32[]{:S(2)}) async-start(s8[9437184]{0:T(1024)(128)(4,1)} %bitcast.327), calls=%async_computation.8 | async-start | bytes 8388608
  189.2 14.2 %slice-start.1 = ((s8[9437184]{0:T(1024)(128)(4,1)}), s8[4194304]{0:T(1024)(128)(4,1)S(1)}, s32[]{:S(2)}) async-start(s8[9437184]{0:T(1024)(128)(4,1)} %bitcast.327), calls=%async_computation.9 | async-start | bytes 8388608
  189.2 14.2 %slice-start.2 = ((s8[9437184]{0:T(1024)(128)(4,1)}), s8[1048576]{0:T(1024)(128)(4,1)S(1)}, s32[]{:S(2)}) async-start(s8[9437184]{0:T(1024)(128)(4,1)} %bitcast.327), calls=%async_computation.10 | async-start | bytes 2097152
  215.0 9.3 copy-start.9
  216.6 19.8 %copy-start.11 = (bf16[2048,1,64]{0,2,1:T(8,128)(2,1)S(1)}, bf16[2048,1,64]{0,2,1:T(8,128)(2,1)}, u32[]{:S(2)}) copy-start(bf16[2048,1,64]{0,2,1:T(8,128)(2,1)} %copy-done.10) | copy-start | bytes 786436
  216.6 19.1 %all-to-all-start.2 = ((bf16[256,8,128]{2,0,1:T(8,128)(2,1)}), bf16[256,8,128]{2,0,1:T(8,128)(2,1)S(1)}, u32[]{:S(2)}, u32[]{:S(2)}) async-start(bf16[256,8,128]{2,0,1:T(8,128)(2,1)} %bitcast.260), calls=%async_computation.2 | async-start | bytes 1048576 | tf_op jit(solution)/shard_map/all_to_all | solution.py:267
  305.8 6.7 copy-start.16
  308.9 30.1 %all-to-all-start.3 = ((bf16[8,2,32768]{2,1,0:T(2,128)(2,1)}), bf16[8,2,32768]{2,1,0:T(2,128)(2,1)S(1)}, u32[]{:S(2)}, u32[]{:S(2)}) async-start(bf16[8,2,32768]{2,1,0:T(2,128)(2,1)} %reshape.495), calls=%async_computation.3 | async-start | bytes 2097152 | tf_op jit(solution)/shard_map/all_to_all | solution.py:293
  312.5 505.0 %reduce-scatter.3.cloned.1.call-start = ((), (), s32[]{:S(2)}) async-start(), calls=%async_computation.6 | async-start | bytes 51904512 | tf_op jit(solution)/shard_map/reduce_scatter | solution.py:317
  329.6 15.2 %copy-start.31 = (f32[256,64]{0,1:T(8,128)S(1)}, f32[256,64]{0,1:T(8,128)}, u32[]{:S(2)}) copy-start(f32[256,64]{0,1:T(8,128)} %copy-done.30) | copy-start | bytes 196612
  386.9 643.3 %reduce-scatter.5.cloned.1.call-start = ((), (), s32[]{:S(2)}) async-start(), calls=%async_computation.7 | async-start | bytes 19464192 | tf_op jit(solution)/shard_map/reduce_scatter | solution.py:330
  402.1 10.2 copy-start.17
  402.1 11.0 %copy-start.23 = (bf16[256,8,64]{0,2,1:T(8,128)(2,1)S(1)}, bf16[256,8,64]{0,2,1:T(8,128)(2,1)}, u32[]{:S(2)}) copy-start(bf16[256,8,64]{0,2,1:T(8,128)(2,1)} %copy-done.22) | copy-start | bytes 786436
  402.1 11.0 %copy-start.33 = (bf16[1024,512]{1,0:T(8,128)(2,1)S(1)}, bf16[1024,512]{1,0:T(8,128)(2,1)}, u32[]{:S(2)}) copy-start(bf16[1024,512]{1,0:T(8,128)(2,1)} %param.22) | copy-start | bytes 3145732
  412.3 41.7 %copy-start.52 = (f32[256]{0:T(256)S(1)}, f32[256]{0:T(256)}, u32[]{:S(2)}) copy-start(f32[256]{0:T(256)} %copy-done.51) | copy-start | bytes 3076
  413.1 617.1 %copy-start.1 = (bf16[1024,1024]{1,0:T(8,128)(2,1)S(1)}, bf16[1024,1024]{1,0:T(8,128)(2,1)}, u32[]{:S(2)}) copy-start(bf16[1024,1024]{1,0:T(8,128)(2,1)} %param.26) | copy-start | bytes 6291460
  (46 other events, 109.1 us)
Sparse Core Ops, SparseCore 0:
  387.0 430.4 reduce-scatter.2
  824.5 205.6 reduce-scatter.4
where the time goes:
time: 1040 us
  waiting for transfers between devices  615 us (59%)
  matrix products  165 us (16%)
  other arithmetic  93.6 us (9%)
  local copies, waits for them, and re-layouts  69.6 us (7%)
  blocking collectives  57.7 us (6%)
  between operations  15.2 us (1%)
  starting transfers between devices  14.4 us (1%)
    reduce_scatter x1, waiting for transfers between devices, body(): lax.psum_scatter(jnp.concatenate([tokens_dot(picker(low_normed), right_in...  361 us
    reduce_scatter x1, waiting for transfers between devices, body(): lax.psum_scatter(tokens_dot(plain_pick()(activated), cotangent), ('dp', '...  207 us
    psum x1, blocking collectives, body(): lax.psum((grad_again, grad_qgain, grad_kgain, grad_fgain), ('dp', 'seq'))  38.6 us
    dot_general x4, matrix products, tokens_dot(): lax.dot_general(left, right, (((0,), (0,)), ((), ())), preferred_element_...  38.2 us
    concatenate x1, other arithmetic, body(): jnp.concatenate([tokens_dot(picker(low_normed), right_inputs), tokens_dot...  33.4 us
    dot_general x7, matrix products, back_dot(): lax.dot_general(grad_rows, weight, (((1,), (1,)), ((), ())), preferred_el...  29 us
    all_to_all x1, waiting for transfers between devices, body(): lax.all_to_all(packed, 'seq', split_axis=1, concat_axis=0, tiled=True)  26.5 us
  transfers between devices with their start and end apart: 5, of which 5 were waited for; matrix products, arithmetic and copies ran while one was open for 5% of the time, Pallas kernels for 0%

commit v1 on v0

v1 whole, which is shorter than its diff:
```python
import functools
import math

import jax
import jax.numpy as jnp
from jax import lax
from jax.experimental import pallas as pl
from jax.experimental.pallas import tpu as pltpu
from jax.sharding import Mesh
from jax.sharding import PartitionSpec as P

EPSILON = 1e-05
ROPE_BASE = 1000000.0
FAR = 16384.0
LANES = 128
VMEM_LIMIT = 56 * 1024 * 1024
ALL = ("y", "x", "z", "c")
F32 = jnp.float32
BF16 = jnp.bfloat16


def dot_nn(left, right):
    return lax.dot_general(left, right, (((1,), (0,)), ((), ())), preferred_element_type=F32)


def dot_nt(left, right):
    return lax.dot_general(left, right, (((1,), (1,)), ((), ())), preferred_element_type=F32)


def dot_tn(left, right):
    return lax.dot_general(left, right, (((0,), (0,)), ((), ())), preferred_element_type=F32)


def params():
    return pltpu.CompilerParams(vmem_limit_bytes=VMEM_LIMIT)


def pick(field, index, axis=0):
    return lax.dynamic_index_in_dim(field, index, axis, keepdims=False)


def swap(field, axis_name):
    return lax.ppermute(field, axis_name, [(0, 1), (1, 0)])


def both(own, other, core):
    rows = own.shape[0]
    first = jnp.where(core == 0, own, other)
    second = jnp.where(core == 0, other, own)
    return jnp.concatenate([first, second], axis=0)


def pair_reduce(parts, axis_name, index):
    got = swap(pick(parts, 1 - index), axis_name)
    return pick(parts, index) + got


def line_reduce(parts, axis_name, index):
    count = parts.shape[0]

    def part(number):
        return pick(parts, jnp.clip(number, 0, count - 1))

    right = left = None
    for step in range(1, count):
        to_right = part(count - step + index)
        to_left = part(step - count + index)
        if right is not None:
            to_right = to_right + right
            to_left = to_left + left
        right = lax.ppermute(to_right, axis_name, [(k, k + 1) for k in range(step)])
        left = lax.ppermute(
            to_left, axis_name, [(count - 1 - k, count - 2 - k) for k in range(step)]
        )
    return part(index) + right + left


def reduce_first(parts, axis_name, index):
    if parts.shape[0] == 1:
        return parts[0]
    if axis_name == "z":
        return line_reduce(parts, axis_name, index)
    if parts.shape[0] == 2:
        return pair_reduce(parts, axis_name, index)
    return lax.psum_scatter(parts, axis_name, scatter_dimension=0, tiled=False)


def exchange_line(parts, index):
    count = parts.shape[0]
    got = []
    for step in range(count - 1, 0, -1):
        arrived = lax.ppermute(
            pick(parts, index ^ step), "z", [(k, k ^ step) for k in range(count)]
        )
        got.append((index ^ step, arrived))
    out = lax.dynamic_update_index_in_dim(jnp.zeros_like(parts), pick(parts, index), index, 0)
    for place, arrived in got:
        out = lax.dynamic_update_index_in_dim(out, arrived, place, 0)
    return out


def sum_all(vector, rows_y, rows_z):
    vector = vector + swap(vector, "c")
    vector = vector + swap(vector, "x")
    if rows_y == 2:
        vector = vector + swap(vector, "y")
    else:
        vector = lax.psum(vector, "y")
    step = 1
    while step < rows_z:
        vector = vector + lax.ppermute(vector, "z", [(k, k ^ step) for k in range(rows_z)])
        step = step * 2
    return vector


def lane_ids(rows):
    return lax.broadcasted_iota(jnp.int32, (rows, LANES), 1)


def half_swap(field, lanes):
    return jnp.where(
        (lanes & 63) < 32, pltpu.roll(field, LANES - 32, 1), pltpu.roll(field, 32, 1)
    )


def half_sums(field, lanes):
    low = jnp.sum(jnp.where(lanes < 64, field, 0.0), axis=1, keepdims=True)
    high = jnp.sum(jnp.where(lanes < 64, 0.0, field), axis=1, keepdims=True)
    return jnp.where(lanes < 64, low, high)


def project_kernel(head_size, ids, x_ref, gain_ref, wq_ref, wk_ref, wv_ref, cos_ref, sin_ref,
                   qg_ref, kg_ref, h_ref, out_ref):
    rows = x_ref.shape[0]
    x = x_ref[...].astype(F32)
    scale = lax.rsqrt(jnp.mean(x * x, axis=1, keepdims=True) + EPSILON)
    h = (x * scale * gain_ref[...]).astype(BF16)
    h_ref[...] = h
    lanes = lane_ids(rows)
    cosine, sine = cos_ref[...], sin_ref[...]

    def turned(raw, gain):
        unit = raw * lax.rsqrt(half_sums(raw * raw, lanes) * (1.0 / head_size) + EPSILON) * gain
        return unit * cosine + half_swap(unit, lanes) * sine

    q_raw = dot_nn(h, wq_ref[...])
    k_raw = dot_nn(h, wk_ref[...])
    v_raw = dot_nn(h, wv_ref[...])
    heads = out_ref.shape[0]
    for head in range(heads):
        span = slice(head * LANES, (head + 1) * LANES)
        out_ref[head, :, 0:LANES] = turned(q_raw[:, span], qg_ref[...]).astype(BF16)
    for pair in range(heads // 2):
        span = slice(pair * LANES, (pair + 1) * LANES)
        keys = turned(k_raw[:, span], kg_ref[...])
        values = v_raw[:, span]
        even = jnp.where(lanes < 64, keys, pltpu.roll(values, 64, 1))
        odd = jnp.where(lanes < 64, pltpu.roll(keys, 64, 1), values)
        out_ref[2 * pair, :, LANES:] = even.astype(BF16)
        out_ref[2 * pair + 1, :, LANES:] = odd.astype(BF16)


def project(ids, x, gain, w_query, w_key, w_value, cosine, sine, qg, kg, head_size):
    rows, width = x.shape
    heads = w_key.shape[1] // head_size // 2
    block = min(256, rows)
    whole = lambda shape: pl.BlockSpec(shape, lambda i, ids: (0,) * len(shape))
    by_core = lambda w: pl.BlockSpec((width, w.shape[1] // 2), lambda i, ids: (0, ids[0]))
    by_row = lambda cols: pl.BlockSpec((block, cols), lambda i, ids: (i, 0))
    return pl.pallas_call(
        functools.partial(project_kernel, head_size),
        grid_spec=pltpu.PrefetchScalarGridSpec(
            num_scalar_prefetch=1,
            grid=(rows // block,),
            in_specs=[by_row(width), whole((1, width)), by_core(w_query), by_core(w_key),
                      by_core(w_value), by_row(LANES), by_row(LANES), whole((1, LANES)),
                      whole((1, LANES))],
            out_specs=[by_row(width),
                       pl.BlockSpec((heads, block, 2 * LANES), lambda i, ids: (0, i, 0))],
        ),
        out_shape=[jax.ShapeDtypeStruct((rows, width), BF16),
                   jax.ShapeDtypeStruct((heads, rows, 2 * LANES), BF16)],
        compiler_params=params(),
        cost_estimate=pl.CostEstimate(
            flops=2 * rows * width * w_query.shape[1], bytes_accessed=6 << 20, transcendentals=0),
        name="project",
    )(ids, x, gain, w_query, w_key, w_value, cosine, sine, qg, kg)


def three_parts(value):
    high = value.astype(BF16).astype(F32)
    rest = value - high
    middle = rest.astype(BF16).astype(F32)
    return high, middle, rest - middle


def marked(lanes, first, value, otherwise):
    high, middle, low = three_parts(value)
    return jnp.where(
        lanes == first,
        high,
        jnp.where(lanes == first + 1, middle, jnp.where(lanes == first + 2, low, otherwise)),
    )


def below(rows, cols):
    return lax.broadcasted_iota(jnp.int32, (rows, cols), 1) <= lax.broadcasted_iota(
        jnp.int32, (rows, cols), 0
    )


def attend_kernel(block, mark, qkv_ref, segq_ref, segk_ref, o_ref, wide_ref, qaug_ref, kaug_ref,
                  vaug_ref):
    rows = qkv_ref.shape[0]
    count = rows // block
    lanes = lane_ids(block)
    for i in range(count):
        span = slice(i * block, (i + 1) * block)
        pair = qkv_ref[span, 0:LANES].astype(F32)
        keyval = qkv_ref[span, LANES:].astype(F32)
        segq = segq_ref[span, :].astype(F32)
        segk = segk_ref[span, :].astype(F32)
        qaug_ref[0, span, :] = jnp.where(lanes < 64, pair, segq).astype(BF16)
        qaug_ref[1, span, :] = jnp.where(lanes < 64, pltpu.roll(pair, 64, 1), segq).astype(BF16)
        kaug_ref[span, :] = jnp.where(lanes < 64, keyval, segk).astype(BF16)
        vaug_ref[span, :] = jnp.where(
            lanes < 64, pltpu.roll(keyval, 64, 1), jnp.where(lanes < 67, 1.0, 0.0)
        ).astype(BF16)
    for i in range(count):
        span = slice(i * block, (i + 1) * block)
        outs = []
        for head in range(2):
            queries = qaug_ref[head, span, :]
            total = jnp.zeros((block, LANES), F32)
            for j in range(i + 1):
                other = slice(j * block, (j + 1) * block)
                weights = jnp.exp2(dot_nt(queries, kaug_ref[other, :]))
                if j == i:
                    weights = jnp.where(below(block, block), weights, 0.0)
                total = total + dot_nn(weights.astype(BF16), vaug_ref[other, :])
            row_sum = total[:, 64:65]
            outs.append(total * (1.0 / row_sum))
            qaug_ref[head, span, :] = marked(
                lanes, mark, -jnp.log2(row_sum), queries.astype(F32)
            ).astype(BF16)
        wide = jnp.where(lanes < 64, outs[0], pltpu.roll(outs[1], 64, 1))
        wide_ref[span, :] = wide
        o_ref[span, :] = wide.astype(BF16)


def attend(qkv, segq, segk, block, mark):
    rows = qkv.shape[0]
    return pl.pallas_call(
        functools.partial(attend_kernel, block, mark),
        out_shape=[jax.ShapeDtypeStruct((rows, LANES), BF16),
                   jax.ShapeDtypeStruct((rows, LANES), F32),
                   jax.ShapeDtypeStruct((2, rows, LANES), BF16),
                   jax.ShapeDtypeStruct((rows, LANES), BF16),
                   jax.ShapeDtypeStruct((rows, LANES), BF16)],
        compiler_params=params(),
        cost_estimate=pl.CostEstimate(
            flops=rows * rows * LANES * 8, bytes_accessed=6 << 20,
            transcendentals=rows * rows),
        name="attend",
    )(qkv, segq, segk)


def attend_back_kernel(block, qaug_ref, kaug_ref, vaug_ref, wide_ref, do_ref, dq_ref, dkv_ref,
                       doaug, dq_sum):
    rows = kaug_ref.shape[0]
    count = rows // block
    lanes = lane_ids(block)
    for i in range(count):
        span = slice(i * block, (i + 1) * block)
        do_pair = do_ref[span, :].astype(F32)
        inner = do_pair * wide_ref[span, :]
        low = jnp.sum(jnp.where(lanes < 64, inner, 0.0), axis=1, keepdims=True)
        high = jnp.sum(jnp.where(lanes < 64, 0.0, inner), axis=1, keepdims=True)
        doaug[0, span, :] = jnp.where(
            lanes < 64, do_pair, marked(lanes, 64, -low, 0.0)).astype(BF16)
        doaug[1, span, :] = jnp.where(
            lanes < 64, pltpu.roll(do_pair, 64, 1), marked(lanes, 64, -high, 0.0)).astype(BF16)
        dq_sum[:, span, :] = jnp.zeros((2, block, LANES), F32)
    for j in range(count):
        here = slice(j * block, (j + 1) * block)
        keys = kaug_ref[here, :]
        values = vaug_ref[here, :]
        dk = jnp.zeros((LANES, block), F32)
        dv = jnp.zeros((LANES, block), F32)
        for i in range(j, count):
            span = slice(i * block, (i + 1) * block)
            for head in range(2):
                queries = qaug_ref[head, span, :]
                grads = doaug[head, span, :]
                weights = jnp.exp2(dot_nt(queries, keys))
                if j == i:
                    weights = jnp.where(below(block, block), weights, 0.0)
                slopes = (weights * dot_nt(grads, values)).astype(BF16)
                dv = dv + dot_tn(grads, weights.astype(BF16))
                dk = dk + dot_tn(queries, slopes)
                dq_sum[head, span, :] = dq_sum[head, span, :] + dot_nn(slopes, keys)
        dk_rows = jnp.transpose(dk) * math.log(2.0)
        dv_rows = jnp.transpose(dv)
        dkv_ref[here, :] = jnp.where(lanes < 64, dk_rows, pltpu.roll(dv_rows, 64, 1))
    for i in range(count):
        span = slice(i * block, (i + 1) * block)
        dq_ref[span, :] = jnp.where(
            lanes < 64, dq_sum[0, span, :], pltpu.roll(dq_sum[1, span, :], 64, 1)) * 0.125


def attend_back(qaug, kaug, vaug, wide, do, block):
    rows = kaug.shape[0]
    return pl.pallas_call(
        functools.partial(attend_back_kernel, block),
        out_shape=[jax.ShapeDtypeStruct((rows, LANES), F32)] * 2,
        scratch_shapes=[pltpu.VMEM((2, rows, LANES), BF16), pltpu.VMEM((2, rows, LANES), F32)],
        compiler_params=params(),
        cost_estimate=pl.CostEstimate(
            flops=rows * rows * LANES * 20, bytes_accessed=6 << 20,
            transcendentals=rows * rows),
        name="attend_back",
    )(qaug, kaug, vaug, wide, do)


def unturn_kernel(head_size, ids, h_ref, wq_ref, wk_ref, cos_ref, sin_ref, qg_ref, kg_ref, dq_ref,
                  dkv_ref, out_ref, gains_ref):
    rows = h_ref.shape[0]
    lanes = lane_ids(rows)
    cosine, sine = cos_ref[...], sin_ref[...]
    h = h_ref[...]

    def undo(raw, grad, gain):
        scale = lax.rsqrt(half_sums(raw * raw, lanes) * (1.0 / head_size) + EPSILON)
        unit = raw * scale
        back = grad * cosine - half_swap(grad, lanes) * sine
        scaled = back * gain
        mean = half_sums(scaled * unit, lanes) * (1.0 / head_size)
        return scale * (scaled - unit * mean), jnp.sum(back * unit, axis=0, keepdims=True)

    q_raw = dot_nn(h, wq_ref[...])
    k_pair = dot_nn(h, wk_ref[...])
    k_raw = jnp.where(ids[2] == 0, k_pair, pltpu.roll(k_pair, 64, 1))
    dkv = dkv_ref[...]
    dqr, q_gain = undo(q_raw, dq_ref[...], qg_ref[...])
    dkr, k_gain = undo(k_raw, jnp.where(lanes < 64, dkv, 0.0), kg_ref[...])
    out_ref[:, 0:LANES] = dqr.astype(BF16)
    out_ref[:, LANES:] = jnp.where(lanes < 64, dkr, dkv).astype(BF16)

    @pl.when(pl.program_id(0) == 0)
    def _():
        gains_ref[...] = jnp.zeros_like(gains_ref)

    gains_ref[0:1, :] = gains_ref[0:1, :] + q_gain
    gains_ref[1:2, :] = gains_ref[1:2, :] + k_gain


def unturn(ids, h, w_query, w_key, cosine, sine, qg, kg, dq, dkv, head_size):
    rows, width = h.shape
    block = min(512, rows)
    whole = lambda shape: pl.BlockSpec(shape, lambda i, ids: (0,) * len(shape))
    by_row = lambda cols: pl.BlockSpec((block, cols), lambda i, ids: (i, 0))
    return pl.pallas_call(
        functools.partial(unturn_kernel, head_size),
        grid_spec=pltpu.PrefetchScalarGridSpec(
            num_scalar_prefetch=1,
            grid=(rows // block,),
            in_specs=[by_row(width),
                      pl.BlockSpec((width, LANES), lambda i, ids: (0, ids[1])),
                      pl.BlockSpec((width, LANES), lambda i, ids: (0, ids[1] // 2)),
                      by_row(LANES), by_row(LANES), whole((1, LANES)), whole((1, LANES)),
                      by_row(LANES), by_row(LANES)],
            out_specs=[by_row(2 * LANES), whole((8, LANES))],
        ),
        out_shape=[jax.ShapeDtypeStruct((rows, 2 * LANES), BF16),
                   jax.ShapeDtypeStruct((8, LANES), F32)],
        compiler_params=params(),
        cost_estimate=pl.CostEstimate(
            flops=4 * rows * width * LANES, bytes_accessed=10 << 20, transcendentals=0),
        name="unturn",
    )(ids, h, w_query, w_key, cosine, sine, qg, kg, dq, dkv)


def feed_kernel(ids, h_ref, c_ref, wg_ref, wu_ref, wd_ref, *refs):
    m_ref, dg_ref, du_ref, dh_ref, y_ref = refs[-5:]
    h, c = h_ref[...], c_ref[...]
    gate = dot_nn(h, wg_ref[...])
    up = dot_nn(h, wu_ref[...])
    sig = jax.nn.sigmoid(gate)
    silu = gate * sig
    m = (silu * up).astype(BF16)
    m_ref[...] = m
    y_ref[...] = dot_nn(m, wd_ref[...]).astype(BF16)
    dm = dot_nt(c, wd_ref[...])
    dg = (dm * up * sig * (1.0 + gate * (1.0 - sig))).astype(BF16)
    du = (dm * silu).astype(BF16)
    dg_ref[...] = dg
    du_ref[...] = du
    dh_ref[...] = (dot_nt(dg, wg_ref[...]) + dot_nt(du, wu_ref[...])).astype(BF16)


def feed(ids, h, c, w_gate, w_up, w_down, earlier, parts):
    rows, width = h.shape
    units = w_gate.shape[1] // parts
    block = min(256, rows)
    steps = rows // block
    half = 0 if earlier is None else 1
    by_row = pl.BlockSpec((block, width), lambda i, ids: (i, 0))
    in_cols = pl.BlockSpec((width, units), lambda i, ids: (0, ids[3]))
    kept = pl.BlockSpec((block, units), lambda i, ids: (i + half * steps, 0))
    extra = () if earlier is None else tuple(earlier)
    big = jax.ShapeDtypeStruct((2 * rows, units), BF16)
    small = jax.ShapeDtypeStruct((rows, width), BF16)
    return pl.pallas_call(
        feed_kernel,
        grid_spec=pltpu.PrefetchScalarGridSpec(
            num_scalar_prefetch=1,
            grid=(steps,),
            in_specs=[by_row, by_row, in_cols, in_cols,
                      pl.BlockSpec((units, width), lambda i, ids: (ids[3], 0))]
            + [pl.BlockSpec(memory_space=pl.ANY)] * len(extra),
            out_specs=[kept, kept, kept, by_row, by_row],
        ),
        out_shape=[big, big, big, small, small],
        input_output_aliases={6 + k: k for k in range(len(extra))},
        compiler_params=params(),
        cost_estimate=pl.CostEstimate(
            flops=12 * rows * width * units, bytes_accessed=16 << 20,
            transcendentals=rows * units),
        name="feed",
    )(ids, h, c, w_gate, w_up, w_down, *extra)


def norm_scale(field):
    return lax.rsqrt(jnp.mean(field * field, axis=-1, keepdims=True) + EPSILON)


def norm_back(field, scale, scaled_grad):
    inner = jnp.mean(scaled_grad * field, axis=-1, keepdims=True)
    return scale * scaled_grad - field * (scale * scale * scale * inner)


def rope_tables(position, head_size):
    half = head_size // 2
    lane = jnp.arange(LANES, dtype=jnp.int32)
    freqs = ROPE_BASE ** (-2.0 * (lane % half).astype(F32) / head_size)
    angles = position.astype(F32)[:, None] * freqs[None, :]
    sign = jnp.where(lane % head_size < half, -1.0, 1.0)
    return jnp.cos(angles), jnp.sin(angles) * sign[None, :]


def body(tokens, lengths, attn_gain, w_query, w_key, w_value, query_gain, key_gain, w_out,
         ffn_gain, w_gate, w_up, w_down, cotangent):
    rows, width = tokens.shape
    head_size = query_gain.shape[0]
    n_y, n_z = lax.axis_size("y"), lax.axis_size("z")
    i_y, i_x, i_z, i_c = (lax.axis_index(name) for name in ALL)
    chip_rows = 2 * rows
    group_rows = chip_rows * n_z
    kv_heads = w_key.shape[1] // head_size
    heads = kv_heads // 2
    slots = lengths.shape[1]
    mark = 64 + slots
    head = i_c * heads + i_z
    ids = jnp.stack([i_c, head, head % 2, 2 * i_x + i_c]).astype(jnp.int32)

    x = both(tokens, swap(tokens, "c"), i_c)
    cot = both(cotangent, swap(cotangent, "c"), i_c)
    cot_far_own = swap(cotangent, "x")
    cot_far = both(cot_far_own, swap(cot_far_own, "c"), i_c)

    index = jnp.arange(group_rows, dtype=jnp.int32)
    lane = jnp.arange(LANES, dtype=jnp.int32)
    start_of = jnp.zeros((group_rows,), jnp.int32)
    lane_start = jnp.zeros((LANES,), jnp.int32)
    lane_end = jnp.zeros((LANES,), jnp.int32)
    run = jnp.zeros((), jnp.int32)
    for slot in range(slots):
        stop = run + lengths[0, slot]
        start_of = jnp.where((index >= run) & (index < stop), run, start_of)
        lane_start = jnp.where(lane == 64 + slot, run, lane_start)
        lane_end = jnp.where(lane == 64 + slot, stop, lane_end)
        run = stop
    inside = (index[:, None] >= lane_start[None, :]) & (index[:, None] < lane_end[None, :])
    slot_lane = (lane >= 64) & (lane < mark)
    ones_lane = (lane >= mark) & (lane < mark + 3)
    segq = jnp.where(inside, 1.0, 0.0).astype(BF16)
    segk = jnp.where(
        slot_lane[None, :], jnp.where(inside, 0.0, -FAR), jnp.where(ones_lane, 1.0, 0.0)[None, :]
    ).astype(BF16)
    position = index - start_of
    cos_all, sin_all = rope_tables(position, head_size)
    cosine = lax.dynamic_slice_in_dim(cos_all, i_z * chip_rows, chip_rows, 0)
    sine = lax.dynamic_slice_in_dim(sin_all, i_z * chip_rows, chip_rows, 0)

    to_exp2 = math.log2(math.e) / math.sqrt(head_size)
    qg = jnp.tile(query_gain, 2)[None, :]
    kg = jnp.tile(key_gain, 2)[None, :]
    h, packed = project(ids, x, attn_gain[None, :], w_query, w_key, w_value, cosine, sine,
                        qg * to_exp2, kg, head_size)
    qkv = exchange_line(packed, i_z).reshape(group_rows, 2 * LANES)
    block = math.gcd(512, group_rows)
    o_head, wide, qaug, kaug, vaug = attend(qkv, segq, segk, block, mark)
    o_own = exchange_line(o_head.reshape(n_z, chip_rows, LANES), i_z)
    o_other = swap(o_own, "c")
    o_first = jnp.where(i_c == 0, o_own, o_other)
    o_second = jnp.where(i_c == 0, o_other, o_own)
    o_all = jnp.concatenate([o_first, o_second], axis=0)
    o_rows = jnp.transpose(o_all, (1, 0, 2)).reshape(chip_rows, width)
    middle = x.astype(F32) + dot_nn(o_rows, w_out)
    scale_two = norm_scale(middle)
    h2 = (middle * scale_two * ffn_gain[None, :]).astype(BF16)

    h2_own = lax.dynamic_slice_in_dim(h2, i_c * rows, rows, 0)
    far_own = swap(h2_own, "x")
    h2_far = both(far_own, swap(far_own, "c"), i_c)
    m, dg, du, dh2_near, y_near = feed(ids, h2, cot, w_gate, w_up, w_down, None, 4)
    m, dg, du, dh2_far, y_far = feed(ids, h2_far, cot_far, w_gate, w_up, w_down, (m, dg, du), 4)

    def home(near, far):
        far_sum = pair_reduce(far.reshape(2, rows, width), "c", i_c)
        near_sum = pair_reduce(near.reshape(2, rows, width), "c", i_c)
        return near_sum.astype(F32) + swap(far_sum, "x").astype(F32)

    dh2 = home(dh2_near, dh2_far)
    own = lambda field: lax.dynamic_slice_in_dim(field, i_c * rows, rows, 0)
    middle_own, scale_own = own(middle), own(scale_two)
    dy = cotangent.astype(F32) + norm_back(middle_own, scale_own, dh2 * ffn_gain[None, :])
    gain_ffn = jnp.sum(dh2 * middle_own * scale_own, axis=0)
    da_own = dy.astype(BF16)
    da = both(da_own, swap(da_own, "c"), i_c)
    w_out_own = lax.dynamic_slice_in_dim(w_out, i_c * (width // 2), width // 2, 0)
    do = dot_nt(da, w_out_own).astype(BF16)
    do_parts = jnp.transpose(do.reshape(chip_rows, heads, LANES), (1, 0, 2))
    do_head = exchange_line(do_parts, i_z).reshape(group_rows, LANES)

    mixed = (middle_own + home(y_near, y_far)).astype(BF16)

    h2_all = jnp.concatenate([h2, h2_far], axis=0)
    cot_all = jnp.concatenate([cot, cot_far], axis=0)
    units = m.shape[1]
    piece = units // (n_y * n_z)
    down = dot_tn(m, cot_all).astype(BF16).reshape(n_z, n_y, piece, width)
    down = reduce_first(jnp.moveaxis(down, 1, 0), "y", i_y)
    down = line_reduce(down, "z", i_z)
    owners = []
    for y in range(n_y):
        for xx in range(2):
            for z in range(n_z):
                for c in range(2):
                    source = ((y * 2 + xx) * n_z + z) * 2 + c
                    owners.append((source, 4 * 0 + n_y * n_z * (2 * xx + c) + z * n_y + y))
    share_down = lax.ppermute(down, ALL, owners).astype(F32)

    row_block = width // (n_y * 2 * n_z * 2)

    def rows_home(grad):
        cols = grad.shape[1]
        parts = grad.reshape(n_y, 2, n_z, 2, row_block, cols)
        parts = reduce_first(parts, "y", i_y)
        parts = line_reduce(jnp.moveaxis(parts, 1, 0), "z", i_z)
        return parts

    def spread(parts):
        kept = pick(parts, i_c, 1)
        got = swap(pick(parts, 1 - i_c, 1), "c")
        cols = jnp.concatenate(
            [jnp.where(i_c == 0, kept, got), jnp.where(i_c == 0, got, kept)], axis=2)
        kept = pick(cols, i_x)
        got = swap(pick(cols, 1 - i_x), "x")
        return jnp.concatenate(
            [jnp.where(i_x == 0, kept, got), jnp.where(i_x == 0, got, kept)], axis=1).astype(F32)

    share_gate = spread(rows_home(dot_tn(h2_all, dg).astype(BF16)))
    share_up = spread(rows_home(dot_tn(h2_all, du).astype(BF16)))

    da_cols = lax.dynamic_slice_in_dim(da, i_c * (width // 2), width // 2, 1)
    out_parts = dot_tn(o_rows, da_cols).astype(BF16).reshape(
        n_y, 2, n_z, 2, row_block, width // 2)
    out_parts = pair_reduce(jnp.moveaxis(out_parts, 1, 0), "x", i_x)
    out_parts = reduce_first(out_parts, "y", i_y)
    out_parts = line_reduce(out_parts, "z", i_z)
    kept = pick(out_parts, i_c)
    got = swap(pick(out_parts, 1 - i_c), "c")
    share_out = jnp.concatenate(
        [jnp.where(i_c == 0, kept, got), jnp.where(i_c == 0, got, kept)], axis=1).astype(F32)

    h_own = own(h)
    blocks = jnp.zeros((n_z, chip_rows, width), BF16)
    blocks = lax.dynamic_update_index_in_dim(blocks, h, i_z, 0)
    right = left = h_own
    for step in range(1, n_z):
        right = lax.ppermute(right, "z", [(k, k + 1) for k in range(n_z - 1)])
        left = lax.ppermute(left, "z", [(k + 1, k) for k in range(n_z - 1)])
        for sent, place in ((right, i_z - step), (left, i_z + step)):
            full = both(sent, swap(sent, "c"), i_c)
            inside_line = (place >= 0) & (place < n_z)
            spot = jnp.clip(place, 0, n_z - 1)
            full = jnp.where(inside_line, full, pick(blocks, spot))
            blocks = lax.dynamic_update_index_in_dim(blocks, full, spot, 0)
    h_group = blocks.reshape(group_rows, width)

    dq, dkv = attend_back(qaug, kaug, vaug, wide, do_head, block)
    back, gains = unturn(ids, h_group, w_query, w_key, cos_all, sin_all, qg, kg, dq, dkv, head_size)
    back_own = exchange_line(back.reshape(n_z, chip_rows, 2 * LANES), i_z)

    half = lambda w, cols: lax.dynamic_slice_in_dim(
        w, i_c * heads * cols, heads * cols, 1).reshape(width, heads, cols)
    w_heads = jnp.concatenate(
        [half(w_query, LANES), half(w_key, head_size), half(w_value, head_size)], axis=2)
    dh_part = lax.dot_general(
        back_own, w_heads, (((0, 2), (1, 2)), ((), ())), preferred_element_type=F32)
    dh = pair_reduce(dh_part.astype(BF16).reshape(2, rows, width), "c", i_c).astype(F32)

    grad_head = dot_tn(h_group, back)
    gain_attn = jnp.sum(grad_head * pick(w_heads, i_z, 1).astype(F32), axis=1) / attn_gain
    parts = grad_head.astype(BF16).reshape(n_y, 2, n_z, 2, row_block, 2 * LANES)
    parts = pair_reduce(jnp.moveaxis(parts, 1, 0), "x", i_x)
    parts = reduce_first(parts, "y", i_y)
    parts = exchange_line(parts, i_z)
    kept = pick(parts, i_c, 1)
    got = swap(pick(parts, 1 - i_c, 1), "c")
    by_head = jnp.concatenate(
        [jnp.where(i_c == 0, kept, got), jnp.where(i_c == 0, got, kept)], axis=0)
    by_head = jnp.transpose(by_head, (1, 0, 2)).astype(F32)
    share_query = by_head[:, :, :LANES].reshape(row_block, -1)
    share_key = by_head[:, :, LANES : LANES + head_size].reshape(row_block, -1)
    share_value = by_head[:, :, LANES + head_size :].reshape(row_block, -1)

    x_own = tokens.astype(F32)
    grad_tokens = dy + norm_back(x_own, norm_scale(x_own), dh * attn_gain[None, :])

    gain_query = gains[0, :head_size] + gains[0, head_size:]
    gain_key = gains[1, :head_size]
    sums = sum_all(
        jnp.concatenate([gain_attn, gain_ffn, gain_query, gain_key]).reshape(1, -1), n_y, n_z)[0]
    return (
        mixed,
        grad_tokens,
        sums[:width],
        share_query,
        share_key,
        share_value,
        sums[2 * width : 2 * width + head_size],
        sums[2 * width + head_size :],
        share_out,
        sums[width : 2 * width],
        share_gate,
        share_up,
        share_down,
    )


def solution(mesh):
    n_dp, n_seq = mesh.shape["dp"], mesh.shape["seq"]
    fine = Mesh(mesh.devices.reshape(n_dp // 2, 2, n_seq // 2, 2), ALL)
    split = P(ALL, None)
    in_specs = (split, P(("y", "x"), None)) + (P(),) * 11 + (split,)
    out_specs = (split, split, P(), split, split, split, P(), P(), split, P(), split, split, split)
    return jax.shard_map(body, mesh=fine, in_specs=in_specs, out_specs=out_specs, check_vma=False)
```

time: 1040 us -> 543 us (0.52)
  waiting for transfers between devices: 615 us -> 154 us
  matrix products: 165 us -> 21.3 us
  starting transfers between devices: 14.4 us -> 149 us
  Pallas kernels: 0 us -> 72.3 us
  blocking collectives: 57.7 us -> 0 us
  other arithmetic: 93.6 us -> 70.5 us
    reduce_scatter x2 -> x0, waiting for transfers between devices: 568 us -> none  [the longest x1 361 us: body(): lax.psum_scatter(jnp.concatenate([tokens_dot(picker(low_normed), right_in...]
    ppermute x0 -> x85, waiting for transfers between devices: none -> 154 us  [the longest x37 56.9 us: swap(): return lax.ppermute(field, axis_name, [(0, 1), (1, 0)])]
    ppermute x0 -> x85, starting transfers between devices: none -> 149 us  [the longest x12 59.6 us: line_reduce(): right = lax.ppermute(to_right, axis_name, [(k, k + 1) for k in range(step)])]
    dot_general x46 -> x8, matrix products: 165 us -> 21.3 us  [the longest x5 17.9 us: dot_tn(): lax.dot_general(left, right, (((0,), (0,)), ((), ())), preferred_element_...]
    pallas_call x0 -> x6, Pallas kernels: none -> 72.3 us  [the longest x2 28.5 us: feed(): pl.pallas_call(feed_kernel, grid_spec=pltpu.PrefetchScalarGridSpec(num_sc...]
    all_to_all x3 -> x0, waiting for transfers between devices: 47.4 us -> none  [the longest x1 26.5 us: body(): lax.all_to_all(packed, 'seq', split_axis=1, concat_axis=0, tiled=True)]
    psum x1 -> x0, blocking collectives: 38.6 us -> none  [body(): lax.psum((grad_again, grad_qgain, grad_kgain, grad_fgain), ('dp', 'seq'))]
    another operation x6 -> x1, other arithmetic: 23.8 us -> 0.59 us  [body(): ids = jnp.stack([i_c, head, head % 2, 2 * i_x + i_c]).astype(jnp.int32)]
  transfers between devices with their start and end apart: 5 -> 85, of which waited for: 5 -> 31; matrix products, arithmetic and copies ran while one was open for 5% -> 27% of each run, Pallas kernels for 0% -> 14%
where the time goes in v1:
time: 543 us; the launch traced here: 533 us
  waiting for transfers between devices  154 us (28%)
  starting transfers between devices  149 us (27%)
  Pallas kernels  72.3 us (13%)
  other arithmetic  70.5 us (13%)
  local copies, waits for them, and re-layouts  61.7 us (11%)
  matrix products  21.3 us (4%)
    ppermute x12, starting transfers between devices, line_reduce(): right = lax.ppermute(to_right, axis_name, [(k, k + 1) for k in range(step)])  59.6 us
    ppermute x37, waiting for transfers between devices, swap(): return lax.ppermute(field, axis_name, [(0, 1), (1, 0)])  56.9 us
    ppermute x15, waiting for transfers between devices, exchange_line(): lax.ppermute(pick(parts, index ^ step), 'z', [(k, k ^ step) for k in rang...  52.1 us
    pallas_call x2, Pallas kernels, feed(): pl.pallas_call(feed_kernel, grid_spec=pltpu.PrefetchScalarGridSpec(num_sc...  28.5 us
    ppermute x15, starting transfers between devices, exchange_line(): lax.ppermute(pick(parts, index ^ step), 'z', [(k, k ^ step) for k in rang...  27.4 us
    ppermute x37, starting transfers between devices, swap(): return lax.ppermute(field, axis_name, [(0, 1), (1, 0)])  26.5 us
    ppermute x12, waiting for transfers between devices, line_reduce(): right = lax.ppermute(to_right, axis_name, [(k, k + 1) for k in range(step)])  18.3 us
    dot_general x5, matrix products, dot_tn(): lax.dot_general(left, right, (((0,), (0,)), ((), ())), preferred_element_...  17.9 us
  transfers between devices with their start and end apart: 85, of which 31 were waited for; matrix products, arithmetic and copies ran while one was open for 27% of the time, Pallas kernels for 14%

profile of v1, /device:TPU:0, one launch (start us, length us, event | category | flops | bytes accessed | tf_op | source)
XLA Modules:
  0.0 533.4 jit_solution(4244765305373671992)
XLA Ops:
  42.0 7.4 %project.1 = (bf16[512,1024]{1,0:T(8,128)(2,1)}, bf16[4,512,256]{2,1,0:T(8,128)(2,1)}) custom-call(s32[4]{0:T(128)} %pad_add_fusion.ids, bf16[512,1024]{1,0:T(8,128)(2,1)} %pad_maximum_fusion.4.x_ref, f32[1,1024]{1,0:T(1,128)} %bitcast.356, bf16[1024,1024]{1,0:T(8,128)(2,1)} %wq_ref.3, bf16[1024,512]{1,0:T(8,128)(2,1)} %wk_ref.3, bf16[1024,512]{1,0:T(8,128)(2,1)} %wv_ref.1, ...), custom_call_target="tpu_custom_call" | custom-call | flops 1073741824 | bytes 6291456 | tf_op jit(solution)/shard_map/project/pallas_call | solution.py:170
  63.1 14.7 %collective-permute-done.2 = bf16[512,256]{1,0:T(8,128)(2,1)S(1)} collective-permute-done((bf16[512,256]{1,0:T(8,128)(2,1)S(1)}, bf16[512,256]{1,0:T(8,128)(2,1)S(1)}, u32[]{:S(2)}, u32[]{:S(2)}) %collective-permute-start.2) | collective-permute-done | bytes 262176 | tf_op jit(solution)/shard_map/ppermute | solution.py:92
  81.4 9.5 %attend.1 = (bf16[2048,128]{1,0:T(8,128)(2,1)}, f32[2048,128]{1,0:T(8,128)}, bf16[2,2048,128]{2,1,0:T(8,128)(2,1)}, bf16[2048,128]{1,0:T(8,128)(2,1)}, bf16[2048,128]{1,0:T(8,128)(2,1)}) custom-call(bf16[2048,256]{1,0:T(8,128)(2,1)} %bitcast.338, bf16[2048,128]{1,0:T(8,128)(2,1)} %select_convert_fusion.1.segq_ref, bf16[2048,128]{1,0:T(8,128)(2,1)} %select_convert_fusion.segk_ref), custom_call_target="tpu_custom_call" | custom-call | flops 4294967296 | bytes 6291456 | tf_op jit(solution)/shard_map/attend/pallas_call | solution.py:253
  103.7 4.7 collective-permute-done.5
  121.3 14.1 %feed.2 = (bf16[1024,1152]{1,0:T(8,128)(2,1)}, bf16[1024,1152]{1,0:T(8,128)(2,1)}, bf16[1024,1152]{1,0:T(8,128)(2,1)}, bf16[512,1024]{1,0:T(8,128)(2,1)}, bf16[512,1024]{1,0:T(8,128)(2,1)}) custom-call(s32[4]{0:T(128)} %pad_add_fusion.ids, bf16[512,1024]{1,0:T(8,128)(2,1)} %copy-done.8, bf16[512,1024]{1,0:T(8,128)(2,1)} %pad_maximum_fusion.6.c_ref, ...), custom_call_target="tpu_custom_call" | custom-call | flops 7247757312 | bytes 16777216 | tf_op jit(solution)/shard_map/feed/pallas_call | solution.py:413
  139.7 5.1 collective-permute-start.27
  158.8 6.5 %collective-permute-done.29 = bf16[256,1024]{1,0:T(8,128)(2,1)} collective-permute-done((bf16[256,1024]{1,0:T(8,128)(2,1)}, bf16[256,1024]{1,0:T(8,128)(2,1)}, u32[]{:S(2)}, u32[]{:S(2)}) %collective-permute-start.29) | collective-permute-done | bytes 524320 | tf_op jit(solution)/shard_map/ppermute | solution.py:593
  170.2 14.5 %feed.3 = (bf16[1024,1152]{1,0:T(8,128)(2,1)}, bf16[1024,1152]{1,0:T(8,128)(2,1)}, bf16[1024,1152]{1,0:T(8,128)(2,1)}, bf16[512,1024]{1,0:T(8,128)(2,1)}, bf16[512,1024]{1,0:T(8,128)(2,1)}) custom-call(s32[4]{0:T(128)} %pad_add_fusion.ids, bf16[512,1024]{1,0:T(8,128)(2,1)} %pad_maximum_fusion.7.h_ref, ...), custom_call_target="tpu_custom_call", output_to_operand_aliasing={{0}: (6, {}), {1}: (7, {}), {2}: (8, {})} | custom-call | flops 7247757312 | bytes 16777216 | tf_op jit(solution)/shard_map/feed/pallas_call | solution.py:413
  184.7 4.7 convolution_convert_fusion
  213.5 5.1 collective-permute-done.18
  221.1 4.8 collective-permute-start.78
  225.8 17.8 %collective-permute-done.68 = bf16[2,4,2,32,1152]{4,3,2,0,1:T(8,128)(2,1)S(1)} collective-permute-done((bf16[2,4,2,32,1152]{4,3,2,0,1:T(8,128)(2,1)S(1)}, bf16[2,4,2,32,1152]{4,3,2,0,1:T(8,128)(2,1)S(1)}, u32[]{:S(2)}, u32[]{:S(2)}) %collective-permute-start.68) | collective-permute-done | bytes 1179680 | tf_op jit(solution)/shard_map/ppermute | solution.py:43
  246.0 22.5 %collective-permute-done.59 = bf16[2,4,2,32,1152]{4,3,2,0,1:T(8,128)(2,1)S(1)} collective-permute-done((bf16[2,4,2,32,1152]{4,3,2,0,1:T(8,128)(2,1)S(1)}, bf16[2,4,2,32,1152]{4,3,2,0,1:T(8,128)(2,1)S(1)}, u32[]{:S(2)}, u32[]{:S(2)}) %collective-permute-start.59) | collective-permute-done | bytes 1179680 | tf_op jit(solution)/shard_map/ppermute | solution.py:43
  273.5 5.2 collective-permute-done.69
  281.3 4.4 collective-permute-start.60
  286.8 5.6 %collective-permute-done.60 = bf16[2,2,32,1152]{3,2,1,0:T(8,128)(2,1)S(1)} collective-permute-done((bf16[2,2,32,1152]{3,2,1,0:T(8,128)(2,1)S(1)}, bf16[2,2,32,1152]{3,2,1,0:T(8,128)(2,1)S(1)}, u32[]{:S(2)}, u32[]{:S(2)}) %collective-permute-start.60) | collective-permute-done | bytes 294944 | tf_op jit(solution)/shard_map/ppermute | solution.py:71
  294.6 4.6 collective-permute-done.32
  316.8 15.1 %attend_back.1 = (f32[2048,128]{1,0:T(8,128)}, f32[2048,128]{1,0:T(8,128)}) custom-call(bf16[2,2048,128]{2,1,0:T(8,128)(2,1)} %get-tuple-element.44.qaug_ref, bf16[2048,128]{1,0:T(8,128)(2,1)} %get-tuple-element.45.kaug_ref, bf16[2048,128]{1,0:T(8,128)(2,1)} %get-tuple-element.46.vaug_ref, f32[2048,128]{1,0:T(8,128)} %get-tuple-element.47.wide_ref, ...), custom_call_target="tpu_custom_call" | custom-call | flops 10737418240 | bytes 6291456 | tf_op jit(solution)/shard_map/attend_back/pallas_call | solution.py:313
  331.8 11.8 %unturn.1 = (bf16[2048,256]{1,0:T(8,128)(2,1)}, f32[8,128]{1,0:T(8,128)}) custom-call(s32[4]{0:T(128)} %pad_add_fusion.ids, bf16[2048,1024]{1,0:T(8,128)(2,1)} %bitcast.53.h_ref, bf16[1024,1024]{1,0:T(8,128)(2,1)} %wq_ref.3, bf16[1024,512]{1,0:T(8,128)(2,1)} %wk_ref.3, f32[2048,128]{1,0:T(8,128)} %copy-done.11, f32[2048,128]{1,0:T(8,128)} %copy-done.10, ...), custom_call_target="tpu_custom_call" | custom-call | flops 1073741824 | bytes 10485760 | tf_op jit(solution)/shard_map/unturn/pallas_call | solution.py:362
  343.6 4.8 fusion.58
  361.8 4.8 collective-permute-start.43
  379.4 4.4 collective-permute-start.61
  386.4 4.9 collective-permute-done.61
  394.0 10.2 %collective-permute-start.36 = (bf16[512,256]{1,0:T(8,128)(2,1)S(1)}, bf16[512,256]{1,0:T(8,128)(2,1)S(1)}, u32[]{:S(2)}, u32[]{:S(2)}) collective-permute-start(bf16[512,256]{1,0:T(8,128)(2,1)S(1)} %get-tuple-element.83), channel_id=1, source_target_pairs={{0,4},{2,6},{4,0},{6,2},{1,5},{3,7},{5,1},{7,3},{8,12},{10,14},{12... | collective-permute-start | bytes 786440 | tf_op jit(solution)/shard_map/ppermute | solution.py:92
  407.3 6.4 %collective-permute-done.36 = bf16[512,256]{1,0:T(8,128)(2,1)S(1)} collective-permute-done((bf16[512,256]{1,0:T(8,128)(2,1)S(1)}, bf16[512,256]{1,0:T(8,128)(2,1)S(1)}, u32[]{:S(2)}, u32[]{:S(2)}) %collective-permute-start.36) | collective-permute-done | bytes 262176 | tf_op jit(solution)/shard_map/ppermute | solution.py:92
  423.2 13.3 %collective-permute-start.71 = (bf16[2,2,32,1152]{3,2,1,0:T(8,128)(2,1)}, bf16[2,2,32,1152]{3,2,1,0:T(8,128)(2,1)}, u32[]{:S(2)}, u32[]{:S(2)}) collective-permute-start(bf16[2,2,32,1152]{3,2,1,0:T(8,128)(2,1)} %get-tuple-element.72), channel_id=1, source_target_pairs={{0,2},{2,4},{4,6},{1,3},{3,5},{5,7},{8,10},{10,12},{12,14},{9,11},... | collective-permute-start | bytes 884744 | tf_op jit(solution)/shard_map/ppermute | solution.py:71
  437.2 6.4 %collective-permute-start.62 = (bf16[2,2,32,1152]{3,2,1,0:T(8,128)(2,1)}, bf16[2,2,32,1152]{3,2,1,0:T(8,128)(2,1)}, u32[]{:S(2)}, u32[]{:S(2)}) collective-permute-start(bf16[2,2,32,1152]{3,2,1,0:T(8,128)(2,1)} %get-tuple-element.76), channel_id=1, source_target_pairs={{0,2},{2,4},{4,6},{1,3},{3,5},{5,7},{8,10},{10,12},{12,14},{9,11},... | collective-permute-start | bytes 884744 | tf_op jit(solution)/shard_map/ppermute | solution.py:71
  449.5 5.7 %collective-permute-done.46 = bf16[2,32,256]{2,1,0:T(8,128)(2,1)S(1)} collective-permute-done((bf16[2,32,256]{2,1,0:T(8,128)(2,1)S(1)}, bf16[2,32,256]{2,1,0:T(8,128)(2,1)S(1)}, u32[]{:S(2)}, u32[]{:S(2)}) %collective-permute-start.46) | collective-permute-done | bytes 32800 | tf_op jit(solution)/shard_map/ppermute | solution.py:92
  455.1 4.8 collective-permute-done.47
  477.7 8.1 %collective-permute-done.74 = bf16[2,2,32,1152]{3,2,1,0:T(8,128)(2,1)S(1)} collective-permute-done((bf16[2,2,32,1152]{3,2,1,0:T(8,128)(2,1)}, bf16[2,2,32,1152]{3,2,1,0:T(8,128)(2,1)S(1)}, u32[]{:S(2)}, u32[]{:S(2)}) %collective-permute-start.74) | collective-permute-done | bytes 294944 | tf_op jit(solution)/shard_map/ppermute | solution.py:72
  507.5 4.6 collective-permute-start.54
  519.6 5.4 %collective-permute-done.57 = bf16[2,32,512]{2,1,0:T(8,128)(2,1)S(1)} collective-permute-done((bf16[2,32,512]{2,1,0:T(8,128)(2,1)S(1)}, bf16[2,32,512]{2,1,0:T(8,128)(2,1)S(1)}, u32[]{:S(2)}, u32[]{:S(2)}) %collective-permute-start.57) | collective-permute-done | bytes 65568 | tf_op jit(solution)/shard_map/ppermute | solution.py:72
  (425 shorter events, 267.1 us)
Async XLA Ops:
  0.7 93.9 %collective-permute-start.8 = (bf16[256,1024]{1,0:T(8,128)(2,1)}, bf16[256,1024]{1,0:T(8,128)(2,1)}, u32[]{:S(2)}, u32[]{:S(2)}) collective-permute-start(bf16[256,1024]{1,0:T(8,128)(2,1)} %param.27), channel_id=1, source_target_pairs={{0,1},{1,0},{2,3},{3,2},{4,5},{5,4},{6,7},{7,6},{8,9},{9,8},{10,11... | collective-permute-start | bytes 1572872 | tf_op jit(solution)/shard_map/ppermute | solution.py:43
  1.2 95.6 %collective-permute-start.12 = (bf16[256,1024]{1,0:T(8,128)(2,1)}, bf16[256,1024]{1,0:T(8,128)(2,1)}, u32[]{:S(2)}, u32[]{:S(2)}) collective-permute-start(bf16[256,1024]{1,0:T(8,128)(2,1)} %param.27), channel_id=1, source_target_pairs={{0,8},{8,0},{1,9},{9,1},{2,10},{10,2},{3,11},{11,3},{4,12},{12,4},... | collective-permute-start | bytes 1572872 | tf_op jit(solution)/shard_map/ppermute | solution.py:43
  3.8 36.0 %collective-permute-start = (bf16[256,1024]{1,0:T(8,128)(2,1)}, bf16[256,1024]{1,0:T(8,128)(2,1)}, u32[]{:S(2)}, u32[]{:S(2)}) collective-permute-start(bf16[256,1024]{1,0:T(8,128)(2,1)} %param.14), channel_id=1, source_target_pairs={{0,1},{1,0},{2,3},{3,2},{4,5},{5,4},{6,7},{7,6},{8,9},{9,8},{10,11... | collective-permute-start | bytes 1572872 | tf_op jit(solution)/shard_map/ppermute | solution.py:43
  54.4 23.4 %collective-permute-start.2 = (bf16[512,256]{1,0:T(8,128)(2,1)S(1)}, bf16[512,256]{1,0:T(8,128)(2,1)S(1)}, u32[]{:S(2)}, u32[]{:S(2)}) collective-permute-start(bf16[512,256]{1,0:T(8,128)(2,1)S(1)} %get-tuple-element.109), channel_id=1, source_target_pairs={{0,4},{2,6},{4,0},{6,2},{1,5},{3,7},{5,1},{7,3},{8,12},{10,14},{12... | collective-permute-start | bytes 786440 | tf_op jit(solution)/shard_map/ppermute | solution.py:92
  58.8 21.5 %collective-permute-start.3 = (bf16[512,256]{1,0:T(8,128)(2,1)S(1)}, bf16[512,256]{1,0:T(8,128)(2,1)S(1)}, u32[]{:S(2)}, u32[]{:S(2)}) collective-permute-start(bf16[512,256]{1,0:T(8,128)(2,1)S(1)} %get-tuple-element.108), channel_id=1, source_target_pairs={{0,2},{2,0},{4,6},{6,4},{1,3},{3,1},{5,7},{7,5},{8,10},{10,8},{12,... | collective-permute-start | bytes 786440 | tf_op jit(solution)/shard_map/ppermute | solution.py:92
  61.8 52.5 %collective-permute-start.21 = (bf16[256,1024]{1,0:T(8,128)(2,1)}, bf16[256,1024]{1,0:T(8,128)(2,1)}, u32[]{:S(2)}, u32[]{:S(2)}) collective-permute-start(bf16[256,1024]{1,0:T(8,128)(2,1)} %constant_dynamic-slice_fusion.13), channel_id=1, source_target_pairs={{2,0},{4,2},{6,4},{3,1},{5,3},{7,5},{10,8},{12,10},{14,12},{11,9},... | collective-permute-start | bytes 1572872 | tf_op jit(solution)/shard_map/ppermute | solution.py:593
  77.8 33.0 %collective-permute-start.19 = (bf16[256,1024]{1,0:T(8,128)(2,1)}, bf16[256,1024]{1,0:T(8,128)(2,1)}, u32[]{:S(2)}, u32[]{:S(2)}) collective-permute-start(bf16[256,1024]{1,0:T(8,128)(2,1)} %constant_dynamic-slice_fusion.13), channel_id=1, source_target_pairs={{0,2},{2,4},{4,6},{1,3},{3,5},{5,7},{8,10},{10,12},{12,14},{9,11},... | collective-permute-start | bytes 1572872 | tf_op jit(solution)/shard_map/ppermute | solution.py:592
  110.8 28.9 %collective-permute-start.20 = (bf16[256,1024]{1,0:T(8,128)(2,1)}, bf16[256,1024]{1,0:T(8,128)(2,1)}, u32[]{:S(2)}, u32[]{:S(2)}) collective-permute-start(bf16[256,1024]{1,0:T(8,128)(2,1)} %collective-permute-done.19), channel_id=1, source_target_pairs={{0,1},{1,0},{2,3},{3,2},{4,5},{5,4},{6,7},{7,6},{8,9},{9,8},{10,11... | collective-permute-start | bytes 1572872 | tf_op jit(solution)/shard_map/ppermute | solution.py:43
  111.3 27.9 %collective-permute-start.23 = (bf16[256,1024]{1,0:T(8,128)(2,1)}, bf16[256,1024]{1,0:T(8,128)(2,1)}, u32[]{:S(2)}, u32[]{:S(2)}) collective-permute-start(bf16[256,1024]{1,0:T(8,128)(2,1)} %collective-permute-done.19), channel_id=1, source_target_pairs={{0,2},{2,4},{4,6},{1,3},{3,5},{5,7},{8,10},{10,12},{12,14},{9,11},... | collective-permute-start | bytes 1572872 | tf_op jit(solution)/shard_map/ppermute | solution.py:592
  114.3 34.4 %collective-permute-start.22 = (bf16[256,1024]{1,0:T(8,128)(2,1)}, bf16[256,1024]{1,0:T(8,128)(2,1)}, u32[]{:S(2)}, u32[]{:S(2)}) collective-permute-start(bf16[256,1024]{1,0:T(8,128)(2,1)} %collective-permute-done.21), channel_id=1, source_target_pairs={{0,1},{1,0},{2,3},{3,2},{4,5},{5,4},{6,7},{7,6},{8,9},{9,8},{10,11... | collective-permute-start | bytes 1572872 | tf_op jit(solution)/shard_map/ppermute | solution.py:43
  114.3 30.5 %collective-permute-start.25 = (bf16[256,1024]{1,0:T(8,128)(2,1)}, bf16[256,1024]{1,0:T(8,128)(2,1)}, u32[]{:S(2)}, u32[]{:S(2)}) collective-permute-start(bf16[256,1024]{1,0:T(8,128)(2,1)} %collective-permute-done.21), channel_id=1, source_target_pairs={{2,0},{4,2},{6,4},{3,1},{5,3},{7,5},{10,8},{12,10},{14,12},{11,9},... | collective-permute-start | bytes 1572872 | tf_op jit(solution)/shard_map/ppermute | solution.py:593
  120.1 33.8 %collective-permute-start.10 = (bf16[256,1024]{1,0:T(8,128)(2,1)S(1)}, bf16[256,1024]{1,0:T(8,128)(2,1)S(1)}, u32[]{:S(2)}, u32[]{:S(2)}) collective-permute-start(bf16[256,1024]{1,0:T(8,128)(2,1)S(1)} %constant_dynamic-slice_fusion.14), channel_id=1, source_target_pairs={{0,8},{8,0},{1,9},{9,1},{2,10},{10,2},{3,11},{11,3},{4,12},{12,4},... | collective-permute-start | bytes 1572872 | tf_op jit(solution)/shard_map/ppermute | solution.py:43
  153.9 58.6 %collective-permute-start.16 = (bf16[256,1024]{1,0:T(8,128)(2,1)}, bf16[256,1024]{1,0:T(8,128)(2,1)S(1)}, u32[]{:S(2)}, u32[]{:S(2)}) collective-permute-start(bf16[256,1024]{1,0:T(8,128)(2,1)} %dynamic-slice_bitcast_fusion.4), channel_id=1, source_target_pairs={{0,1},{1,0},{2,3},{3,2},{4,5},{5,4},{6,7},{7,6},{8,9},{9,8},{10,11... | collective-permute-start | bytes 1572872 | tf_op jit(solution)/shard_map/ppermute | solution.py:43
  158.2 348.6 %collective-permute-start.9 = (bf16[256,1024]{1,0:T(8,128)(2,1)}, bf16[256,1024]{1,0:T(8,128)(2,1)}, u32[]{:S(2)}, u32[]{:S(2)}) collective-permute-start(bf16[256,1024]{1,0:T(8,128)(2,1)} %dynamic-slice_bitcast_fusion.6), channel_id=1, source_target_pairs={{0,1},{1,0},{2,3},{3,2},{4,5},{5,4},{6,7},{7,6},{8,9},{9,8},{10,11... | collective-permute-start | bytes 1572872 | tf_op jit(solution)/shard_map/ppermute | solution.py:43
  158.7 42.5 %collective-permute-start.28 = (bf16[256,1024]{1,0:T(8,128)(2,1)}, bf16[256,1024]{1,0:T(8,128)(2,1)}, u32[]{:S(2)}, u32[]{:S(2)}) collective-permute-start(bf16[256,1024]{1,0:T(8,128)(2,1)} %collective-permute-done.27), channel_id=1, source_target_pairs={{0,1},{1,0},{2,3},{3,2},{4,5},{5,4},{6,7},{7,6},{8,9},{9,8},{10,11... | collective-permute-start | bytes 1572872 | tf_op jit(solution)/shard_map/ppermute | solution.py:43
  165.2 37.6 %collective-permute-start.30 = (bf16[256,1024]{1,0:T(8,128)(2,1)}, bf16[256,1024]{1,0:T(8,128)(2,1)}, u32[]{:S(2)}, u32[]{:S(2)}) collective-permute-start(bf16[256,1024]{1,0:T(8,128)(2,1)} %collective-permute-done.29), channel_id=1, source_target_pairs={{0,1},{1,0},{2,3},{3,2},{4,5},{5,4},{6,7},{7,6},{8,9},{9,8},{10,11... | collective-permute-start | bytes 1572872 | tf_op jit(solution)/shard_map/ppermute | solution.py:43
  189.5 30.5 %collective-permute-start.77 = (bf16[4,144,1024]{2,1,0:T(8,128)(2,1)S(1)}, bf16[4,144,1024]{2,1,0:T(8,128)(2,1)S(1)}, u32[]{:S(2)}, u32[]{:S(2)}) collective-permute-start(bf16[4,144,1024]{2,1,0:T(8,128)(2,1)S(1)} %dynamic-slice_bitcast_fusion), channel_id=1, source_target_pairs={{0,16},{16,0},{1,17},{17,1},{2,18},{18,2},{3,19},{19,3},{4,20},{20... | collective-permute-start | bytes 3538952 | tf_op jit(solution)/shard_map/ppermute | solution.py:43
  210.6 33.0 %collective-permute-start.68 = (bf16[2,4,2,32,1152]{4,3,2,0,1:T(8,128)(2,1)S(1)}, bf16[2,4,2,32,1152]{4,3,2,0,1:T(8,128)(2,1)S(1)}, u32[]{:S(2)}, u32[]{:S(2)}) collective-permute-start(bf16[2,4,2,32,1152]{4,3,2,0,1:T(8,128)(2,1)S(1)} %bitcast.334), channel_id=1, source_target_pairs={{0,16},{16,0},{1,17},{17,1},{2,18},{18,2},{3,19},{19,3},{4,20},{20... | collective-permute-start | bytes 3538952 | tf_op jit(solution)/shard_map/ppermute | solution.py:43
  212.6 55.9 %collective-permute-start.59 = (bf16[2,4,2,32,1152]{4,3,2,0,1:T(8,128)(2,1)S(1)}, bf16[2,4,2,32,1152]{4,3,2,0,1:T(8,128)(2,1)S(1)}, u32[]{:S(2)}, u32[]{:S(2)}) collective-permute-start(bf16[2,4,2,32,1152]{4,3,2,0,1:T(8,128)(2,1)S(1)} %bitcast.333), channel_id=1, source_target_pairs={{0,16},{16,0},{1,17},{17,1},{2,18},{18,2},{3,19},{19,3},{4,20},{20... | collective-permute-start | bytes 3538952 | tf_op jit(solution)/shard_map/ppermute | solution.py:43
  219.6 61.7 %collective-permute-start.31 = (bf16[256,1024]{1,0:T(8,128)(2,1)S(1)}, bf16[256,1024]{1,0:T(8,128)(2,1)S(1)}, u32[]{:S(2)}, u32[]{:S(2)}) collective-permute-start(bf16[256,1024]{1,0:T(8,128)(2,1)S(1)} %fusion.57), channel_id=1, source_target_pairs={{0,1},{1,0},{2,3},{3,2},{4,5},{5,4},{6,7},{7,6},{8,9},{9,8},{10,11... | collective-permute-start | bytes 1572872 | tf_op jit(solution)/shard_map/ppermute | solution.py:43
  221.1 128.3 %collective-permute-start.78 = (bf16[144,1024]{1,0:T(8,128)(2,1)}, bf16[144,1024]{1,0:T(8,128)(2,1)}, u32[]{:S(2)}, u32[]{:S(2)}) collective-permute-start(bf16[144,1024]{1,0:T(8,128)(2,1)} %get-tuple-element.70), channel_id=1, source_target_pairs={{0,2},{1,3},{8,10},{9,11},{16,18},{17,19},{24,26},{25,27}} | collective-permute-start | bytes 884744 | tf_op jit(solution)/shard_map/ppermute | solution.py:71
  243.6 149.4 %collective-permute-start.81 = (bf16[144,1024]{1,0:T(8,128)(2,1)}, bf16[144,1024]{1,0:T(8,128)(2,1)}, u32[]{:S(2)}, u32[]{:S(2)}) collective-permute-start(bf16[144,1024]{1,0:T(8,128)(2,1)} %get-tuple-element.71), channel_id=1, source_target_pairs={{6,4},{7,5},{14,12},{15,13},{22,20},{23,21},{30,28},{31,29}} | collective-permute-start | bytes 884744 | tf_op jit(solution)/shard_map/ppermute | solution.py:72
  278.7 94.6 %collective-permute-start.72 = (bf16[2,2,32,1152]{3,2,1,0:T(8,128)(2,1)}, bf16[2,2,32,1152]{3,2,1,0:T(8,128)(2,1)}, u32[]{:S(2)}, u32[]{:S(2)}) collective-permute-start(bf16[2,2,32,1152]{3,2,1,0:T(8,128)(2,1)} %get-tuple-element.75), channel_id=1, source_target_pairs={{6,4},{7,5},{14,12},{15,13},{22,20},{23,21},{30,28},{31,29}} | collective-permute-start | bytes 884744 | tf_op jit(solution)/shard_map/ppermute | solution.py:72
  312.7 73.0 %collective-permute-start.63 = (bf16[2,2,32,1152]{3,2,1,0:T(8,128)(2,1)}, bf16[2,2,32,1152]{3,2,1,0:T(8,128)(2,1)}, u32[]{:S(2)}, u32[]{:S(2)}) collective-permute-start(bf16[2,2,32,1152]{3,2,1,0:T(8,128)(2,1)} %get-tuple-element.79), channel_id=1, source_target_pairs={{6,4},{7,5},{14,12},{15,13},{22,20},{23,21},{30,28},{31,29}} | collective-permute-start | bytes 884744 | tf_op jit(solution)/shard_map/ppermute | solution.py:72
  373.3 20.7 %collective-permute-start.79 = (bf16[144,1024]{1,0:T(8,128)(2,1)S(1)}, bf16[144,1024]{1,0:T(8,128)(2,1)S(1)}, u32[]{:S(2)}, u32[]{:S(2)}) collective-permute-start(bf16[144,1024]{1,0:T(8,128)(2,1)S(1)} %bitcast_add_fusion.11), channel_id=1, source_target_pairs={{0,2},{2,4},{1,3},{3,5},{8,10},{10,12},{9,11},{11,13},{16,18},{18,... | collective-permute-start | bytes 884744 | tf_op jit(solution)/shard_map/ppermute | solution.py:71
  385.6 58.7 %collective-permute-start.50 = (bf16[2,4,2,32,512]{4,3,2,1,0:T(8,128)(2,1)S(1)}, bf16[2,4,2,32,512]{4,3,2,1,0:T(8,128)(2,1)S(1)}, u32[]{:S(2)}, u32[]{:S(2)}) collective-permute-start(bf16[2,4,2,32,512]{4,3,2,1,0:T(8,128)(2,1)S(1)} %dynamic-slice_bitcast_fusion.1), channel_id=1, source_target_pairs={{0,8},{8,0},{1,9},{9,1},{2,10},{10,2},{3,11},{11,3},{4,12},{12,4},... | collective-permute-start | bytes 1572872 | tf_op jit(solution)/shard_map/ppermute | solution.py:43
  393.0 27.1 %collective-permute-start.44 = (bf16[2,4,2,32,256]{4,3,2,1,0:T(8,128)(2,1)S(1)}, bf16[2,4,2,32,256]{4,3,2,1,0:T(8,128)(2,1)S(1)}, u32[]{:S(2)}, u32[]{:S(2)}) collective-permute-start(bf16[2,4,2,32,256]{4,3,2,1,0:T(8,128)(2,1)S(1)} %dynamic-slice_bitcast_fusion.14), channel_id=1, source_target_pairs={{0,8},{8,0},{1,9},{9,1},{2,10},{10,2},{3,11},{11,3},{4,12},{12,4},... | collective-permute-start | bytes 786440 | tf_op jit(solution)/shard_map/ppermute | solution.py:43
  394.0 19.7 %collective-permute-start.36 = (bf16[512,256]{1,0:T(8,128)(2,1)S(1)}, bf16[512,256]{1,0:T(8,128)(2,1)S(1)}, u32[]{:S(2)}, u32[]{:S(2)}) collective-permute-start(bf16[512,256]{1,0:T(8,128)(2,1)S(1)} %get-tuple-element.83), channel_id=1, source_target_pairs={{0,4},{2,6},{4,0},{6,2},{1,5},{3,7},{5,1},{7,3},{8,12},{10,14},{12... | collective-permute-start | bytes 786440 | tf_op jit(solution)/shard_map/ppermute | solution.py:92
  414.4 73.9 %collective-permute-start.80 = (bf16[144,1024]{1,0:T(8,128)(2,1)}, bf16[144,1024]{1,0:T(8,128)(2,1)}, u32[]{:S(2)}, u32[]{:S(2)}) collective-permute-start(bf16[144,1024]{1,0:T(8,128)(2,1)} %get-tuple-element.68), channel_id=1, source_target_pairs={{0,2},{2,4},{4,6},{1,3},{3,5},{5,7},{8,10},{10,12},{12,14},{9,11},... | collective-permute-start | bytes 884744 | tf_op jit(solution)/shard_map/ppermute | solution.py:71
  423.2 53.1 %collective-permute-start.71 = (bf16[2,2,32,1152]{3,2,1,0:T(8,128)(2,1)}, bf16[2,2,32,1152]{3,2,1,0:T(8,128)(2,1)}, u32[]{:S(2)}, u32[]{:S(2)}) collective-permute-start(bf16[2,2,32,1152]{3,2,1,0:T(8,128)(2,1)} %get-tuple-element.72), channel_id=1, source_target_pairs={{0,2},{2,4},{4,6},{1,3},{3,5},{5,7},{8,10},{10,12},{12,14},{9,11},... | collective-permute-start | bytes 884744 | tf_op jit(solution)/shard_map/ppermute | solution.py:71
  437.2 56.3 %collective-permute-start.62 = (bf16[2,2,32,1152]{3,2,1,0:T(8,128)(2,1)}, bf16[2,2,32,1152]{3,2,1,0:T(8,128)(2,1)}, u32[]{:S(2)}, u32[]{:S(2)}) collective-permute-start(bf16[2,2,32,1152]{3,2,1,0:T(8,128)(2,1)} %get-tuple-element.76), channel_id=1, source_target_pairs={{0,2},{2,4},{4,6},{1,3},{3,5},{5,7},{8,10},{10,12},{12,14},{9,11},... | collective-permute-start | bytes 884744 | tf_op jit(solution)/shard_map/ppermute | solution.py:71
  499.1 33.2 %collective-permute-start.84 = (bf16[144,1024]{1,0:T(8,128)(2,1)S(1)}, bf16[144,1024]{1,0:T(8,128)(2,1)S(1)}, u32[]{:S(2)}, u32[]{:S(2)}) collective-permute-start(bf16[144,1024]{1,0:T(8,128)(2,1)S(1)} %fusion.24), channel_id=1, source_target_pairs={{0,0},{1,8},{2,2},{3,10},{4,4},{5,12},{6,6},{7,14},{8,16},{9,24},{... | collective-permute-start | bytes 884744 | tf_op jit(solution)/shard_map/ppermute | solution.py:552
  (103 other events, 1286.5 us)

commit v2 on v1

v2 whole, which is shorter than its diff:
```python
import functools
import math

import jax
import jax.numpy as jnp
import numpy as np
from jax import lax
from jax.experimental import pallas as pl
from jax.experimental.pallas import tpu as pltpu
from jax.sharding import Mesh
from jax.sharding import PartitionSpec as P

EPSILON = 1e-05
ROPE_BASE = 1000000.0
FAR = 16384.0
LANES = 128
MIB = 1024 * 1024
ALL = ("y", "x", "z", "c")
F32 = jnp.float32
BF16 = jnp.bfloat16
CORE, PLANE, FIRST_LENGTH = 0, 1, 4


def dot_nn(left, right):
    return lax.dot_general(left, right, (((1,), (0,)), ((), ())), preferred_element_type=F32)


def dot_nt(left, right):
    return lax.dot_general(left, right, (((1,), (1,)), ((), ())), preferred_element_type=F32)


def dot_tn(left, right):
    return lax.dot_general(left, right, (((0,), (0,)), ((), ())), preferred_element_type=F32)


def after(value, *needed):
    return lax.optimization_barrier((value, needed))[0]


def pick(field, index, axis=0):
    return lax.dynamic_index_in_dim(field, index, axis, keepdims=False)


def swap(field, axis_name):
    return lax.ppermute(field, axis_name, [(0, 1), (1, 0)])


def crossed(field, step, count):
    return lax.ppermute(field, "z", [(k, k ^ step) for k in range(count)])


def pair_reduce(parts, axis_name, index, *needed):
    got = after(swap(pick(parts, 1 - index), axis_name), *needed)
    return pick(parts, index) + got


def reduce_y(parts, index, *needed):
    if parts.shape[0] == 1:
        return parts[0]
    if parts.shape[0] == 2:
        return pair_reduce(parts, "y", index, *needed)
    return lax.psum_scatter(parts, "y", scatter_dimension=0, tiled=False)


class Halving:
    def __init__(self, parts, index):
        self.parts, self.index, self.step, self.count = parts, index, 1, parts.shape[0]

    def advance(self, *needed):
        far = self.parts.shape[0] // 2
        parts = self.parts.reshape(far, 2, *self.parts.shape[1:])
        bit = (self.index // self.step) % 2
        sent = pick(parts, 1 - bit, 1)
        kept = pick(parts, bit, 1)
        if needed:
            sent = after(sent, *needed)
        self.parts = kept + crossed(sent, self.step, self.count)
        self.step = self.step * 2

    def finish(self):
        while self.step < self.count:
            self.advance()
        return self.parts[0]


def in_order(index, own, other, axis):
    return jnp.concatenate(
        [jnp.where(index == 0, own, other), jnp.where(index == 0, other, own)], axis=axis)


def sum_all(vector, rows_y, rows_z):
    vector = vector + swap(vector, "c")
    vector = vector + swap(vector, "x")
    if rows_y == 2:
        vector = vector + swap(vector, "y")
    else:
        vector = lax.psum(vector, "y")
    step = 1
    while step < rows_z:
        vector = vector + crossed(vector, step, rows_z)
        step = step * 2
    return vector


def run_kernel(kernel, name, ids, operands, in_specs, out_shapes, out_specs, grid=(1,), scratch=(),
               vmem=32, micros=5, aliases=None):
    return pl.pallas_call(
        kernel,
        grid_spec=pltpu.PrefetchScalarGridSpec(
            num_scalar_prefetch=1, grid=grid, in_specs=in_specs, out_specs=out_specs,
            scratch_shapes=list(scratch)),
        out_shape=out_shapes,
        input_output_aliases=aliases or {},
        compiler_params=pltpu.CompilerParams(vmem_limit_bytes=vmem * MIB),
        cost_estimate=pl.CostEstimate(
            flops=int(micros * 1.15e9), bytes_accessed=MIB, transcendentals=0),
        name=name,
    )(ids, *operands)


def whole(shape):
    return pl.BlockSpec(tuple(shape), lambda i, ids: (0,) * len(shape))


def of_core(rows, cols):
    return pl.BlockSpec((rows, cols), lambda i, ids: (0, ids[CORE]))


def shaped(*shape, dtype=BF16):
    return jax.ShapeDtypeStruct(shape, dtype)


def lane_ids(rows):
    return lax.broadcasted_iota(jnp.int32, (rows, LANES), 1)


def half_swap(field, lanes):
    return jnp.where(
        (lanes & 63) < 32, pltpu.roll(field, LANES - 32, 1), pltpu.roll(field, 32, 1))


def half_sums(field, lanes):
    low = jnp.sum(jnp.where(lanes < 64, field, 0.0), axis=1, keepdims=True)
    high = jnp.sum(jnp.where(lanes < 64, 0.0, field), axis=1, keepdims=True)
    return jnp.where(lanes < 64, low, high)


def tables(ids, slots, first_row, rows, freq):
    token = lax.broadcasted_iota(jnp.int32, (rows, LANES), 0) + first_row
    start = jnp.zeros((rows, LANES), jnp.int32)
    edge = jnp.int32(0)
    for slot in range(slots - 1):
        edge = edge + ids[FIRST_LENGTH + slot]
        start = jnp.where(token >= edge, edge, start)
    angles = (token - start).astype(F32) * freq
    sines = jnp.sin(angles)
    return jnp.cos(angles), jnp.where((lane_ids(rows) & 63) < 32, -sines, sines)


def project_kernel(head_size, slots, ids, xo_ref, xt_ref, gain_ref, wq_ref, wk_ref, wv_ref,
                   freq_ref, qg_ref, kg_ref, ho_ref, ht_ref, *refs):
    outs, packed = refs[:-1], refs[-1]
    heads, rows, _ = packed.shape
    turn = pl.program_id(0)
    x = jnp.where(turn == 0, xo_ref[...], xt_ref[...]).astype(F32)
    scale = lax.rsqrt(jnp.mean(x * x, axis=1, keepdims=True) + EPSILON)
    h = (x * scale * gain_ref[...]).astype(BF16)

    @pl.when(turn == 0)
    def _():
        ho_ref[...] = h

    @pl.when(turn == 1)
    def _():
        ht_ref[...] = h

    lanes = lane_ids(rows)
    spot = jnp.bitwise_xor(turn, ids[CORE])
    cosine, sine = tables(ids, slots, (ids[PLANE] * 2 + spot) * rows, rows, freq_ref[...])

    def turned(raw, gain):
        unit = raw * lax.rsqrt(half_sums(raw * raw, lanes) * (1.0 / head_size) + EPSILON) * gain
        return unit * cosine + half_swap(unit, lanes) * sine

    q_raw = dot_nn(h, wq_ref[...])
    k_raw = dot_nn(h, wk_ref[...])
    v_raw = dot_nn(h, wv_ref[...])
    for head in range(heads):
        span = slice(head * LANES, (head + 1) * LANES)
        packed[head, :, 0:LANES] = turned(q_raw[:, span], qg_ref[...]).astype(BF16)
    for pair in range(heads // 2):
        span = slice(pair * LANES, (pair + 1) * LANES)
        keys = turned(k_raw[:, span], kg_ref[...])
        values = v_raw[:, span]
        even = jnp.where(lanes < 64, keys, pltpu.roll(values, 64, 1))
        odd = jnp.where(lanes < 64, pltpu.roll(keys, 64, 1), values)
        packed[2 * pair, :, LANES:] = even.astype(BF16)
        packed[2 * pair + 1, :, LANES:] = odd.astype(BF16)
    for step in range(heads):
        outs[step][...] = packed[jnp.bitwise_xor(ids[PLANE], step)]


def project(ids, x_own, x_other, gain, w_query, w_key, w_value, freq, qg, kg, head_size, slots,
            heads):
    rows, width = x_own.shape
    block = pl.BlockSpec((rows, 2 * LANES), lambda i, ids: (jnp.bitwise_xor(i, ids[CORE]), 0))
    part = whole((rows, width))
    row = whole((1, LANES))
    return run_kernel(
        functools.partial(project_kernel, head_size, slots), "project", ids,
        (x_own, x_other, gain, w_query, w_key, w_value, freq, qg, kg),
        [part, part, whole((1, width)), of_core(width, w_query.shape[1] // 2),
         of_core(width, w_key.shape[1] // 2), of_core(width, w_value.shape[1] // 2), row, row, row],
        [shaped(rows, width)] * 2 + [shaped(2 * rows, 2 * LANES)] * heads,
        [part, part] + [block] * heads,
        grid=(2,), scratch=[pltpu.VMEM((heads, rows, 2 * LANES), BF16)], vmem=32,
        micros=5)


def three_parts(value):
    high = value.astype(BF16).astype(F32)
    rest = value - high
    middle = rest.astype(BF16).astype(F32)
    return high, middle, rest - middle


def marked(lanes, first, value, otherwise):
    high, middle, low = three_parts(value)
    return jnp.where(
        lanes == first, high,
        jnp.where(lanes == first + 1, middle, jnp.where(lanes == first + 2, low, otherwise)))


def below(rows, cols):
    return lax.broadcasted_iota(jnp.int32, (rows, cols), 1) <= lax.broadcasted_iota(
        jnp.int32, (rows, cols), 0)


def attend_kernel(slots, ids, *refs):
    count = (len(refs) - 4) // 2
    arrived, sent = refs[:count], refs[count : 2 * count]
    wide_ref, qaug_ref, kaug_ref, vaug_ref = refs[2 * count :]
    block = arrived[0].shape[0]
    mark = 64 + slots
    lanes = lane_ids(block)
    plane = ids[PLANE]
    slot_lane = (lanes >= 64) & (lanes < mark)
    ones_lane = (lanes >= mark) & (lanes < mark + 3)
    for step in range(count):
        first = pl.multiple_of(jnp.bitwise_xor(plane, step) * block, block)
        span = pl.ds(first, block)
        token = lax.broadcasted_iota(jnp.int32, (block, LANES), 0) + first
        inside = lanes < 0
        edge = jnp.int32(0)
        for slot in range(slots):
            stop = edge + ids[FIRST_LENGTH + slot]
            inside = inside | ((lanes == 64 + slot) & (token >= edge) & (token < stop))
            edge = stop
        segq = jnp.where(inside, 1.0, 0.0)
        segk = jnp.where(ones_lane, 1.0, jnp.where(slot_lane & jnp.logical_not(inside), -FAR, 0.0))
        pair = arrived[step][:, 0:LANES].astype(F32)
        keyval = arrived[step][:, LANES:].astype(F32)
        qaug_ref[0, span, :] = jnp.where(lanes < 64, pair, segq).astype(BF16)
        qaug_ref[1, span, :] = jnp.where(lanes < 64, pltpu.roll(pair, 64, 1), segq).astype(BF16)
        kaug_ref[span, :] = jnp.where(lanes < 64, keyval, segk).astype(BF16)
        vaug_ref[span, :] = jnp.where(
            lanes < 64, pltpu.roll(keyval, 64, 1), jnp.where(lanes < 67, 1.0, 0.0)).astype(BF16)
    for i in range(count):
        span = slice(i * block, (i + 1) * block)
        outs = []
        for head in range(2):
            queries = qaug_ref[head, span, :]
            total = jnp.zeros((block, LANES), F32)
            for j in range(i + 1):
                other = slice(j * block, (j + 1) * block)
                weights = jnp.exp2(dot_nt(queries, kaug_ref[other, :]))
                if j == i:
                    weights = jnp.where(below(block, block), weights, 0.0)
                total = total + dot_nn(weights.astype(BF16), vaug_ref[other, :])
            row_sum = total[:, 64:65]
            outs.append(total * (1.0 / row_sum))
            qaug_ref[head, span, :] = marked(
                lanes, mark, -jnp.log2(row_sum), queries.astype(F32)).astype(BF16)
        wide_ref[span, :] = jnp.where(lanes < 64, outs[0], pltpu.roll(outs[1], 64, 1))
    for step in range(count):
        first = pl.multiple_of(jnp.bitwise_xor(plane, step) * block, block)
        sent[step][...] = wide_ref[pl.ds(first, block), :].astype(BF16)


def attend(ids, arrived, slots):
    count, block = len(arrived), arrived[0].shape[0]
    rows = count * block
    outs = [shaped(block, LANES)] * count + [
        shaped(rows, LANES, dtype=F32), shaped(2, rows, LANES), shaped(rows, LANES),
        shaped(rows, LANES)]
    return run_kernel(
        functools.partial(attend_kernel, slots), "attend", ids, arrived,
        [whole(a.shape) for a in arrived], outs, [whole(o.shape) for o in outs], vmem=40,
        micros=9)


def middle_kernel(count, ids, *refs):
    own, other = refs[:count], refs[count : 2 * count]
    xo_ref, xt_ref, w_ref, gain_ref, y_ref, ho_ref, ht_ref, o_ref = refs[2 * count :]
    turn = pl.program_id(0)
    y = jnp.where(turn == 0, xo_ref[...], xt_ref[...]).astype(F32)
    for core, blocks in ((ids[CORE], own), (1 - ids[CORE], other)):
        for step in range(count):
            head = core * count + jnp.bitwise_xor(ids[PLANE], step)
            span = pl.ds(pl.multiple_of(head * LANES, LANES), LANES)
            part = blocks[step][...]
            o_ref[:, span] = part
            y = y + dot_nn(part, w_ref[span, :])
    h = (y * lax.rsqrt(jnp.mean(y * y, axis=1, keepdims=True) + EPSILON) * gain_ref[...]).astype(
        BF16)

    @pl.when(turn == 0)
    def _():
        y_ref[...] = y
        ho_ref[...] = h

    @pl.when(turn == 1)
    def _():
        ht_ref[...] = h


def middle(ids, own, other, x_own, x_other, w_out, gain):
    rows, width = x_own.shape
    count = len(own)
    block = pl.BlockSpec((rows, LANES), lambda i, ids: (jnp.bitwise_xor(i, ids[CORE]), 0))
    part = whole((rows, width))
    return run_kernel(
        functools.partial(middle_kernel, count), "middle", ids,
        (*own, *other, x_own, x_other, w_out, gain),
        [block] * (2 * count) + [part, part, whole(w_out.shape), whole((1, width))],
        [shaped(rows, width, dtype=F32), shaped(rows, width), shaped(rows, width),
         shaped(2 * rows, width)],
        [part, part, part, pl.BlockSpec((rows, width), lambda i, ids: (i, 0))],
        grid=(2,), vmem=24, micros=4)


def feed_kernel(ids, ho_ref, ht_ref, co_ref, ct_ref, wg_ref, wu_ref, wd_ref, *refs):
    m_ref, dg_ref, du_ref, ha_ref, ca_ref, do_ref, dt_ref, yo_ref, yt_ref = refs[-9:]
    rows = ho_ref.shape[0]
    ha_ref[0:rows, :] = ho_ref[...]
    ha_ref[rows:, :] = ht_ref[...]
    ca_ref[0:rows, :] = co_ref[...]
    ca_ref[rows:, :] = ct_ref[...]
    gate = dot_nn(ha_ref[...], wg_ref[...])
    up = dot_nn(ha_ref[...], wu_ref[...])
    sig = jax.nn.sigmoid(gate)
    silu = gate * sig
    m_ref[...] = (silu * up).astype(BF16)
    dm = dot_nt(ca_ref[...], wd_ref[...])
    dg_ref[...] = (dm * up * sig * (1.0 + gate * (1.0 - sig))).astype(BF16)
    du_ref[...] = (dm * silu).astype(BF16)
    dh = dot_nt(dg_ref[...], wg_ref[...]) + dot_nt(du_ref[...], wu_ref[...])
    do_ref[...] = dh[:rows].astype(BF16)
    dt_ref[...] = dh[rows:].astype(BF16)
    y = dot_nn(m_ref[...], wd_ref[...])
    yo_ref[...] = y[:rows].astype(BF16)
    yt_ref[...] = y[rows:].astype(BF16)


def feed(ids, h_own, h_other, c_own, c_other, w_gate, w_up, w_down, earlier):
    rows, width = h_own.shape
    units = w_gate.shape[1]
    half = 1 if earlier else 0
    part = whole((rows, width))
    kept = lambda cols: pl.BlockSpec((2 * rows, cols), lambda i, ids: (half, 0))
    cols = [units] * 3 + [width] * 2
    return run_kernel(
        feed_kernel, "feed", ids, (h_own, h_other, c_own, c_other, w_gate, w_up, w_down, *earlier),
        [part] * 4 + [whole(w.shape) for w in (w_gate, w_up, w_down)]
        + [pl.BlockSpec(memory_space=pl.ANY)] * len(earlier),
        [shaped(4 * rows, n) for n in cols] + [shaped(rows, width)] * 4,
        [kept(n) for n in cols] + [part] * 4,
        vmem=44, micros=12, aliases={8 + k: k for k in range(len(earlier))})


def turn_kernel(ids, near_ref, twin_ref, far_ref, y_ref, c_ref, gain_ref, dy_ref, da_ref, sum_ref):
    y = y_ref[...]
    grad = near_ref[...].astype(F32) + twin_ref[...].astype(F32) + far_ref[...].astype(F32)
    scale = lax.rsqrt(jnp.mean(y * y, axis=1, keepdims=True) + EPSILON)
    unit = y * scale
    scaled = grad * gain_ref[...]
    inner = jnp.mean(scaled * unit, axis=1, keepdims=True)
    dy = c_ref[...].astype(F32) + scale * (scaled - unit * inner)
    dy_ref[...] = dy
    da_ref[...] = dy.astype(BF16)
    sum_ref[...] = jnp.sum(grad * unit, axis=0, keepdims=True)


def turn(ids, near, twin, far, y, c, gain):
    part, line = whole(y.shape), whole(gain.shape)
    return run_kernel(
        turn_kernel, "turn", ids, (near, twin, far, y, c, gain), [part] * 5 + [line],
        [shaped(*y.shape, dtype=F32), shaped(*y.shape), shaped(*gain.shape, dtype=F32)],
        [part, part, line], vmem=24, micros=2)


def heads_kernel(count, ids, ao_ref, at_ref, w_ref, cols_ref, *outs):
    a = jnp.where(pl.program_id(0) == 0, ao_ref[...], at_ref[...])
    half = cols_ref.shape[1]
    cols_ref[...] = jnp.where(ids[CORE] == 0, a[:, :half], a[:, half:])
    for step in range(count):
        head = ids[CORE] * count + jnp.bitwise_xor(ids[PLANE], step)
        span = pl.ds(pl.multiple_of(head * LANES, LANES), LANES)
        outs[step][...] = dot_nt(a, w_ref[span, :]).astype(BF16)


def to_heads(ids, da_own, da_other, w_out, count):
    rows, width = da_own.shape
    block = pl.BlockSpec((rows, LANES), lambda i, ids: (jnp.bitwise_xor(i, ids[CORE]), 0))
    part = whole((rows, width))
    return run_kernel(
        functools.partial(heads_kernel, count), "to_heads", ids, (da_own, da_other, w_out),
        [part, part, whole(w_out.shape)],
        [shaped(2 * rows, width // 2)] + [shaped(2 * rows, LANES)] * count,
        [pl.BlockSpec((rows, width // 2), lambda i, ids: (i, 0))] + [block] * count,
        grid=(2,), vmem=24, micros=2)


def attend_back_kernel(ids, qaug_ref, kaug_ref, vaug_ref, wide_ref, *refs):
    arrived, (dq_ref, dkv_ref, doaug, dq_sum) = refs[:-4], refs[-4:]
    count, block = len(arrived), arrived[0].shape[0]
    lanes = lane_ids(block)
    for step in range(count):
        first = pl.multiple_of(jnp.bitwise_xor(ids[PLANE], step) * block, block)
        span = pl.ds(first, block)
        do_pair = arrived[step][...].astype(F32)
        inner = do_pair * wide_ref[span, :]
        low = jnp.sum(jnp.where(lanes < 64, inner, 0.0), axis=1, keepdims=True)
        high = jnp.sum(jnp.where(lanes < 64, 0.0, inner), axis=1, keepdims=True)
        doaug[0, span, :] = jnp.where(
            lanes < 64, do_pair, marked(lanes, 64, -low, 0.0)).astype(BF16)
        doaug[1, span, :] = jnp.where(
            lanes < 64, pltpu.roll(do_pair, 64, 1), marked(lanes, 64, -high, 0.0)).astype(BF16)
    dq_sum[...] = jnp.zeros(dq_sum.shape, F32)
    for j in range(count):
        here = slice(j * block, (j + 1) * block)
        keys = kaug_ref[here, :]
        values = vaug_ref[here, :]
        dk = jnp.zeros((LANES, block), F32)
        dv = jnp.zeros((LANES, block), F32)
        for i in range(j, count):
            span = slice(i * block, (i + 1) * block)
            for head in range(2):
                queries = qaug_ref[head, span, :]
                grads = doaug[head, span, :]
                weights = jnp.exp2(dot_nt(queries, keys))
                if j == i:
                    weights = jnp.where(below(block, block), weights, 0.0)
                slopes = (weights * dot_nt(grads, values)).astype(BF16)
                dv = dv + dot_tn(grads, weights.astype(BF16))
                dk = dk + dot_tn(queries, slopes)
                dq_sum[head, span, :] = dq_sum[head, span, :] + dot_nn(slopes, keys)
        dk_rows = jnp.transpose(dk) * math.log(2.0)
        dv_rows = jnp.transpose(dv)
        dkv_ref[here, :] = jnp.where(lanes < 64, dk_rows, pltpu.roll(dv_rows, 64, 1))
    for i in range(count):
        span = slice(i * block, (i + 1) * block)
        dq_ref[span, :] = jnp.where(
            lanes < 64, dq_sum[0, span, :], pltpu.roll(dq_sum[1, span, :], 64, 1)) * 0.125


def attend_back(ids, qaug, kaug, vaug, wide, arrived):
    rows = kaug.shape[0]
    operands = (qaug, kaug, vaug, wide, *arrived)
    outs = [shaped(rows, LANES, dtype=F32)] * 2
    return run_kernel(
        attend_back_kernel, "attend_back", ids, operands, [whole(a.shape) for a in operands], outs,
        [whole(o.shape) for o in outs],
        scratch=[pltpu.VMEM((2, rows, LANES), BF16), pltpu.VMEM((2, rows, LANES), F32)], vmem=44,
        micros=13)


def pair_of(wk, wv, odd, lanes):
    keys = jnp.where(odd, pltpu.roll(wk, 64, 1), wk)
    values = jnp.where(odd, wv, pltpu.roll(wv, 64, 1))
    return jnp.where(lanes < 64, keys, values)


def unturn_kernel(head_size, ids, *refs):
    count = (len(refs) - 13) // 3
    blocks = refs[: 2 * count]
    wq_ref, wk_ref, wv_ref, cos_ref, sin_ref, qg_ref, kg_ref, dq_ref, dkv_ref = refs[
        2 * count : 2 * count + 9]
    backs = refs[2 * count + 9 : 3 * count + 9]
    grad_ref, row_ref, gains_ref, total = refs[3 * count + 9 :]
    rows = blocks[0].shape[0]
    width = wq_ref.shape[0]
    lanes = lane_ids(rows)
    odd = (ids[PLANE] & 1) == 1
    wkv = pair_of(
        wk_ref[...].astype(F32), wv_ref[...].astype(F32), odd, lane_ids(width)).astype(BF16)
    wq = wq_ref[...]

    def undo(raw, grad, gain, cosine, sine):
        scale = lax.rsqrt(half_sums(raw * raw, lanes) * (1.0 / head_size) + EPSILON)
        unit = raw * scale
        back = grad * cosine - half_swap(grad, lanes) * sine
        scaled = back * gain
        mean = half_sums(scaled * unit, lanes) * (1.0 / head_size)
        return scale * (scaled - unit * mean), jnp.sum(back * unit, axis=0, keepdims=True)

    q_gain = jnp.zeros((1, LANES), F32)
    k_gain = jnp.zeros((1, LANES), F32)
    for step in range(count):
        for twin in range(2):
            h = blocks[2 * step + twin][...]
            spot = jnp.bitwise_xor(ids[CORE], twin)
            first = pl.multiple_of(
                (jnp.bitwise_xor(ids[PLANE], step) * 2 + spot) * rows, rows)
            span = pl.ds(first, rows)
            cosine, sine = cos_ref[span, :], sin_ref[span, :]
            dkv = dkv_ref[span, :]
            dqr, add_q = undo(dot_nn(h, wq), dq_ref[span, :], qg_ref[...], cosine, sine)
            dkr, add_k = undo(
                dot_nn(h, wkv), jnp.where(lanes < 64, dkv, 0.0), kg_ref[...], cosine, sine)
            q_gain = q_gain + add_q
            k_gain = k_gain + add_k
            dqr = dqr.astype(BF16)
            dkr = jnp.where(lanes < 64, dkr, dkv).astype(BF16)
            place = pl.ds(pl.multiple_of(spot * rows, rows), rows)
            backs[step][place, 0:LANES] = dqr
            backs[step][place, LANES:] = dkr
            for at, grad in ((slice(0, LANES), dqr), (slice(LANES, 2 * LANES), dkr)):
                term = dot_tn(grad, h)
                total[at, :] = term if step + twin == 0 else total[at, :] + term
    gains_ref[...] = jnp.concatenate([q_gain, k_gain, jnp.zeros((6, LANES), F32)], axis=0)
    for at, weight in ((slice(0, LANES), wq), (slice(LANES, 2 * LANES), wkv)):
        grad_ref[:, at] = jnp.transpose(total[at, :]).astype(BF16)
    row_ref[...] = jnp.sum(
        jnp.transpose(wq.astype(F32)) * total[0:LANES, :]
        + jnp.transpose(wkv.astype(F32)) * total[LANES:, :], axis=0, keepdims=True)


def unturn(ids, blocks, w_query, w_key, w_value, cosine, sine, qg, kg, dq, dkv, head_size, heads):
    rows, width = blocks[0].shape
    count = len(blocks) // 2
    head = lambda ids: ids[CORE] * heads + ids[PLANE]
    pair = pl.BlockSpec((width, LANES), lambda i, ids: (0, head(ids) // 2))
    row = whole((1, LANES))
    outs = [shaped(2 * rows, 2 * LANES)] * count + [
        shaped(width, 2 * LANES), shaped(1, width, dtype=F32), shaped(8, LANES, dtype=F32)]
    return run_kernel(
        functools.partial(unturn_kernel, head_size), "unturn", ids,
        (*blocks, w_query, w_key, w_value, cosine, sine, qg, kg, dq, dkv),
        [whole((rows, width))] * (2 * count)
        + [pl.BlockSpec((width, LANES), lambda i, ids: (0, head(ids))), pair, pair,
           whole(cosine.shape), whole(sine.shape), row, row, whole(dq.shape), whole(dkv.shape)],
        outs, [whole(o.shape) for o in outs],
        scratch=[pltpu.VMEM((2 * LANES, width), F32)], vmem=44, micros=7)


def back_kernel(ids, *refs):
    arrived, (wq_ref, wk_ref, wv_ref, own_ref, other_ref) = refs[:-5], refs[-5:]
    rows, width = own_ref.shape
    total = [jnp.zeros((rows, width), F32)] * 2
    for step in range(len(arrived)):
        head = jnp.bitwise_xor(ids[PLANE], step)
        span = pl.ds(pl.multiple_of(head * LANES, LANES), LANES)
        both = pl.ds(pl.multiple_of(head // 2 * LANES, LANES), LANES)
        wkv = pair_of(wk_ref[:, both].astype(F32), wv_ref[:, both].astype(F32), (head & 1) == 1,
                      lane_ids(width)).astype(BF16)
        wq = wq_ref[:, span]
        for twin in range(2):
            spot = jnp.bitwise_xor(ids[CORE], twin)
            grads = arrived[step][pl.ds(pl.multiple_of(spot * rows, rows), rows), :]
            total[twin] = total[twin] + dot_nt(grads[:, :LANES], wq) + dot_nt(grads[:, LANES:], wkv)
    own_ref[...] = total[0].astype(BF16)
    other_ref[...] = total[1].astype(BF16)


def to_tokens(ids, arrived, w_query, w_key, w_value):
    width = w_query.shape[0]
    rows = arrived[0].shape[0] // 2
    return run_kernel(
        back_kernel, "to_tokens", ids, (*arrived, w_query, w_key, w_value),
        [whole(a.shape) for a in arrived]
        + [of_core(width, w.shape[1] // 2) for w in (w_query, w_key, w_value)],
        [shaped(rows, width)] * 2, [whole((rows, width))] * 2, vmem=24, micros=4)


def last_kernel(ids, mine_ref, twin_ref, x_ref, dy_ref, gain_ref, out_ref):
    x = x_ref[...].astype(F32)
    scaled = (mine_ref[...].astype(F32) + twin_ref[...].astype(F32)) * gain_ref[...]
    scale = lax.rsqrt(jnp.mean(x * x, axis=1, keepdims=True) + EPSILON)
    unit = x * scale
    inner = jnp.mean(scaled * unit, axis=1, keepdims=True)
    out_ref[...] = dy_ref[...] + scale * (scaled - unit * inner)


def last(ids, mine, twin, x, dy, gain):
    part = whole(x.shape)
    return run_kernel(
        last_kernel, "last", ids, (mine, twin, x, dy, gain), [part] * 4 + [whole(gain.shape)],
        shaped(*x.shape, dtype=F32), part, vmem=24, micros=2)


def body(tokens, lengths, attn_gain, w_query, w_key, w_value, query_gain, key_gain, w_out,
         ffn_gain, w_gate, w_up, w_down, cotangent):
    rows, width = tokens.shape
    head_size = query_gain.shape[0]
    n_y, n_z = lax.axis_size("y"), lax.axis_size("z")
    i_y, i_x, i_z, i_c = (lax.axis_index(name) for name in ALL)
    heads = w_key.shape[1] // head_size // 2
    slots = lengths.shape[1]
    ids = jnp.concatenate(
        [jnp.stack([i_c, i_z, i_x, i_y]).astype(jnp.int32), lengths[0].astype(jnp.int32)])
    lane = np.arange(LANES)
    freq = jnp.asarray(
        (ROPE_BASE ** (-2.0 * (lane % (head_size // 2)) / head_size)).astype(np.float32))[None, :]
    to_exp2 = math.log2(math.e) / math.sqrt(head_size)
    qg = jnp.tile(query_gain, 2)[None, :]
    kg = jnp.tile(key_gain, 2)[None, :]
    a_gain, f_gain = attn_gain[None, :], ffn_gain[None, :]
    steps = range(1, n_z)

    x_other = swap(tokens, "c")
    h_own, h_other, *packed = project(
        ids, tokens, x_other, a_gain, w_query, w_key, w_value, freq, qg * to_exp2, kg, head_size,
        slots, heads)
    arrived = [packed[0]] + [crossed(packed[s], s, n_z) for s in steps]

    cot, lengths_late, *w_late = after(
        (cotangent, lengths, w_gate, w_up, w_down), packed[0])
    cot_other = swap(cot, "c")
    cot_far = swap(cot, "x")
    cot_far_other = swap(cot_far, "c")
    units = w_gate.shape[1] // 4
    place = (2 * i_x + i_c) * units
    wg, wu = (lax.dynamic_slice_in_dim(w, place, units, 1) for w in w_late[:2])
    wd = lax.dynamic_slice_in_dim(w_late[2], place, units, 0)
    token = jnp.arange(2 * rows * n_z, dtype=jnp.int32)
    start, edge = jnp.zeros_like(token), jnp.zeros((), jnp.int32)
    for slot in range(slots - 1):
        edge = edge + lengths_late[0, slot]
        start = jnp.where(token >= edge, edge, start)
    angles = (token - start).astype(F32)[:, None] * freq
    sign = jnp.asarray(np.where(lane % head_size < head_size // 2, -1.0, 1.0).astype(np.float32))
    cosine, sine = jnp.cos(angles), jnp.sin(angles) * sign[None, :]

    *o_sent, wide, qaug, kaug, vaug = attend(ids, arrived, slots)
    o_own = [o_sent[0]] + [crossed(o_sent[s], s, n_z) for s in steps]
    o_other = [swap(o, "c") for o in o_own]
    y_mine, h2_own, h2_other, o_rows = middle(
        ids, o_own, o_other, tokens, x_other, w_out, f_gain)

    h_line = after(h_own, o_own[-1])
    blocks = [h_own, h_other]
    for s in steps:
        one = crossed(h_line, s, n_z)
        blocks += [one, swap(one, "c")]

    h2_far = swap(h2_own, "x")
    *kept, d_own, d_other, y_own, y_other = feed(
        ids, h2_own, h2_other, cot, cot_other, wg, wu, wd, ())
    h2_far_other = swap(after(h2_far, d_own), "c")
    d_twin = swap(d_other, "c")
    *kept, d_far, d_far_other, y_far, y_far_other = feed(
        ids, h2_far, h2_far_other, cot_far, cot_far_other, wg, wu, wd, tuple(kept))
    d_home = swap(d_far + swap(d_far_other, "c"), "x")

    m, dg, du, h2_all, cot_all = kept
    piece = units // (n_y * n_z)
    row_block = width // (n_y * 2 * n_z * 2)
    m, dg, du = after((m, dg, du), d_far_other, *blocks[2:])

    dy, da, gain_ffn = turn(ids, d_own, d_twin, d_home, y_mine, cotangent, f_gain)
    da_other = swap(da, "c")
    da_cols, *do_sent = to_heads(ids, da, da_other, w_out, heads)
    do_arrived = [do_sent[0]] + [crossed(do_sent[s], s, n_z) for s in steps]
    dq, dkv = attend_back(ids, qaug, kaug, vaug, wide, do_arrived)

    down = dot_tn(m, cot_all).astype(BF16).reshape(n_z, n_y, piece, width)
    down = Halving(reduce_y(jnp.moveaxis(down, 1, 0), i_y, do_sent[0]), i_z)

    def over_y(grad, *needed):
        grad = grad.astype(BF16).reshape(n_y, 2, n_z, 2, row_block, -1)
        return Halving(jnp.moveaxis(reduce_y(grad, i_y, *needed), 1, 0), i_z)

    down.advance(do_arrived[-1])
    out_parts = dot_tn(o_rows, after(da_cols, do_sent[0])).astype(BF16).reshape(
        n_y, 2, n_z, 2, row_block, width // 2)
    out_parts = pair_reduce(jnp.moveaxis(out_parts, 1, 0), "x", i_x, dq)

    *back, grad_head, gain_attn, gains = unturn(
        ids, blocks, w_query, w_key, w_value, cosine, sine, qg, kg, dq, dkv, head_size, heads)
    back_arrived = [back[0]] + [crossed(back[s], s, n_z) for s in steps]
    late = back_arrived[-1]
    gate = over_y(dot_tn(h2_all, dg), back[0])
    up = over_y(dot_tn(h2_all, du), late)
    down.advance(dq)
    gate.advance()
    dh_own, dh_other = to_tokens(ids, back_arrived, w_query, w_key, w_value)
    grad_tokens = last(ids, dh_own, swap(dh_other, "c"), tokens, dy, a_gain)

    gate.advance(late)
    up.advance()
    owners = []
    for y in range(n_y):
        for x in range(2):
            for z in range(n_z):
                for c in range(2):
                    source = ((y * 2 + x) * n_z + z) * 2 + c
                    owners.append((source, n_y * n_z * (2 * x + c) + z * n_y + y))
    share_down = lax.ppermute(after(down.finish(), late), ALL, owners).astype(F32)

    def spread(parts):
        got = swap(pick(parts, 1 - i_c, 1), "c")
        cols = in_order(i_c, pick(parts, i_c, 1), got, 2)
        got = swap(pick(cols, 1 - i_x), "x")
        return in_order(i_x, pick(cols, i_x), got, 1).astype(F32)

    share_gate = spread(gate.finish())
    share_up = spread(up.finish())

    parts = after(grad_head, back[0]).reshape(n_y, 2, n_z, 2, row_block, 2 * LANES)
    parts = pair_reduce(jnp.moveaxis(parts, 1, 0), "x", i_x, late)
    half = width // 2
    parts = reduce_y(jnp.concatenate([out_parts, parts], axis=-1), i_y)
    got = [pick(parts, i_z)] + [crossed(pick(parts, i_z ^ s), s, n_z) for s in steps]
    out_sum = got[0][..., :half].astype(F32)
    for one in got[1:]:
        out_sum = out_sum + one[..., :half].astype(F32)
    by_step = jnp.stack(got)[..., half:]
    merged = jnp.concatenate(
        [out_sum.astype(BF16)] + [pick(by_step, i_z ^ z) for z in range(n_z)], axis=-1)
    kept_c, got = pick(merged, i_c), swap(pick(merged, 1 - i_c), "c")
    share_out = in_order(i_c, kept_c[:, :half], got[:, :half], 1).astype(F32)
    by_head = in_order(i_c, kept_c[:, half:], got[:, half:], 1).astype(F32)
    by_head = by_head.reshape(row_block, 2 * heads, 2 * LANES)
    share_query = by_head[:, :, :LANES].reshape(row_block, -1)
    share_key = by_head[:, :, LANES : LANES + head_size].reshape(row_block, -1)
    share_value = by_head[:, :, LANES + head_size :].reshape(row_block, -1)

    y_own, y_other, y_far, y_far_other = after((y_own, y_other, y_far, y_far_other), do_sent[0])
    y_home = swap(y_far + swap(y_far_other, "c"), "x")
    y_sum = y_own.astype(F32) + swap(y_other, "c").astype(F32) + y_home.astype(F32)
    mixed = (y_mine + y_sum).astype(BF16)

    sums = sum_all(
        after(jnp.concatenate(
            [gain_attn / a_gain, gain_ffn, gains[0:1, :head_size] + gains[0:1, head_size:],
             gains[1:2, :head_size]], axis=1), late), n_y, n_z)[0]
    return (
        mixed,
        grad_tokens,
        sums[:width],
        share_query,
        share_key,
        share_value,
        sums[2 * width : 2 * width + head_size],
        sums[2 * width + head_size :],
        share_out,
        sums[width : 2 * width],
        share_gate,
        share_up,
        share_down,
    )


def solution(mesh):
    n_dp, n_seq = mesh.shape["dp"], mesh.shape["seq"]
    fine = Mesh(mesh.devices.reshape(n_dp // 2, 2, n_seq // 2, 2), ALL)
    split = P(ALL, None)
    in_specs = (split, P(("y", "x"), None)) + (P(),) * 11 + (split,)
    out_specs = (split, split, P(), split, split, split, P(), P(), split, P(), split, split, split)
    return jax.shard_map(body, mesh=fine, in_specs=in_specs, out_specs=out_specs, check_vma=False)
```

time: 543 us -> 346 us (0.64); the launches traced: 533 us -> 343 us
  starting transfers between devices: 149 us -> 65.1 us
  other arithmetic: 70.5 us -> 16.8 us
  waiting for transfers between devices: 154 us -> 120 us
  local copies, waits for them, and re-layouts: 61.7 us -> 48.2 us
  matrix products: 21.3 us -> 11.7 us
    ppermute x48 -> x27, starting transfers between devices: 122 us -> 49.4 us  [the longest x26 48.7 us: crossed(): return lax.ppermute(field, 'z', [(k, k ^ step) for k in range(count)])]
    ppermute x37 -> x35, waiting for transfers between devices: 56.9 us -> 28 us  [swap(): return lax.ppermute(field, axis_name, [(0, 1), (1, 0)])]
    concatenate x12 -> x0, other arithmetic: 16.4 us -> none  [the longest x10 12.7 us: both(): return jnp.concatenate([first, second], axis=0)]
    dynamic_update_slice x6 -> x0, other arithmetic: 16 us -> none  [body(): blocks = lax.dynamic_update_index_in_dim(blocks, full, spot, 0)]
    add x19 -> x9, other arithmetic: 16.6 us -> 1.88 us  [the longest x1 1.23 us: body(): y_home = swap(y_far + swap(y_far_other, 'c'), 'x')]
    unnamed x104 -> x144, local copies, waits for them, and re-layouts: 13.4 us -> 28.2 us
    ppermute x37 -> x35, starting transfers between devices: 26.5 us -> 15.7 us  [swap(): return lax.ppermute(field, axis_name, [(0, 1), (1, 0)])]
    dynamic_update_slice x20 -> x0, local copies, waits for them, and re-layouts: 6.88 us -> none  [the longest x16 5.12 us: exchange_line(): out = lax.dynamic_update_index_in_dim(out, arrived, place, 0)]
  transfers between devices with their start and end apart: 85 -> 62, of which waited for: 31 -> 23; matrix products, arithmetic and copies ran while one was open for 27% -> 14% of each run, Pallas kernels for 14% -> 18%
where the time goes in v2:
time: 346 us; the launch traced here: 343 us
  waiting for transfers between devices  120 us (35%)
  Pallas kernels  77.4 us (22%)
  starting transfers between devices  65.1 us (19%)
  local copies, waits for them, and re-layouts  48.2 us (14%)
  other arithmetic  16.8 us (5%)
  matrix products  11.7 us (3%)
  between operations  3.87 us (1%)
    ppermute x26, waiting for transfers between devices, crossed(): return lax.ppermute(field, 'z', [(k, k ^ step) for k in range(count)])  92 us
    pallas_call x11, Pallas kernels, run_kernel(): pl.pallas_call(kernel, grid_spec=pltpu.PrefetchScalarGridSpec(num_scalar_...  77.4 us
    ppermute x26, starting transfers between devices, crossed(): return lax.ppermute(field, 'z', [(k, k ^ step) for k in range(count)])  48.7 us
    unnamed x144, local copies, waits for them, and re-layouts  28.2 us
    ppermute x35, waiting for transfers between devices, swap(): return lax.ppermute(field, axis_name, [(0, 1), (1, 0)])  28 us
    ppermute x35, starting transfers between devices, swap(): return lax.ppermute(field, axis_name, [(0, 1), (1, 0)])  15.7 us
    dot_general x4, matrix products, dot_tn(): lax.dot_general(left, right, (((0,), (0,)), ((), ())), preferred_element_...  11.7 us
  transfers between devices with their start and end apart: 62, of which 23 were waited for; matrix products, arithmetic and copies ran while one was open for 14% of the time, Pallas kernels for 18%

profile of v2, /device:TPU:0, one launch (start us, length us, event | category | flops | bytes accessed | tf_op | source)
XLA Modules:
  0.0 343.0 jit_solution(15933881835866063026)
XLA Ops:
  9.8 5.4 %project.1 = (bf16[256,1024]{1,0:T(8,128)(2,1)S(1)}, bf16[256,1024]{1,0:T(8,128)(2,1)S(1)}, bf16[512,256]{1,0:T(8,128)(2,1)S(1)}, bf16[512,256]{1,0:T(8,128)(2,1...) custom-call(s32[8]{0:T(128)S(1)} %concatenate.35.ids, bf16[256,1024]{1,0:T(8,128)(2,1)S(1)} %copy-done.13, ...), custom_call_target="tpu_custom_call" | custom-call | flops 5750000128 | bytes 1048576 | tf_op jit(solution)/shard_map/project/pallas_call | solution.py:107
  21.3 9.6 %collective-permute-done.1.refs_1_ = bf16[512,256]{1,0:T(8,128)(2,1)S(1)} collective-permute-done((bf16[512,256]{1,0:T(8,128)(2,1)S(1)}, bf16[512,256]{1,0:T(8,128)(2,1)S(1)}, u32[]{:S(2)}, u32[]{:S(2)}) %collective-permute-start.1) | collective-permute-done | bytes 262176 | tf_op jit(solution)/shard_map/ppermute | solution.py:49
  30.8 9.2 %collective-permute-done.2.refs_2_ = bf16[512,256]{1,0:T(8,128)(2,1)S(1)} collective-permute-done((bf16[512,256]{1,0:T(8,128)(2,1)S(1)}, bf16[512,256]{1,0:T(8,128)(2,1)S(1)}, u32[]{:S(2)}, u32[]{:S(2)}) %collective-permute-start.2) | collective-permute-done | bytes 262176 | tf_op jit(solution)/shard_map/ppermute | solution.py:49
  40.0 9.4 %attend.1 = (bf16[512,128]{1,0:T(8,128)(2,1)S(1)}, bf16[512,128]{1,0:T(8,128)(2,1)S(1)}, bf16[512,128]{1,0:T(8,128)(2,1)S(1)}, bf16[512,128]{1,0:T(8,128)(2,1)S(...) custom-call(s32[8]{0:T(128)S(1)} %concatenate.35.ids, ...), custom_call_target="tpu_custom_call" | custom-call | flops 10350000128 | bytes 1048576 | tf_op jit(solution)/shard_map/attend/pallas_call | solution.py:107
  52.0 4.6 %collective-permute-start.4 = (bf16[512,128]{1,0:T(8,128)(2,1)S(1)}, bf16[512,128]{1,0:T(8,128)(2,1)S(1)}, u32[]{:S(2)}, u32[]{:S(2)}) collective-permute-start(bf16[512,128]{1,0:T(8,128)(2,1)S(1)} %get-tuple-element.99), channel_id=1, source_target_pairs={{0,2},{2,0},{4,6},{6,4},{1,3},{3,1},{5,7},{7,5},{8,10},{10,8},{12,... | collective-permute-start | bytes 393224 | tf_op jit(solution)/shard_map/ppermute | solution.py:49
  56.5 4.9 %constant_dynamic-slice_fusion.9 = (bf16[1024,1152]{1,0:T(8,128)(2,1)}, bf16[1024,1152]{1,0:T(8,128)(2,1)}) fusion(bf16[1024,4608]{1,0:T(8,128)(2,1)} %param.27, s32[]{:T(128)S(6)} %select_n.203, bf16[1024,4608]{1,0:T(8,128)(2,1)} %param.26), kind=kLoop, calls=%fused_computation.94 | loop fusion | bytes 9437188 | tf_op jit(solution)/shard_map/dynamic_slice | solution.py:634
  65.0 3.4 constant_dynamic-slice_fusion.8.wd_ref
  86.0 4.0 %middle.1 = (f32[256,1024]{1,0:T(8,128)S(1)}, bf16[256,1024]{1,0:T(8,128)(2,1)S(1)}, bf16[256,1024]{1,0:T(8,128)(2,1)S(1)}, bf16[512,1024]{1,0:T(8,128)(2,1)S(1)}) custom-call(s32[8]{0:T(128)S(1)} %concatenate.35.ids, bf16[512,128]{1,0:T(8,128)(2,1)S(1)} %get-tuple-element.98.refs_0_, bf16[512,128]{1,0:T(8,128)(2,1)S(1)} %collective-permute-done.4.refs_1_, ...), custom_call_target="tpu_custom_call" | custom-call | flops 4600000000 | bytes 1048576 | tf_op jit(solution)/shard_map/middle/pallas_call | solution.py:107
  90.7 12.5 %feed.2 = (bf16[1024,1152]{1,0:T(8,128)(2,1)}, bf16[1024,1152]{1,0:T(8,128)(2,1)}, bf16[1024,1152]{1,0:T(8,128)(2,1)}, bf16[1024,1024]{1,0:T(8,128)(2,1)S(1)}, b...) custom-call(s32[8]{0:T(128)S(1)} %concatenate.35.ids, ...), custom_call_target="tpu_custom_call" | custom-call | flops 13799999488 | bytes 1048576 | tf_op jit(solution)/shard_map/feed/pallas_call | solution.py:107
  107.1 3.7 %fusion = (f32[2048,128]{1,0:T(8,128)S(1)}, f32[2048,128]{1,0:T(8,128)S(1)}) fusion(f32[128]{0:T(128)S(1)} %copy-done.67, f32[128]{0:T(128)S(1)} %copy-done.66, f32[2048]{0:T(1024)S(1)} %subtract_convert_fusion), kind=kLoop, calls=%fused_computation.12 | loop fusion | flops 524288 | bytes 2106368 | tf_op jit(solution)/shard_map/mul | solution.py:643
  116.8 13.7 %feed.3 = (bf16[1024,1152]{1,0:T(8,128)(2,1)}, bf16[1024,1152]{1,0:T(8,128)(2,1)}, bf16[1024,1152]{1,0:T(8,128)(2,1)}, bf16[1024,1024]{1,0:T(8,128)(2,1)S(1)}, b...) custom-call(s32[8]{0:T(128)S(1)} %concatenate.35.ids, ...), custom_call_target="tpu_custom_call", output_to_operand_aliasing={{0}: (8, {}), {1}: (9, {}), {2}: (10, {}), {3}: (11, {}), {... | custom-call | flops 13799999488 | bytes 1048576 | tf_op jit(solution)/shard_map/feed/pallas_call | solution.py:107
  131.0 4.6 %convolution_convert_fusion = bf16[1152,1024]{1,0:T(8,128)(2,1)S(1)} fusion(bf16[1024,1152]{1,0:T(8,128)(2,1)} %get-tuple-element.169, bf16[1024,1024]{1,0:T(8,128)(2,1)S(1)} %get-tuple-element.170), kind=kOutput, calls=%fused_computation | convolution fusion | flops 2417098752 | bytes 6815744 | tf_op jit(solution)/shard_map/dot_general | solution.py:33
  138.1 3.2 convolution_convert_fusion.1
  143.1 8.0 %collective-permute-done.18.far_ref = bf16[256,1024]{1,0:T(8,128)(2,1)S(1)} collective-permute-done((bf16[256,1024]{1,0:T(8,128)(2,1)S(1)}, bf16[256,1024]{1,0:T(8,128)(2,1)S(1)}, u32[]{:S(2)}, u32[]{:S(2)}) %collective-permute-start.18) | collective-permute-done | bytes 524320 | tf_op jit(solution)/shard_map/ppermute | solution.py:45
  152.8 3.2 convolution_convert_fusion.2
  161.1 3.5 %collective-permute-done.58 = bf16[4,144,1024]{2,1,0:T(8,128)(2,1)S(1)} collective-permute-done((bf16[4,144,1024]{2,1,0:T(8,128)(2,1)S(1)}, bf16[4,144,1024]{2,1,0:T(8,128)(2,1)S(1)}, u32[]{:S(2)}, u32[]{:S(2)}) %collective-permute-start.58) | collective-permute-done | bytes 1179680 | tf_op jit(solution)/shard_map/ppermute | solution.py:45
  166.9 9.2 %collective-permute-start.29 = (bf16[512,128]{1,0:T(8,128)(2,1)S(1)}, bf16[512,128]{1,0:T(8,128)(2,1)S(1)}, u32[]{:S(2)}, u32[]{:S(2)}) collective-permute-start(bf16[512,128]{1,0:T(8,128)(2,1)S(1)} %get-tuple-element.137), channel_id=1, source_target_pairs={{0,2},{2,0},{4,6},{6,4},{1,3},{3,1},{5,7},{7,5},{8,10},{10,8},{12,... | collective-permute-start | bytes 393224 | tf_op jit(solution)/shard_map/ppermute | solution.py:49
  179.4 5.3 %collective-permute-done.30.refs_2_ = bf16[512,128]{1,0:T(8,128)(2,1)S(1)} collective-permute-done((bf16[512,128]{1,0:T(8,128)(2,1)S(1)}, bf16[512,128]{1,0:T(8,128)(2,1)S(1)}, u32[]{:S(2)}, u32[]{:S(2)}) %collective-permute-start.30) | collective-permute-done | bytes 131104 | tf_op jit(solution)/shard_map/ppermute | solution.py:49
  184.7 13.6 %attend_back.1 = (f32[2048,128]{1,0:T(8,128)S(1)}, f32[2048,128]{1,0:T(8,128)S(1)}) custom-call(s32[8]{0:T(128)S(1)} %concatenate.35.ids, bf16[2,2048,128]{2,1,0:T(8,128)(2,1)S(1)} %copy-done.52, bf16[2048,128]{1,0:T(8,128)(2,1)S(1)} %copy-done.54, bf16[2048,128]{1,0:T(8,128)(2,1)S(1)} %copy-done.56, f32[2048,128]{1,0:T(8,128)S(1)} %copy-done.50, ...), custom_call_target="tpu_custom_call" | custom-call | flops 14949999616 | bytes 1048576 | tf_op jit(solution)/shard_map/attend_back/pallas_call | solution.py:107
  200.4 9.2 %unturn.1 = (bf16[512,256]{1,0:T(8,128)(2,1)S(1)}, bf16[512,256]{1,0:T(8,128)(2,1)S(1)}, bf16[512,256]{1,0:T(8,128)(2,1)S(1)}, bf16[512,256]{1,0:T(8,128)(2,1)},...) custom-call(s32[8]{0:T(128)S(1)} %concatenate.35.ids, ...), custom_call_target="tpu_custom_call" | custom-call | flops 8049999872 | bytes 1048576 | tf_op jit(solution)/shard_map/unturn/pallas_call | solution.py:107
  216.4 4.3 %collective-permute-done.34.refs_3_ = bf16[512,256]{1,0:T(8,128)(2,1)} collective-permute-done((bf16[512,256]{1,0:T(8,128)(2,1)}, bf16[512,256]{1,0:T(8,128)(2,1)}, u32[]{:S(2)}, u32[]{:S(2)}) %collective-permute-start.34) | collective-permute-done | bytes 262176 | tf_op jit(solution)/shard_map/ppermute | solution.py:49
  220.9 6.9 %collective-permute-start.32 = (bf16[512,256]{1,0:T(8,128)(2,1)S(1)}, bf16[512,256]{1,0:T(8,128)(2,1)S(1)}, u32[]{:S(2)}, u32[]{:S(2)}) collective-permute-start(bf16[512,256]{1,0:T(8,128)(2,1)S(1)} %copy-done.20), channel_id=1, source_target_pairs={{0,2},{2,0},{4,6},{6,4},{1,3},{3,1},{5,7},{7,5},{8,10},{10,8},{12,... | collective-permute-start | bytes 786440 | tf_op jit(solution)/shard_map/ppermute | solution.py:49
  232.4 7.2 %collective-permute-done.32.refs_1_ = bf16[512,256]{1,0:T(8,128)(2,1)S(1)} collective-permute-done((bf16[512,256]{1,0:T(8,128)(2,1)S(1)}, bf16[512,256]{1,0:T(8,128)(2,1)S(1)}, u32[]{:S(2)}, u32[]{:S(2)}) %collective-permute-start.32) | collective-permute-done | bytes 262176 | tf_op jit(solution)/shard_map/ppermute | solution.py:49
  243.8 4.0 %to_tokens.1 = (bf16[256,1024]{1,0:T(8,128)(2,1)S(1)}, bf16[256,1024]{1,0:T(8,128)(2,1)S(1)}) custom-call(s32[8]{0:T(128)S(1)} %concatenate.35.ids, bf16[512,256]{1,0:T(8,128)(2,1)S(1)} %copy-done.48, bf16[512,256]{1,0:T(8,128)(2,1)S(1)} %collective-permute-done.32.refs_1_, bf16[512,256]{1,0:T(8,128)(2,1)S(1)} %collective-permute-done.33.refs_2_, ...), custom_call_target="tpu_custom_call" | custom-call | flops 4600000000 | bytes 1048576 | tf_op jit(solution)/shard_map/to_tokens/pallas_call | solution.py:107
  252.7 9.6 %collective-permute-done.40 = f32[1,2176]{1,0:T(1,128)S(1)} collective-permute-done((f32[1,2176]{1,0:T(1,128)S(1)}, f32[1,2176]{1,0:T(1,128)S(1)}, u32[]{:S(2)}, u32[]{:S(2)}) %collective-permute-start.40) | collective-permute-done | bytes 8736 | tf_op jit(solution)/shard_map/ppermute | solution.py:49
  268.1 10.5 %collective-permute-done.49 = bf16[2,2,2,32,1152]{4,3,1,2,0:T(8,128)(2,1)S(1)} collective-permute-done((bf16[2,2,2,32,1152]{4,3,1,2,0:T(8,128)(2,1)S(1)}, bf16[2,2,2,32,1152]{4,3,1,2,0:T(8,128)(2,1)S(1)}, u32[]{:S(2)}, u32[]{:S(2)}) %collective-permute-start.49) | collective-permute-done | bytes 589856 | tf_op jit(solution)/shard_map/ppermute | solution.py:49
  280.1 6.2 %collective-permute-done.43 = bf16[4,2,32,768]{3,2,1,0:T(8,128)(2,1)S(1)} collective-permute-done((bf16[4,2,32,768]{3,2,1,0:T(8,128)(2,1)S(1)}, bf16[4,2,32,768]{3,2,1,0:T(8,128)(2,1)S(1)}, u32[]{:S(2)}, u32[]{:S(2)}) %collective-permute-start.43) | collective-permute-done | bytes 393248 | tf_op jit(solution)/shard_map/ppermute | solution.py:45
  286.4 3.4 collective-permute-start.60
  292.1 3.0 collective-permute-done.54
  295.9 11.0 %collective-permute-done.60 = bf16[1,144,1024]{2,1,0:T(8,128)(2,1)S(1)} collective-permute-done((bf16[1,144,1024]{2,1,0:T(8,128)(2,1)S(1)}, bf16[1,144,1024]{2,1,0:T(8,128)(2,1)S(1)}, u32[]{:S(2)}, u32[]{:S(2)}) %collective-permute-start.60) | collective-permute-done | bytes 294944 | tf_op jit(solution)/shard_map/ppermute | solution.py:49
  307.0 11.2 %collective-permute-done.50 = bf16[1,2,2,32,1152]{4,3,1,2,0:T(8,128)(2,1)S(1)} collective-permute-done((bf16[1,2,2,32,1152]{4,3,1,2,0:T(8,128)(2,1)S(1)}, bf16[1,2,2,32,1152]{4,3,1,2,0:T(8,128)(2,1)S(1)}, u32[]{:S(2)}, u32[]{:S(2)}) %collective-permute-start.50) | collective-permute-done | bytes 294944 | tf_op jit(solution)/shard_map/ppermute | solution.py:49
  331.7 4.9 %collective-permute-done.52 = bf16[32,2304]{1,0:T(8,128)(2,1)S(1)} collective-permute-done((bf16[32,2304]{1,0:T(8,128)(2,1)S(1)}, bf16[32,2304]{1,0:T(8,128)(2,1)S(1)}, u32[]{:S(2)}, u32[]{:S(2)}) %collective-permute-start.52) | collective-permute-done | bytes 147488 | tf_op jit(solution)/shard_map/ppermute | solution.py:45
  (327 shorter events, 116.8 us)
Async XLA Ops:
  16.1 14.7 %collective-permute-start.1 = (bf16[512,256]{1,0:T(8,128)(2,1)S(1)}, bf16[512,256]{1,0:T(8,128)(2,1)S(1)}, u32[]{:S(2)}, u32[]{:S(2)}) collective-permute-start(bf16[512,256]{1,0:T(8,128)(2,1)S(1)} %get-tuple-element.95), channel_id=1, source_target_pairs={{0,2},{2,0},{4,6},{6,4},{1,3},{3,1},{5,7},{7,5},{8,10},{10,8},{12,... | collective-permute-start | bytes 786440 | tf_op jit(solution)/shard_map/ppermute | solution.py:49
  18.7 21.3 %collective-permute-start.2 = (bf16[512,256]{1,0:T(8,128)(2,1)S(1)}, bf16[512,256]{1,0:T(8,128)(2,1)S(1)}, u32[]{:S(2)}, u32[]{:S(2)}) collective-permute-start(bf16[512,256]{1,0:T(8,128)(2,1)S(1)} %get-tuple-element.96), channel_id=1, source_target_pairs={{0,4},{2,6},{4,0},{6,2},{1,5},{3,7},{5,1},{7,3},{8,12},{10,14},{12... | collective-permute-start | bytes 786440 | tf_op jit(solution)/shard_map/ppermute | solution.py:49
  21.3 18.7 %collective-permute-start.3 = (bf16[512,256]{1,0:T(8,128)(2,1)S(1)}, bf16[512,256]{1,0:T(8,128)(2,1)S(1)}, u32[]{:S(2)}, u32[]{:S(2)}) collective-permute-start(bf16[512,256]{1,0:T(8,128)(2,1)S(1)} %get-tuple-element.97), channel_id=1, source_target_pairs={{0,6},{2,4},{4,2},{6,0},{1,7},{3,5},{5,3},{7,1},{8,14},{10,12},{12... | collective-permute-start | bytes 786440 | tf_op jit(solution)/shard_map/ppermute | solution.py:49
  68.4 21.7 %collective-permute-start.11 = (bf16[256,1024]{1,0:T(8,128)(2,1)S(1)}, bf16[256,1024]{1,0:T(8,128)(2,1)}, u32[]{:S(2)}, u32[]{:S(2)}) collective-permute-start(bf16[256,1024]{1,0:T(8,128)(2,1)S(1)} %copy-done.12), channel_id=1, source_target_pairs={{0,1},{1,0},{2,3},{3,2},{4,5},{5,4},{6,7},{7,6},{8,9},{9,8},{10,11... | collective-permute-start | bytes 1572872 | tf_op jit(solution)/shard_map/ppermute | solution.py:45
  69.5 21.2 %collective-permute-start.14 = (bf16[256,1024]{1,0:T(8,128)(2,1)S(1)}, bf16[256,1024]{1,0:T(8,128)(2,1)}, u32[]{:S(2)}, u32[]{:S(2)}) collective-permute-start(bf16[256,1024]{1,0:T(8,128)(2,1)S(1)} %copy-done.12), channel_id=1, source_target_pairs={{0,8},{8,0},{1,9},{9,1},{2,10},{10,2},{3,11},{11,3},{4,12},{12,4},... | collective-permute-start | bytes 1572872 | tf_op jit(solution)/shard_map/ppermute | solution.py:45
  74.2 36.6 %collective-permute-start.23 = (bf16[256,1024]{1,0:T(8,128)(2,1)S(1)}, bf16[256,1024]{1,0:T(8,128)(2,1)S(1)}, u32[]{:S(2)}, u32[]{:S(2)}) collective-permute-start(bf16[256,1024]{1,0:T(8,128)(2,1)S(1)} %get-tuple-element.131.refs_0_), channel_id=1, source_target_pairs={{0,2},{2,0},{4,6},{6,4},{1,3},{3,1},{5,7},{7,5},{8,10},{10,8},{12,... | collective-permute-start | bytes 1572872 | tf_op jit(solution)/shard_map/ppermute | solution.py:49
  74.9 38.2 %collective-permute-start.25 = (bf16[256,1024]{1,0:T(8,128)(2,1)S(1)}, bf16[256,1024]{1,0:T(8,128)(2,1)S(1)}, u32[]{:S(2)}, u32[]{:S(2)}) collective-permute-start(bf16[256,1024]{1,0:T(8,128)(2,1)S(1)} %get-tuple-element.131.refs_0_), channel_id=1, source_target_pairs={{0,4},{2,6},{4,0},{6,2},{1,5},{3,7},{5,1},{7,3},{8,12},{10,14},{12... | collective-permute-start | bytes 1572872 | tf_op jit(solution)/shard_map/ppermute | solution.py:49
  78.4 34.7 %collective-permute-start.27 = (bf16[256,1024]{1,0:T(8,128)(2,1)S(1)}, bf16[256,1024]{1,0:T(8,128)(2,1)S(1)}, u32[]{:S(2)}, u32[]{:S(2)}) collective-permute-start(bf16[256,1024]{1,0:T(8,128)(2,1)S(1)} %get-tuple-element.131.refs_0_), channel_id=1, source_target_pairs={{0,6},{2,4},{4,2},{6,0},{1,7},{3,5},{5,3},{7,1},{8,14},{10,12},{12... | collective-permute-start | bytes 1572872 | tf_op jit(solution)/shard_map/ppermute | solution.py:49
  90.1 15.8 %collective-permute-start.12 = (bf16[256,1024]{1,0:T(8,128)(2,1)S(1)}, bf16[256,1024]{1,0:T(8,128)(2,1)S(1)}, u32[]{:S(2)}, u32[]{:S(2)}) collective-permute-start(bf16[256,1024]{1,0:T(8,128)(2,1)S(1)} %get-tuple-element.103.ho_ref), channel_id=1, source_target_pairs={{0,8},{8,0},{1,9},{9,1},{2,10},{10,2},{3,11},{11,3},{4,12},{12,4},... | collective-permute-start | bytes 1572872 | tf_op jit(solution)/shard_map/ppermute | solution.py:45
  90.7 22.9 %collective-permute-start.15 = (bf16[256,1024]{1,0:T(8,128)(2,1)}, bf16[256,1024]{1,0:T(8,128)(2,1)S(1)}, u32[]{:S(2)}, u32[]{:S(2)}) collective-permute-start(bf16[256,1024]{1,0:T(8,128)(2,1)} %collective-permute-done.14.co_ref), channel_id=1, source_target_pairs={{0,1},{1,0},{2,3},{3,2},{4,5},{5,4},{6,7},{7,6},{8,9},{9,8},{10,11... | collective-permute-start | bytes 1572872 | tf_op jit(solution)/shard_map/ppermute | solution.py:45
  110.8 32.3 %collective-permute-start.16 = (bf16[256,1024]{1,0:T(8,128)(2,1)S(1)}, bf16[256,1024]{1,0:T(8,128)(2,1)S(1)}, u32[]{:S(2)}, u32[]{:S(2)}) collective-permute-start(bf16[256,1024]{1,0:T(8,128)(2,1)S(1)} %get-tuple-element.120), channel_id=1, source_target_pairs={{0,1},{1,0},{2,3},{3,2},{4,5},{5,4},{6,7},{7,6},{8,9},{9,8},{10,11... | collective-permute-start | bytes 1572872 | tf_op jit(solution)/shard_map/ppermute | solution.py:45
  113.1 17.9 %collective-permute-start.24 = (bf16[256,1024]{1,0:T(8,128)(2,1)S(1)}, bf16[256,1024]{1,0:T(8,128)(2,1)S(1)}, u32[]{:S(2)}, u32[]{:S(2)}) collective-permute-start(bf16[256,1024]{1,0:T(8,128)(2,1)S(1)} %collective-permute-done.23.refs_2_), channel_id=1, source_target_pairs={{0,1},{1,0},{2,3},{3,2},{4,5},{5,4},{6,7},{7,6},{8,9},{9,8},{10,11... | collective-permute-start | bytes 1572872 | tf_op jit(solution)/shard_map/ppermute | solution.py:45
  113.1 17.9 %collective-permute-start.26 = (bf16[256,1024]{1,0:T(8,128)(2,1)S(1)}, bf16[256,1024]{1,0:T(8,128)(2,1)S(1)}, u32[]{:S(2)}, u32[]{:S(2)}) collective-permute-start(bf16[256,1024]{1,0:T(8,128)(2,1)S(1)} %collective-permute-done.25.refs_4_), channel_id=1, source_target_pairs={{0,1},{1,0},{2,3},{3,2},{4,5},{5,4},{6,7},{7,6},{8,9},{9,8},{10,11... | collective-permute-start | bytes 1572872 | tf_op jit(solution)/shard_map/ppermute | solution.py:45
  113.6 17.4 %collective-permute-start.28 = (bf16[256,1024]{1,0:T(8,128)(2,1)S(1)}, bf16[256,1024]{1,0:T(8,128)(2,1)S(1)}, u32[]{:S(2)}, u32[]{:S(2)}) collective-permute-start(bf16[256,1024]{1,0:T(8,128)(2,1)S(1)} %collective-permute-done.27.refs_6_), channel_id=1, source_target_pairs={{0,1},{1,0},{2,3},{3,2},{4,5},{5,4},{6,7},{7,6},{8,9},{9,8},{10,11... | collective-permute-start | bytes 1572872 | tf_op jit(solution)/shard_map/ppermute | solution.py:45
  135.7 28.9 %collective-permute-start.58 = (bf16[4,144,1024]{2,1,0:T(8,128)(2,1)S(1)}, bf16[4,144,1024]{2,1,0:T(8,128)(2,1)S(1)}, u32[]{:S(2)}, u32[]{:S(2)}) collective-permute-start(bf16[4,144,1024]{2,1,0:T(8,128)(2,1)S(1)} %dynamic-slice_bitcast_fusion), channel_id=1, source_target_pairs={{0,16},{16,0},{1,17},{17,1},{2,18},{18,2},{3,19},{19,3},{4,20},{20... | collective-permute-start | bytes 3538952 | tf_op jit(solution)/shard_map/ppermute | solution.py:45
  142.4 85.3 %collective-permute-start.53 = (bf16[2,4,2,32,1152]{4,3,2,1,0:T(8,128)(2,1)}, bf16[2,4,2,32,1152]{4,3,2,1,0:T(8,128)(2,1)}, u32[]{:S(2)}, u32[]{:S(2)}) collective-permute-start(bf16[2,4,2,32,1152]{4,3,2,1,0:T(8,128)(2,1)} %dynamic-slice_bitcast_fusion.1), channel_id=1, source_target_pairs={{0,16},{16,0},{1,17},{17,1},{2,18},{18,2},{3,19},{19,3},{4,20},{20... | collective-permute-start | bytes 3538952 | tf_op jit(solution)/shard_map/ppermute | solution.py:45
  157.2 57.1 %collective-permute-start.48 = (bf16[2,4,2,32,1152]{4,3,2,1,0:T(8,128)(2,1)}, bf16[2,4,2,32,1152]{4,3,2,1,0:T(8,128)(2,1)}, u32[]{:S(2)}, u32[]{:S(2)}) collective-permute-start(bf16[2,4,2,32,1152]{4,3,2,1,0:T(8,128)(2,1)} %dynamic-slice_bitcast_fusion.2), channel_id=1, source_target_pairs={{0,16},{16,0},{1,17},{17,1},{2,18},{18,2},{3,19},{19,3},{4,20},{20... | collective-permute-start | bytes 3538952 | tf_op jit(solution)/shard_map/ppermute | solution.py:45
  178.7 86.0 %collective-permute-start.41 = (bf16[2,4,2,32,512]{4,3,2,1,0:T(8,128)(2,1)}, bf16[2,4,2,32,512]{4,3,2,1,0:T(8,128)(2,1)}, u32[]{:S(2)}, u32[]{:S(2)}) collective-permute-start(bf16[2,4,2,32,512]{4,3,2,1,0:T(8,128)(2,1)} %dynamic-slice_bitcast_fusion.4), channel_id=1, source_target_pairs={{0,8},{8,0},{1,9},{9,1},{2,10},{10,2},{3,11},{11,3},{4,12},{12,4},... | collective-permute-start | bytes 1572872 | tf_op jit(solution)/shard_map/ppermute | solution.py:45
  179.4 86.2 %collective-permute-start.21 = (bf16[256,1024]{1,0:T(8,128)(2,1)}, bf16[256,1024]{1,0:T(8,128)(2,1)}, u32[]{:S(2)}, u32[]{:S(2)}) collective-permute-start(bf16[256,1024]{1,0:T(8,128)(2,1)} %get-tuple-element.128), channel_id=1, source_target_pairs={{0,1},{1,0},{2,3},{3,2},{4,5},{5,4},{6,7},{7,6},{8,9},{9,8},{10,11... | collective-permute-start | bytes 1572872 | tf_op jit(solution)/shard_map/ppermute | solution.py:45
  220.9 18.7 %collective-permute-start.32 = (bf16[512,256]{1,0:T(8,128)(2,1)S(1)}, bf16[512,256]{1,0:T(8,128)(2,1)S(1)}, u32[]{:S(2)}, u32[]{:S(2)}) collective-permute-start(bf16[512,256]{1,0:T(8,128)(2,1)S(1)} %copy-done.20), channel_id=1, source_target_pairs={{0,2},{2,0},{4,6},{6,4},{1,3},{3,1},{5,7},{7,5},{8,10},{10,8},{12,... | collective-permute-start | bytes 786440 | tf_op jit(solution)/shard_map/ppermute | solution.py:49
  227.8 14.5 %collective-permute-start.33 = (bf16[512,256]{1,0:T(8,128)(2,1)S(1)}, bf16[512,256]{1,0:T(8,128)(2,1)S(1)}, u32[]{:S(2)}, u32[]{:S(2)}) collective-permute-start(bf16[512,256]{1,0:T(8,128)(2,1)S(1)} %get-tuple-element.144), channel_id=1, source_target_pairs={{0,4},{2,6},{4,0},{6,2},{1,5},{3,7},{5,1},{7,3},{8,12},{10,14},{12... | collective-permute-start | bytes 786440 | tf_op jit(solution)/shard_map/ppermute | solution.py:49
  232.4 92.4 %collective-permute-start.20 = (bf16[256,1024]{1,0:T(8,128)(2,1)S(1)}, bf16[256,1024]{1,0:T(8,128)(2,1)S(1)}, u32[]{:S(2)}, u32[]{:S(2)}) collective-permute-start(bf16[256,1024]{1,0:T(8,128)(2,1)S(1)} %copy-done.18), channel_id=1, source_target_pairs={{0,1},{1,0},{2,3},{3,2},{4,5},{5,4},{6,7},{7,6},{8,9},{9,8},{10,11... | collective-permute-start | bytes 1572872 | tf_op jit(solution)/shard_map/ppermute | solution.py:45
  248.9 30.5 %collective-permute-start.59 = (bf16[2,144,1024]{2,1,0:T(8,128)(2,1)S(1)}, bf16[2,144,1024]{2,1,0:T(8,128)(2,1)S(1)}, u32[]{:S(2)}, u32[]{:S(2)}) collective-permute-start(bf16[2,144,1024]{2,1,0:T(8,128)(2,1)S(1)} %copy-done.64), channel_id=1, source_target_pairs={{0,2},{2,0},{4,6},{6,4},{1,3},{3,1},{5,7},{7,5},{8,10},{10,8},{12,... | collective-permute-start | bytes 1769480 | tf_op jit(solution)/shard_map/ppermute | solution.py:49
  262.3 16.3 %collective-permute-start.49 = (bf16[2,2,2,32,1152]{4,3,1,2,0:T(8,128)(2,1)S(1)}, bf16[2,2,2,32,1152]{4,3,1,2,0:T(8,128)(2,1)S(1)}, u32[]{:S(2)}, u32[]{:S(2)}) collective-permute-start(bf16[2,2,2,32,1152]{4,3,1,2,0:T(8,128)(2,1)S(1)} %bitcast.150), channel_id=1, source_target_pairs={{0,2},{2,0},{4,6},{6,4},{1,3},{3,1},{5,7},{7,5},{8,10},{10,8},{12,... | collective-permute-start | bytes 1769480 | tf_op jit(solution)/shard_map/ppermute | solution.py:49
  264.7 30.4 %collective-permute-start.54 = (bf16[2,2,2,32,1152]{4,3,1,2,0:T(8,128)(2,1)S(1)}, bf16[2,2,2,32,1152]{4,3,1,2,0:T(8,128)(2,1)S(1)}, u32[]{:S(2)}, u32[]{:S(2)}) collective-permute-start(bf16[2,2,2,32,1152]{4,3,1,2,0:T(8,128)(2,1)S(1)} %bitcast.151), channel_id=1, source_target_pairs={{0,2},{2,0},{4,6},{6,4},{1,3},{3,1},{5,7},{7,5},{8,10},{10,8},{12,... | collective-permute-start | bytes 1769480 | tf_op jit(solution)/shard_map/ppermute | solution.py:49
  265.6 24.4 %collective-permute-start.35 = (bf16[256,1024]{1,0:T(8,128)(2,1)S(1)}, bf16[256,1024]{1,0:T(8,128)(2,1)S(1)}, u32[]{:S(2)}, u32[]{:S(2)}) collective-permute-start(bf16[256,1024]{1,0:T(8,128)(2,1)S(1)} %get-tuple-element.147), channel_id=1, source_target_pairs={{0,1},{1,0},{2,3},{3,2},{4,5},{5,4},{6,7},{7,6},{8,9},{9,8},{10,11... | collective-permute-start | bytes 1572872 | tf_op jit(solution)/shard_map/ppermute | solution.py:45
  279.4 46.0 %collective-permute-start.22 = (bf16[256,1024]{1,0:T(8,128)(2,1)S(1)}, bf16[256,1024]{1,0:T(8,128)(2,1)S(1)}, u32[]{:S(2)}, u32[]{:S(2)}) collective-permute-start(bf16[256,1024]{1,0:T(8,128)(2,1)S(1)} %add.198), channel_id=1, source_target_pairs={{0,8},{8,0},{1,9},{9,1},{2,10},{10,2},{3,11},{11,3},{4,12},{12,4},... | collective-permute-start | bytes 1572872 | tf_op jit(solution)/shard_map/ppermute | solution.py:45
  286.4 20.6 %collective-permute-start.60 = (bf16[1,144,1024]{2,1,0:T(8,128)(2,1)S(1)}, bf16[1,144,1024]{2,1,0:T(8,128)(2,1)S(1)}, u32[]{:S(2)}, u32[]{:S(2)}) collective-permute-start(bf16[1,144,1024]{2,1,0:T(8,128)(2,1)S(1)} %constant_dynamic-slice_fusion), channel_id=1, source_target_pairs={{0,4},{2,6},{4,0},{6,2},{1,5},{3,7},{5,1},{7,3},{8,12},{10,14},{12... | collective-permute-start | bytes 884744 | tf_op jit(solution)/shard_map/ppermute | solution.py:49
  289.9 28.3 %collective-permute-start.50 = (bf16[1,2,2,32,1152]{4,3,1,2,0:T(8,128)(2,1)S(1)}, bf16[1,2,2,32,1152]{4,3,1,2,0:T(8,128)(2,1)S(1)}, u32[]{:S(2)}, u32[]{:S(2)}) collective-permute-start(bf16[1,2,2,32,1152]{4,3,1,2,0:T(8,128)(2,1)S(1)} %constant_dynamic-slice_fusion.4), channel_id=1, source_target_pairs={{0,4},{2,6},{4,0},{6,2},{1,5},{3,7},{5,1},{7,3},{8,12},{10,14},{12... | collective-permute-start | bytes 884744 | tf_op jit(solution)/shard_map/ppermute | solution.py:49
  295.1 26.4 %collective-permute-start.44 = (bf16[2,32,768]{2,1,0:T(8,128)(2,1)S(1)}, bf16[2,32,768]{2,1,0:T(8,128)(2,1)S(1)}, u32[]{:S(2)}, u32[]{:S(2)}) collective-permute-start(bf16[2,32,768]{2,1,0:T(8,128)(2,1)S(1)} %get-tuple-element.190), channel_id=1, source_target_pairs={{0,2},{2,0},{4,6},{6,4},{1,3},{3,1},{5,7},{7,5},{8,10},{10,8},{12,... | collective-permute-start | bytes 294920 | tf_op jit(solution)/shard_map/ppermute | solution.py:49
  307.0 14.5 %collective-permute-start.45 = (bf16[2,32,768]{2,1,0:T(8,128)(2,1)S(1)}, bf16[2,32,768]{2,1,0:T(8,128)(2,1)S(1)}, u32[]{:S(2)}, u32[]{:S(2)}) collective-permute-start(bf16[2,32,768]{2,1,0:T(8,128)(2,1)S(1)} %get-tuple-element.189), channel_id=1, source_target_pairs={{0,4},{2,6},{4,0},{6,2},{1,5},{3,7},{5,1},{7,3},{8,12},{10,14},{12... | collective-permute-start | bytes 294920 | tf_op jit(solution)/shard_map/ppermute | solution.py:49
  321.5 17.0 %collective-permute-start.61 = (bf16[144,1024]{1,0:T(8,128)(2,1)S(1)}, bf16[144,1024]{1,0:T(8,128)(2,1)S(1)}, u32[]{:S(2)}, u32[]{:S(2)}) collective-permute-start(bf16[144,1024]{1,0:T(8,128)(2,1)S(1)} %add_bitcast_fusion), channel_id=1, source_target_pairs={{0,0},{1,8},{2,2},{3,10},{4,4},{5,12},{6,6},{7,14},{8,16},{9,24},{... | collective-permute-start | bytes 884744 | tf_op jit(solution)/shard_map/ppermute | solution.py:709
  (100 other events, 832.2 us)

commit v3 on v2

--- a/solution.py
+++ b/solution.py
@@ -49,17 +49,25 @@
     return lax.ppermute(field, "z", [(k, k ^ step) for k in range(count)])
 
 
-def pair_reduce(parts, axis_name, index, *needed):
-    got = after(swap(pick(parts, 1 - index), axis_name), *needed)
-    return pick(parts, index) + got
-
-
-def reduce_y(parts, index, *needed):
-    if parts.shape[0] == 1:
-        return parts[0]
-    if parts.shape[0] == 2:
-        return pair_reduce(parts, "y", index, *needed)
-    return lax.psum_scatter(parts, "y", scatter_dimension=0, tiled=False)
+def along(to_right, to_left, count):
+    pairs = range(count - 1)
+    return (lax.ppermute(to_right, "z", [(k, k + 1) for k in pairs]),
+            lax.ppermute(to_left, "z", [(k + 1, k) for k in pairs]))
+
+
+class Pair:
+    def __init__(self, parts, index, *needed, axis_name="y"):
+        self.parts, self.index, self.sent, self.got = parts, index, parts, None
+        if parts.shape[0] == 2:
+            self.sent = after(pick(parts, 1 - index), *needed)
+            self.got = swap(self.sent, axis_name)
+
+    def finish(self, *needed):
+        if self.parts.shape[0] == 1:
+            return self.parts[0]
+        if self.got is None:
+            return lax.psum_scatter(self.parts, "y", scatter_dimension=0, tiled=False)
+        return pick(self.parts, self.index) + after(self.got, *needed)
 
 
 class Halving:
@@ -74,6 +82,7 @@
         kept = pick(parts, bit, 1)
         if needed:
             sent = after(sent, *needed)
+        self.sent = sent
         self.parts = kept + crossed(sent, self.step, self.count)
         self.step = self.step * 2
 
@@ -88,18 +97,11 @@
         [jnp.where(index == 0, own, other), jnp.where(index == 0, other, own)], axis=axis)
 
 
-def sum_all(vector, rows_y, rows_z):
-    vector = vector + swap(vector, "c")
-    vector = vector + swap(vector, "x")
-    if rows_y == 2:
-        vector = vector + swap(vector, "y")
-    else:
-        vector = lax.psum(vector, "y")
-    step = 1
-    while step < rows_z:
-        vector = vector + crossed(vector, step, rows_z)
-        step = step * 2
-    return vector
+def split_up(field):
+    high = field.astype(BF16)
+    rest = field - high.astype(F32)
+    middle = rest.astype(BF16)
+    return [high, middle, (rest - middle.astype(F32)).astype(BF16)]
 
 
 def run_kernel(kernel, name, ids, operands, in_specs, out_shapes, out_specs, grid=(1,), scratch=(),
@@ -113,7 +115,7 @@
         input_output_aliases=aliases or {},
         compiler_params=pltpu.CompilerParams(vmem_limit_bytes=vmem * MIB),
         cost_estimate=pl.CostEstimate(
-            flops=int(micros * 1.15e9), bytes_accessed=MIB, transcendentals=0),
+            flops=int(micros * 1e5), bytes_accessed=1024, transcendentals=0),
         name=name,
     )(ids, *operands)
 
@@ -213,7 +215,7 @@
          of_core(width, w_key.shape[1] // 2), of_core(width, w_value.shape[1] // 2), row, row, row],
         [shaped(rows, width)] * 2 + [shaped(2 * rows, 2 * LANES)] * heads,
         [part, part] + [block] * heads,
-        grid=(2,), scratch=[pltpu.VMEM((heads, rows, 2 * LANES), BF16)], vmem=32,
+        grid=(2,), scratch=[pltpu.VMEM((heads, rows, 2 * LANES), BF16)], vmem=58,
         micros=5)
 
 
@@ -303,14 +305,12 @@
     own, other = refs[:count], refs[count : 2 * count]
     xo_ref, xt_ref, w_ref, gain_ref, y_ref, ho_ref, ht_ref, o_ref = refs[2 * count :]
     turn = pl.program_id(0)
-    y = jnp.where(turn == 0, xo_ref[...], xt_ref[...]).astype(F32)
     for core, blocks in ((ids[CORE], own), (1 - ids[CORE], other)):
         for step in range(count):
             head = core * count + jnp.bitwise_xor(ids[PLANE], step)
-            span = pl.ds(pl.multiple_of(head * LANES, LANES), LANES)
-            part = blocks[step][...]
-            o_ref[:, span] = part
-            y = y + dot_nn(part, w_ref[span, :])
+            o_ref[:, pl.ds(pl.multiple_of(head * LANES, LANES), LANES)] = blocks[step][...]
+    y = jnp.where(turn == 0, xo_ref[...], xt_ref[...]).astype(F32)
+    y = y + dot_nn(o_ref[...], w_ref[...])
     h = (y * lax.rsqrt(jnp.mean(y * y, axis=1, keepdims=True) + EPSILON) * gain_ref[...]).astype(
         BF16)
 
@@ -336,18 +336,30 @@
         [shaped(rows, width, dtype=F32), shaped(rows, width), shaped(rows, width),
          shaped(2 * rows, width)],
         [part, part, part, pl.BlockSpec((rows, width), lambda i, ids: (i, 0))],
-        grid=(2,), vmem=24, micros=4)
-
-
-def feed_kernel(ids, ho_ref, ht_ref, co_ref, ct_ref, wg_ref, wu_ref, wd_ref, *refs):
-    m_ref, dg_ref, du_ref, ha_ref, ca_ref, do_ref, dt_ref, yo_ref, yt_ref = refs[-9:]
+        grid=(2,), vmem=58, micros=4)
+
+
+def feed_kernel(ids, ho_ref, ht_ref, co_ref, ct_ref, wg_all, wu_all, wd_all, *refs):
+    m_ref, dg_ref, du_ref, ha_ref, ca_ref, do_ref, dt_ref, yo_ref, yt_ref = refs[-13:-4]
+    wg_ref, wu_ref, wd_ref, arrivals = refs[-4:]
     rows = ho_ref.shape[0]
+    units = wg_ref.shape[1]
+    mine = pl.ds(pl.multiple_of((2 * ids[2] + ids[CORE]) * units, LANES), units)
+    gates = pltpu.make_async_copy(wg_all.at[:, mine], wg_ref, arrivals.at[0])
+    ups = pltpu.make_async_copy(wu_all.at[:, mine], wu_ref, arrivals.at[1])
+    downs = pltpu.make_async_copy(wd_all.at[mine, :], wd_ref, arrivals.at[2])
+    gates.start()
+    ups.start()
+    downs.start()
     ha_ref[0:rows, :] = ho_ref[...]
     ha_ref[rows:, :] = ht_ref[...]
     ca_ref[0:rows, :] = co_ref[...]
     ca_ref[rows:, :] = ct_ref[...]
+    gates.wait()
     gate = dot_nn(ha_ref[...], wg_ref[...])
+    ups.wait()
     up = dot_nn(ha_ref[...], wu_ref[...])
+    downs.wait()
     sig = jax.nn.sigmoid(gate)
     silu = gate * sig
     m_ref[...] = (silu * up).astype(BF16)
@@ -362,20 +374,21 @@
     yt_ref[...] = y[rows:].astype(BF16)
 
 
-def feed(ids, h_own, h_other, c_own, c_other, w_gate, w_up, w_down, earlier):
+def feed(ids, h_own, h_other, c_own, c_other, w_gate, w_up, w_down, earlier, units):
     rows, width = h_own.shape
-    units = w_gate.shape[1]
     half = 1 if earlier else 0
     part = whole((rows, width))
+    anywhere = pl.BlockSpec(memory_space=pl.ANY)
     kept = lambda cols: pl.BlockSpec((2 * rows, cols), lambda i, ids: (half, 0))
     cols = [units] * 3 + [width] * 2
     return run_kernel(
         feed_kernel, "feed", ids, (h_own, h_other, c_own, c_other, w_gate, w_up, w_down, *earlier),
-        [part] * 4 + [whole(w.shape) for w in (w_gate, w_up, w_down)]
-        + [pl.BlockSpec(memory_space=pl.ANY)] * len(earlier),
+        [part] * 4 + [anywhere] * (3 + len(earlier)),
         [shaped(4 * rows, n) for n in cols] + [shaped(rows, width)] * 4,
         [kept(n) for n in cols] + [part] * 4,
-        vmem=44, micros=12, aliases={8 + k: k for k in range(len(earlier))})
+        scratch=[pltpu.VMEM((width, units), BF16)] * 2
+        + [pltpu.VMEM((units, width), BF16), pltpu.SemaphoreType.DMA((3,))],
+        vmem=58, micros=12, aliases={8 + k: k for k in range(len(earlier))})
 
 
 def turn_kernel(ids, near_ref, twin_ref, far_ref, y_ref, c_ref, gain_ref, dy_ref, da_ref, sum_ref):
@@ -418,7 +431,7 @@
         [part, part, whole(w_out.shape)],
         [shaped(2 * rows, width // 2)] + [shaped(2 * rows, LANES)] * count,
         [pl.BlockSpec((rows, width // 2), lambda i, ids: (i, 0))] + [block] * count,
-        grid=(2,), vmem=24, micros=2)
+        grid=(2,), vmem=58, micros=2)
 
 
 def attend_back_kernel(ids, qaug_ref, kaug_ref, vaug_ref, wide_ref, *refs):
@@ -551,7 +564,7 @@
         + [pl.BlockSpec((width, LANES), lambda i, ids: (0, head(ids))), pair, pair,
            whole(cosine.shape), whole(sine.shape), row, row, whole(dq.shape), whole(dkv.shape)],
         outs, [whole(o.shape) for o in outs],
-        scratch=[pltpu.VMEM((2 * LANES, width), F32)], vmem=44, micros=7)
+        scratch=[pltpu.VMEM((2 * LANES, width), F32)], vmem=58, micros=7)
 
 
 def back_kernel(ids, *refs):
@@ -580,7 +593,7 @@
         back_kernel, "to_tokens", ids, (*arrived, w_query, w_key, w_value),
         [whole(a.shape) for a in arrived]
         + [of_core(width, w.shape[1] // 2) for w in (w_query, w_key, w_value)],
-        [shaped(rows, width)] * 2, [whole((rows, width))] * 2, vmem=24, micros=4)
+        [shaped(rows, width)] * 2, [whole((rows, width))] * 2, vmem=58, micros=4)
 
 
 def last_kernel(ids, mine_ref, twin_ref, x_ref, dy_ref, gain_ref, out_ref):
@@ -597,6 +610,38 @@
     return run_kernel(
         last_kernel, "last", ids, (mine, twin, x, dy, gain), [part] * 4 + [whole(gain.shape)],
         shaped(*x.shape, dtype=F32), part, vmem=24, micros=2)
+
+
+def unpack_kernel(half, ids, kept_ref, got_ref, out_ref, q_ref, k_ref, v_ref):
+    kept, got = kept_ref[...].astype(F32), got_ref[...].astype(F32)
+    lanes = lane_ids(kept.shape[0])
+    count = (kept.shape[1] - half) // (2 * LANES)
+    odd = (ids[PLANE] & 1) == 1
+    for core in range(2):
+        rows = jnp.where(ids[CORE] == core, kept, got)
+        out_ref[:, core * half : (core + 1) * half] = rows[:, :half]
+        blocks = [rows[:, half + s * 2 * LANES :][:, : 2 * LANES] for s in range(count)]
+        for s in range(count):
+            head = core * count + jnp.bitwise_xor(ids[PLANE], s)
+            q_ref[:, pl.ds(pl.multiple_of(head * LANES, LANES), LANES)] = blocks[s][:, :LANES]
+        for s in range(0, count, 2):
+            low = jnp.where(odd, blocks[s + 1][:, LANES:], blocks[s][:, LANES:])
+            high = jnp.where(odd, blocks[s][:, LANES:], blocks[s + 1][:, LANES:])
+            pair = core * (count // 2) + jnp.bitwise_xor(ids[PLANE], s) // 2
+            span = pl.ds(pl.multiple_of(pair * LANES, LANES), LANES)
+            k_ref[:, span] = jnp.where(lanes < 64, low, pltpu.roll(high, 64, 1))
+            v_ref[:, span] = jnp.where(lanes < 64, pltpu.roll(low, 64, 1), high)
+
+
+def unpack(ids, kept, got, half):
+    rows = kept.shape[0]
+    count = (kept.shape[1] - half) // (2 * LANES)
+    outs = [shaped(rows, n, dtype=F32)
+            for n in (2 * half, 2 * count * LANES, count * LANES, count * LANES)]
+    return run_kernel(
+        functools.partial(unpack_kernel, half), "unpack", ids, (kept, got),
+        [whole(kept.shape), whole(got.shape)], outs, [whole(o.shape) for o in outs], vmem=16,
+        micros=1)
 
 
 def body(tokens, lengths, attn_gain, w_query, w_key, w_value, query_gain, key_gain, w_out,
@@ -624,15 +669,8 @@
         slots, heads)
     arrived = [packed[0]] + [crossed(packed[s], s, n_z) for s in steps]
 
-    cot, lengths_late, *w_late = after(
-        (cotangent, lengths, w_gate, w_up, w_down), packed[0])
-    cot_other = swap(cot, "c")
-    cot_far = swap(cot, "x")
-    cot_far_other = swap(cot_far, "c")
+    lengths_late = after(lengths, arrived[1])
     units = w_gate.shape[1] // 4
-    place = (2 * i_x + i_c) * units
-    wg, wu = (lax.dynamic_slice_in_dim(w, place, units, 1) for w in w_late[:2])
-    wd = lax.dynamic_slice_in_dim(w_late[2], place, units, 0)
     token = jnp.arange(2 * rows * n_z, dtype=jnp.int32)
     start, edge = jnp.zeros_like(token), jnp.zeros((), jnp.int32)
     for slot in range(slots - 1):
@@ -642,63 +680,89 @@
     sign = jnp.asarray(np.where(lane % head_size < head_size // 2, -1.0, 1.0).astype(np.float32))
     cosine, sine = jnp.cos(angles), jnp.sin(angles) * sign[None, :]
 
+    arrived = after(arrived, cosine, sine)
     *o_sent, wide, qaug, kaug, vaug = attend(ids, arrived, slots)
     o_own = [o_sent[0]] + [crossed(o_sent[s], s, n_z) for s in steps]
-    o_other = [swap(o, "c") for o in o_own]
+    o_other = [swap(o, "c") for o in [o_own[0]] + after(o_own[1:], *o_own[1:])]
+    cot = after(cotangent, *o_own[1:])
+    cot_other = swap(cot, "c")
+    cot_far = swap(cot, "x")
+    cot_far_other = swap(cot_far, "c")
     y_mine, h2_own, h2_other, o_rows = middle(
         ids, o_own, o_other, tokens, x_other, w_out, f_gain)
 
-    h_line = after(h_own, o_own[-1])
-    blocks = [h_own, h_other]
-    for s in steps:
-        one = crossed(h_line, s, n_z)
-        blocks += [one, swap(one, "c")]
+    h_line = after(h_own, h2_own)
+    line = [along(h_line, h_line, n_z)]
 
     h2_far = swap(h2_own, "x")
     *kept, d_own, d_other, y_own, y_other = feed(
-        ids, h2_own, h2_other, cot, cot_other, wg, wu, wd, ())
-    h2_far_other = swap(after(h2_far, d_own), "c")
+        ids, h2_own, h2_other, cot, cot_other, w_gate, w_up, w_down, (), units)
+    h2_far_other = swap(after(h2_far, d_own, line[0]), "c")
+    line.append(along(*line[0], n_z))
     d_twin = swap(d_other, "c")
     *kept, d_far, d_far_other, y_far, y_far_other = feed(
-        ids, h2_far, h2_far_other, cot_far, cot_far_other, wg, wu, wd, tuple(kept))
-    d_home = swap(d_far + swap(d_far_other, "c"), "x")
+        ids, h2_far, after(h2_far_other, d_twin, cot_far_other), cot_far, cot_far_other, w_gate, w_up, w_down,
+        tuple(kept), units)
 
     m, dg, du, h2_all, cot_all = kept
     piece = units // (n_y * n_z)
     row_block = width // (n_y * 2 * n_z * 2)
-    m, dg, du = after((m, dg, du), d_far_other, *blocks[2:])
-
+    grad_down = dot_tn(m, cot_all).astype(BF16)
+    down = Pair(jnp.moveaxis(grad_down.reshape(n_z, n_y, piece, width), 1, 0), i_y)
+    d_far_other, y_far, y_far_other, y_other = after(
+        (d_far_other, y_far, y_far_other, y_other), line[1], down.sent)
+    line.append(along(*line[1], n_z))
+    d_sum = d_far + swap(d_far_other, "c")
+    d_home = swap(d_sum, "x")
+    y_far = y_far + swap(y_far_other, "c")
+    y_near = y_own.astype(F32) + swap(y_other, "c").astype(F32)
+    dg = after(dg, d_sum, y_far, y_near)
+    grad_gate = dot_tn(h2_all, dg).astype(BF16).reshape(n_y, 2, n_z, 2, row_block, units)
+    du = after(du, grad_gate)
+    grad_up = dot_tn(h2_all, du).astype(BF16).reshape(n_y, 2, n_z, 2, row_block, units)
+    d_home = after(d_home, grad_down, grad_gate, grad_up, *line[2])
     dy, da, gain_ffn = turn(ids, d_own, d_twin, d_home, y_mine, cotangent, f_gain)
     da_other = swap(da, "c")
+    gate = Pair(grad_gate, i_y)
+    y_home = swap(after(y_far, da), "x")
     da_cols, *do_sent = to_heads(ids, da, da_other, w_out, heads)
+    do_sent = after(do_sent, down.got)
+    near = jnp.where(i_z % 2 == 0, line[0][1], line[0][0])
+    beyond = jnp.where(i_z <= 1, line[1][1], line[1][0])
+    across = jnp.where(
+        i_z == 0, line[2][1],
+        jnp.where(i_z == 1, line[0][1], jnp.where(i_z == 2, line[0][0], line[2][0])))
+    blocks = [h_own, h_other]
+    for one in after((near, beyond, across), do_sent[0]):
+        blocks += [one, swap(one, "c")]
+
     do_arrived = [do_sent[0]] + [crossed(do_sent[s], s, n_z) for s in steps]
-    dq, dkv = attend_back(ids, qaug, kaug, vaug, wide, do_arrived)
-
-    down = dot_tn(m, cot_all).astype(BF16).reshape(n_z, n_y, piece, width)
-    down = Halving(reduce_y(jnp.moveaxis(down, 1, 0), i_y, do_sent[0]), i_z)
-
-    def over_y(grad, *needed):
-        grad = grad.astype(BF16).reshape(n_y, 2, n_z, 2, row_block, -1)
-        return Halving(jnp.moveaxis(reduce_y(grad, i_y, *needed), 1, 0), i_z)
-
-    down.advance(do_arrived[-1])
+    down = Halving(down.finish(*do_arrived[1:]), i_z)
+    down.advance()
     out_parts = dot_tn(o_rows, after(da_cols, do_sent[0])).astype(BF16).reshape(
         n_y, 2, n_z, 2, row_block, width // 2)
-    out_parts = pair_reduce(jnp.moveaxis(out_parts, 1, 0), "x", i_x, dq)
-
-    *back, grad_head, gain_attn, gains = unturn(
-        ids, blocks, w_query, w_key, w_value, cosine, sine, qg, kg, dq, dkv, head_size, heads)
-    back_arrived = [back[0]] + [crossed(back[s], s, n_z) for s in steps]
-    late = back_arrived[-1]
-    gate = over_y(dot_tn(h2_all, dg), back[0])
-    up = over_y(dot_tn(h2_all, du), late)
+    out_parts = Pair(jnp.moveaxis(out_parts, 1, 0), i_x, do_arrived[-1], axis_name="x")
+    up = Pair(grad_up, i_y, do_sent[0])
+    dq, dkv = attend_back(
+        ids, qaug, kaug, vaug, wide, after(do_arrived, *blocks[3::2]))
+    mixed = (y_mine + (y_near + after(y_home, dq).astype(F32))).astype(BF16)
+
+    out_parts = out_parts.finish(dq)
+    gate = Halving(jnp.moveaxis(gate.finish(dq), 1, 0), i_z)
     down.advance(dq)
     gate.advance()
+    *back, grad_head, gain_attn, gains = unturn(
+        ids, blocks, w_query, w_key, w_value, cosine, sine, qg, kg,
+        after(dq, down.sent, gate.sent, out_parts, mixed), dkv, head_size, heads)
+    up = Halving(jnp.moveaxis(up.finish(back[0]), 1, 0), i_z)
+    back = after(back, down.parts, gate.parts, up.parts)
+    back_arrived = [back[0]] + [crossed(back[s], s, n_z) for s in steps]
+    late = tuple(back_arrived[1:])
+    up.advance()
     dh_own, dh_other = to_tokens(ids, back_arrived, w_query, w_key, w_value)
+    gate.advance(back_arrived[1])
     grad_tokens = last(ids, dh_own, swap(dh_other, "c"), tokens, dy, a_gain)
 
-    gate.advance(late)
-    up.advance()
     owners = []
     for y in range(n_y):
         for x in range(2):
@@ -706,7 +770,7 @@
                 for c in range(2):
                     source = ((y * 2 + x) * n_z + z) * 2 + c
                     owners.append((source, n_y * n_z * (2 * x + c) + z * n_y + y))
-    share_down = lax.ppermute(after(down.finish(), late), ALL, owners).astype(F32)
+    share_down = lax.ppermute(after(down.finish(), *late), ALL, owners).astype(F32)
 
     def spread(parts):
         got = swap(pick(parts, 1 - i_c, 1), "c")
@@ -717,34 +781,51 @@
     share_gate = spread(gate.finish())
     share_up = spread(up.finish())
 
-    parts = after(grad_head, back[0]).reshape(n_y, 2, n_z, 2, row_block, 2 * LANES)
-    parts = pair_reduce(jnp.moveaxis(parts, 1, 0), "x", i_x, late)
     half = width // 2
-    parts = reduce_y(jnp.concatenate([out_parts, parts], axis=-1), i_y)
-    got = [pick(parts, i_z)] + [crossed(pick(parts, i_z ^ s), s, n_z) for s in steps]
-    out_sum = got[0][..., :half].astype(F32)
-    for one in got[1:]:
-        out_sum = out_sum + one[..., :half].astype(F32)
-    by_step = jnp.stack(got)[..., half:]
-    merged = jnp.concatenate(
-        [out_sum.astype(BF16)] + [pick(by_step, i_z ^ z) for z in range(n_z)], axis=-1)
-    kept_c, got = pick(merged, i_c), swap(pick(merged, 1 - i_c), "c")
-    share_out = in_order(i_c, kept_c[:, :half], got[:, :half], 1).astype(F32)
-    by_head = in_order(i_c, kept_c[:, half:], got[:, half:], 1).astype(F32)
-    by_head = by_head.reshape(row_block, 2 * heads, 2 * LANES)
-    share_query = by_head[:, :, :LANES].reshape(row_block, -1)
-    share_key = by_head[:, :, LANES : LANES + head_size].reshape(row_block, -1)
-    share_value = by_head[:, :, LANES + head_size :].reshape(row_block, -1)
-
-    y_own, y_other, y_far, y_far_other = after((y_own, y_other, y_far, y_far_other), do_sent[0])
-    y_home = swap(y_far + swap(y_far_other, "c"), "x")
-    y_sum = y_own.astype(F32) + swap(y_other, "c").astype(F32) + y_home.astype(F32)
-    mixed = (y_mine + y_sum).astype(BF16)
-
-    sums = sum_all(
-        after(jnp.concatenate(
-            [gain_attn / a_gain, gain_ffn, gains[0:1, :head_size] + gains[0:1, head_size:],
-             gains[1:2, :head_size]], axis=1), late), n_y, n_z)[0]
+    sums = jnp.concatenate(
+        [gain_attn / a_gain, gain_ffn, gains[0:1, :head_size] + gains[0:1, head_size:],
+         gains[1:2, :head_size]], axis=1)
+    total = sums.shape[1]
+    sums = jnp.pad(sums, ((0, 0), (0, -total % (16 * 2 * LANES)))).reshape(-1, 2 * LANES)
+    depth = sums.shape[0]
+    parts = after(grad_head, back[0]).reshape(n_y, 2, n_z * 2 * row_block, 2 * LANES)
+    parts = jnp.moveaxis(parts, 1, 0).reshape(2, -1, 2 * LANES)
+    kept_x = pick(parts, i_x)
+    got = swap(jnp.concatenate([pick(parts, 1 - i_x), *split_up(sums)], axis=0), "x")
+    count = kept_x.shape[0]
+    sums = sums + sum(got[count + k * depth :][:depth].astype(F32) for k in range(3))
+    parts = jnp.concatenate([out_parts.reshape(-1, half), kept_x + got[:count]], axis=1)
+    parts = parts.reshape(n_y, n_z * 2 * row_block, half + 2 * LANES)
+
+    def joined(rows_sent, vector):
+        beside = jnp.concatenate(split_up(vector), axis=1)
+        wider = rows_sent.shape[1] - beside.shape[1]
+        return jnp.concatenate([rows_sent, jnp.pad(beside, ((0, 0), (0, wider)))], axis=0)
+
+    def parted(got):
+        vector = got[-depth:].astype(F32)
+        return got[:-depth], sum(
+            vector[:, k * 2 * LANES : (k + 1) * 2 * LANES] for k in range(3))
+
+    if n_y == 2:
+        got, more = parted(swap(joined(pick(parts, 1 - i_y), sums), "y"))
+        parts, sums = pick(parts, i_y) + got, sums + more
+    else:
+        parts = lax.psum_scatter(parts, "y", scatter_dimension=0, tiled=False)
+        sums = lax.psum(sums, "y")
+    parts = parts.reshape(n_z, 2 * row_block, half + 2 * LANES)
+    kept_z, sums_z = pick(parts, i_z), sums
+    out_sum, by_step = kept_z[:, :half].astype(F32), [kept_z[:, half:]]
+    for s in steps:
+        got, more = parted(crossed(joined(pick(parts, i_z ^ s), sums), s, n_z))
+        out_sum, sums_z = out_sum + got[:, :half].astype(F32), sums_z + more
+        by_step.append(got[:, half:])
+    merged = jnp.concatenate([out_sum.astype(BF16), *by_step], axis=1)
+    merged = merged.reshape(2, row_block, merged.shape[1])
+    got, more = parted(swap(joined(pick(merged, 1 - i_c), sums_z), "c"))
+    sums = (sums_z + more).reshape(-1)
+    share_out, share_query, share_key, share_value = unpack(ids, pick(merged, i_c), got, half)
+
     return (
         mixed,
         grad_tokens,
@@ -753,7 +834,7 @@
         share_key,
         share_value,
         sums[2 * width : 2 * width + head_size],
-        sums[2 * width + head_size :],
+        sums[2 * width + head_size : total],
         share_out,
         sums[width : 2 * width],
         share_gate,

time: 346 us -> 322 us (0.931)
  waiting for transfers between devices: 120 us -> 83.5 us
  local copies, waits for them, and re-layouts: 48.2 us -> 24.4 us
  Pallas kernels: 77.4 us -> 93.6 us
  other arithmetic: 16.8 us -> 27.1 us
  starting transfers between devices: 65.1 us -> 71.8 us
    ppermute x26 -> x21, waiting for transfers between devices: 92 us -> 67.7 us  [crossed(): return lax.ppermute(field, 'z', [(k, k ^ step) for k in range(count)])]
    ppermute x1 -> x7, starting transfers between devices: 0.68 us -> 18.7 us  [the longest x3 13.7 us: along(): lax.ppermute(to_right, 'z', [(k, k + 1) for k in pairs])]
    pallas_call x11 -> x12, Pallas kernels: 77.4 us -> 93.6 us  [run_kernel(): pl.pallas_call(kernel, grid_spec=pltpu.PrefetchScalarGridSpec(num_scalar_...]
    ppermute x26 -> x21, starting transfers between devices: 48.7 us -> 34.4 us  [crossed(): return lax.ppermute(field, 'z', [(k, k ^ step) for k in range(count)])]
    unnamed x144 -> x151, local copies, waits for them, and re-layouts: 28.2 us -> 14.3 us
    ppermute x35 -> x32, waiting for transfers between devices: 28 us -> 15.8 us  [swap(): return lax.ppermute(field, axis_name, [(0, 1), (1, 0)])]
    dynamic_slice x2 -> x0, local copies, waits for them, and re-layouts: 8.33 us -> none  [the longest x1 4.94 us: body(): wg, wu = (lax.dynamic_slice_in_dim(w, place, units, 1) for w in w_late[:2])]
    ppermute x35 -> x32, starting transfers between devices: 15.7 us -> 18.7 us  [swap(): return lax.ppermute(field, axis_name, [(0, 1), (1, 0)])]
  transfers between devices with their start and end apart: 62 -> 60, of which waited for: 23 -> 15; matrix products, arithmetic and copies ran while one was open for 14% -> 16% of each run, Pallas kernels for 18% -> 24%
where the time goes in v3:
time: 322 us; the launch traced here: 318 us
  Pallas kernels  93.6 us (29%)
  waiting for transfers between devices  83.5 us (26%)
  starting transfers between devices  71.8 us (22%)
  other arithmetic  27.1 us (8%)
  local copies, waits for them, and re-layouts  24.4 us (8%)
  matrix products  13.6 us (4%)
  between operations  4.28 us (1%)
    pallas_call x12, Pallas kernels, run_kernel(): pl.pallas_call(kernel, grid_spec=pltpu.PrefetchScalarGridSpec(num_scalar_...  93.6 us
    ppermute x21, waiting for transfers between devices, crossed(): return lax.ppermute(field, 'z', [(k, k ^ step) for k in range(count)])  67.7 us
    ppermute x21, starting transfers between devices, crossed(): return lax.ppermute(field, 'z', [(k, k ^ step) for k in range(count)])  34.4 us
    ppermute x32, starting transfers between devices, swap(): return lax.ppermute(field, axis_name, [(0, 1), (1, 0)])  18.7 us
    ppermute x32, waiting for transfers between devices, swap(): return lax.ppermute(field, axis_name, [(0, 1), (1, 0)])  15.8 us
    unnamed x151, local copies, waits for them, and re-layouts  14.3 us
    ppermute x3, starting transfers between devices, along(): lax.ppermute(to_right, 'z', [(k, k + 1) for k in pairs])  13.7 us
    dot_general x4, matrix products, dot_tn(): lax.dot_general(left, right, (((0,), (0,)), ((), ())), preferred_element_...  13.6 us
  transfers between devices with their start and end apart: 60, of which 15 were waited for; matrix products, arithmetic and copies ran while one was open for 16% of the time, Pallas kernels for 24%

profile of v3, /device:TPU:0, one launch (start us, length us, event | category | flops | bytes accessed | tf_op | source)
XLA Modules:
  0.0 318.3 jit_solution(9627504652488885663)
XLA Ops:
  5.8 8.0 %project.1 = (bf16[256,1024]{1,0:T(8,128)(2,1)}, bf16[256,1024]{1,0:T(8,128)(2,1)}, bf16[512,256]{1,0:T(8,128)(2,1)}, bf16[512,256]{1,0:T(8,128)(2,1)}, bf16[512...) custom-call(s32[8]{0:T(128)} %concatenate.58.ids, bf16[256,1024]{1,0:T(8,128)(2,1)} %x_ref.1, bf16[256,1024]{1,0:T(8,128)(2,1)} %copy-done.40, ...), custom_call_target="tpu_custom_call" | custom-call | flops 500000 | bytes 1024 | tf_op jit(solution)/shard_map/project/pallas_call | solution.py:109
  13.8 2.7 collective-permute-start.1
  16.5 2.6 collective-permute-start.2
  19.1 9.7 %collective-permute-done.1.refs_1_ = bf16[512,256]{1,0:T(8,128)(2,1)S(1)} collective-permute-done((bf16[512,256]{1,0:T(8,128)(2,1)}, bf16[512,256]{1,0:T(8,128)(2,1)S(1)}, u32[]{:S(2)}, u32[]{:S(2)}) %collective-permute-start.1) | collective-permute-done | bytes 262176 | tf_op jit(solution)/shard_map/ppermute | solution.py:49
  32.0 6.1 %fusion = (f32[2048,128]{1,0:T(8,128)}, f32[2048,128]{1,0:T(8,128)}) fusion(f32[128]{0:T(128)S(1)} %copy-done.66, f32[128]{0:T(128)S(1)} %copy-done.67, f32[2048]{0:T(1024)S(1)} %subtract_convert_fusion.4), kind=kLoop, calls=%fused_computation.12 | loop fusion | flops 524288 | bytes 2106368 | tf_op jit(solution)/shard_map/mul | solution.py:681
  42.5 9.4 %attend.1 = (bf16[512,128]{1,0:T(8,128)(2,1)S(1)}, bf16[512,128]{1,0:T(8,128)(2,1)S(1)}, bf16[512,128]{1,0:T(8,128)(2,1)S(1)}, bf16[512,128]{1,0:T(8,128)(2,1)S(...) custom-call(s32[8]{0:T(128)S(1)} %copy-done.24, ...), custom_call_target="tpu_custom_call" | custom-call | flops 900000 | bytes 1024 | tf_op jit(solution)/shard_map/attend/pallas_call | solution.py:109
  52.7 4.5 %collective-permute-start.4 = (bf16[512,128]{1,0:T(8,128)(2,1)S(1)}, bf16[512,128]{1,0:T(8,128)(2,1)S(1)}, u32[]{:S(2)}, u32[]{:S(2)}) collective-permute-start(bf16[512,128]{1,0:T(8,128)(2,1)S(1)} %get-tuple-element.130), channel_id=1, source_target_pairs={{0,2},{2,0},{4,6},{6,4},{1,3},{3,1},{5,7},{7,5},{8,10},{10,8},{12,... | collective-permute-start | bytes 393224 | tf_op jit(solution)/shard_map/ppermute | solution.py:49
  61.5 8.1 %collective-permute-done.5.refs_2_ = bf16[512,128]{1,0:T(8,128)(2,1)S(1)} collective-permute-done((bf16[512,128]{1,0:T(8,128)(2,1)S(1)}, bf16[512,128]{1,0:T(8,128)(2,1)S(1)}, u32[]{:S(2)}, u32[]{:S(2)}) %collective-permute-start.5) | collective-permute-done | bytes 131104 | tf_op jit(solution)/shard_map/ppermute | solution.py:49
  73.0 6.8 %middle.1 = (f32[256,1024]{1,0:T(8,128)}, bf16[256,1024]{1,0:T(8,128)(2,1)}, bf16[256,1024]{1,0:T(8,128)(2,1)}, bf16[512,1024]{1,0:T(8,128)(2,1)}) custom-call(s32[8]{0:T(128)} %concatenate.58.ids, bf16[512,128]{1,0:T(8,128)(2,1)} %copy-done.23, bf16[512,128]{1,0:T(8,128)(2,1)} %copy-done.57, bf16[512,128]{1,0:T(8,128)(2,1)} %copy-done.58, ...), custom_call_target="tpu_custom_call" | custom-call | flops 400000 | bytes 1024 | tf_op jit(solution)/shard_map/middle/pallas_call | solution.py:109
  80.6 3.8 %collective-permute-start.13 = (bf16[256,1024]{1,0:T(8,128)(2,1)S(1)}, bf16[256,1024]{1,0:T(8,128)(2,1)S(1)}, u32[]{:S(2)}, u32[]{:S(2)}) collective-permute-start(bf16[256,1024]{1,0:T(8,128)(2,1)S(1)} %copy-done.43), channel_id=1, source_target_pairs={{0,2},{2,4},{4,6},{1,3},{3,5},{5,7},{8,10},{10,12},{12,14},{9,11},... | collective-permute-start | bytes 1572872 | tf_op jit(solution)/shard_map/ppermute | solution.py:54
  86.8 14.2 %feed.2 = (bf16[1024,1152]{1,0:T(8,128)(2,1)}, bf16[1024,1152]{1,0:T(8,128)(2,1)}, bf16[1024,1152]{1,0:T(8,128)(2,1)}, bf16[1024,1024]{1,0:T(8,128)(2,1)}, bf16[...) custom-call(s32[8]{0:T(128)} %concatenate.58.ids, ...), custom_call_target="tpu_custom_call" | custom-call | flops 1200000 | bytes 1024 | tf_op jit(solution)/shard_map/feed/pallas_call | solution.py:109
  103.3 5.3 %collective-permute-start.19 = (bf16[256,1024]{1,0:T(8,128)(2,1)}, bf16[256,1024]{1,0:T(8,128)(2,1)}, u32[]{:S(2)}, u32[]{:S(2)}) collective-permute-start(bf16[256,1024]{1,0:T(8,128)(2,1)} %copy-done.52), channel_id=1, source_target_pairs={{0,2},{2,4},{4,6},{1,3},{3,5},{5,7},{8,10},{10,12},{12,14},{9,11},... | collective-permute-start | bytes 1572872 | tf_op jit(solution)/shard_map/ppermute | solution.py:54
  111.0 14.3 %feed.3 = (bf16[1024,1152]{1,0:T(8,128)(2,1)}, bf16[1024,1152]{1,0:T(8,128)(2,1)}, bf16[1024,1152]{1,0:T(8,128)(2,1)}, bf16[1024,1024]{1,0:T(8,128)(2,1)}, bf16[...) custom-call(s32[8]{0:T(128)} %concatenate.58.ids, ...), custom_call_target="tpu_custom_call", output_to_operand_aliasing={{0}: (8, {}), {1}: (9, {}), {2}: (10, {}), {3}: (11, {}), {... | custom-call | flops 1200000 | bytes 1024 | tf_op jit(solution)/shard_map/feed/pallas_call | solution.py:109
  125.3 4.9 %convolution_convert_fusion.2 = bf16[1152,1024]{1,0:T(8,128)(2,1)S(1)} fusion(bf16[1024,1152]{1,0:T(8,128)(2,1)} %get-tuple-element.156, bf16[1024,1024]{1,0:T(8,128)(2,1)} %get-tuple-element.157), kind=kOutput, calls=%fused_computation.2 | convolution fusion | flops 2417098752 | bytes 6815744 | tf_op jit(solution)/shard_map/dot_general | solution.py:33
  134.7 4.6 %collective-permute-start.25 = (bf16[256,1024]{1,0:T(8,128)(2,1)}, bf16[256,1024]{1,0:T(8,128)(2,1)S(1)}, u32[]{:S(2)}, u32[]{:S(2)}) collective-permute-start(bf16[256,1024]{1,0:T(8,128)(2,1)} %collective-permute-done.19), channel_id=1, source_target_pairs={{0,2},{2,4},{4,6},{1,3},{3,5},{5,7},{8,10},{10,12},{12,14},{9,11},... | collective-permute-start | bytes 1572872 | tf_op jit(solution)/shard_map/ppermute | solution.py:54
  147.2 3.2 %convolution_convert_fusion.1 = bf16[1024,1152]{1,0:T(8,128)(2,1)S(1)} fusion(bf16[1024,1024]{1,0:T(8,128)(2,1)S(1)} %copy-done.38, bf16[1024,1152]{1,0:T(8,128)(2,1)S(1)} %copy-done.30), kind=kOutput, calls=%fused_computation.1 | convolution fusion | flops 2417098752 | bytes 6815744 | tf_op jit(solution)/shard_map/dot_general | solution.py:33
  153.3 3.2 convolution_convert_fusion
  161.7 5.2 %to_heads.1 = (bf16[512,512]{1,0:T(8,128)(2,1)}, bf16[512,128]{1,0:T(8,128)(2,1)}, bf16[512,128]{1,0:T(8,128)(2,1)}, bf16[512,128]{1,0:T(8,128)(2,1)}, bf16[512,128]{1,0:T(8,128)(2,1)}) custom-call(s32[8]{0:T(128)} %concatenate.58.ids, bf16[256,1024]{1,0:T(8,128)(2,1)} %copy-done.14, bf16[256,1024]{1,0:T(8,128)(2,1)} %copy-done.56, bf16[1024,1024]{1,0:T(8,128)(2,1)} %w_ref.1), custom_call_target="tpu_custom_call" | custom-call | flops 200000 | bytes 1024 | tf_op jit(solution)/shard_map/to_heads/pallas_call | solution.py:109
  167.0 2.4 collective-permute-start.30
  175.5 7.1 %collective-permute-done.31.refs_2_ = bf16[512,128]{1,0:T(8,128)(2,1)S(1)} collective-permute-done((bf16[512,128]{1,0:T(8,128)(2,1)}, bf16[512,128]{1,0:T(8,128)(2,1)S(1)}, u32[]{:S(2)}, u32[]{:S(2)}) %collective-permute-start.31) | collective-permute-done | bytes 131104 | tf_op jit(solution)/shard_map/ppermute | solution.py:49
  188.8 13.3 %attend_back.1 = (f32[2048,128]{1,0:T(8,128)S(1)}, f32[2048,128]{1,0:T(8,128)S(1)}) custom-call(s32[8]{0:T(128)S(1)} %copy-done.26, bf16[2,2048,128]{2,1,0:T(8,128)(2,1)S(1)} %get-tuple-element.171.qaug_ref, bf16[2048,128]{1,0:T(8,128)(2,1)S(1)} %copy-done.8, bf16[2048,128]{1,0:T(8,128)(2,1)S(1)} %copy-done.10, f32[2048,128]{1,0:T(8,128)S(1)} %get-tuple-element.174.wide_ref, ...), custom_call_target="tpu_custom_call" | custom-call | flops 1300000 | bytes 1024 | tf_op jit(solution)/shard_map/attend_back/pallas_call | solution.py:109
  207.2 8.5 %collective-permute-done.38 = bf16[2,4,2,32,512]{4,3,2,1,0:T(8,128)(2,1)S(1)} collective-permute-done((bf16[2,4,2,32,512]{4,3,2,1,0:T(8,128)(2,1)S(1)}, bf16[2,4,2,32,512]{4,3,2,1,0:T(8,128)(2,1)S(1)}, u32[]{:S(2)}, u32[]{:S(2)}) %collective-permute-start.38) | collective-permute-done | bytes 524320 | tf_op jit(solution)/shard_map/ppermute | solution.py:45
  217.1 12.0 %unturn.1 = (bf16[512,256]{1,0:T(8,128)(2,1)}, bf16[512,256]{1,0:T(8,128)(2,1)}, bf16[512,256]{1,0:T(8,128)(2,1)}, bf16[512,256]{1,0:T(8,128)(2,1)}, bf16[1024,2...) custom-call(s32[8]{0:T(128)} %concatenate.58.ids, bf16[256,1024]{1,0:T(8,128)(2,1)} %get-tuple-element.143.refs_0_, ...), custom_call_target="tpu_custom_call" | custom-call | flops 700000 | bytes 1024 | tf_op jit(solution)/shard_map/unturn/pallas_call | solution.py:109
  240.2 6.3 %collective-permute-done.42.refs_1_ = bf16[512,256]{1,0:T(8,128)(2,1)} collective-permute-done((bf16[512,256]{1,0:T(8,128)(2,1)S(1)}, bf16[512,256]{1,0:T(8,128)(2,1)}, u32[]{:S(2)}, u32[]{:S(2)}) %collective-permute-start.42) | collective-permute-done | bytes 262176 | tf_op jit(solution)/shard_map/ppermute | solution.py:49
  246.5 8.3 %collective-permute-done.43.refs_2_ = bf16[512,256]{1,0:T(8,128)(2,1)} collective-permute-done((bf16[512,256]{1,0:T(8,128)(2,1)S(1)}, bf16[512,256]{1,0:T(8,128)(2,1)}, u32[]{:S(2)}, u32[]{:S(2)}) %collective-permute-start.43) | collective-permute-done | bytes 262176 | tf_op jit(solution)/shard_map/ppermute | solution.py:49
  254.8 5.8 %to_tokens.1 = (bf16[256,1024]{1,0:T(8,128)(2,1)}, bf16[256,1024]{1,0:T(8,128)(2,1)}) custom-call(s32[8]{0:T(128)} %concatenate.58.ids, bf16[512,256]{1,0:T(8,128)(2,1)} %get-tuple-element.209.refs_0_, bf16[512,256]{1,0:T(8,128)(2,1)} %collective-permute-done.42.refs_1_, bf16[512,256]{1,0:T(8,128)(2,1)} %collective-permute-done.43.refs_2_, ...), custom_call_target="tpu_custom_call" | custom-call | flops 400000 | bytes 1024 | tf_op jit(solution)/shard_map/to_tokens/pallas_call | solution.py:109
  260.9 4.3 %collective-permute-start.52 = (bf16[1,2,2,32,1152]{4,3,1,2,0:T(8,128)(2,1)}, bf16[1,2,2,32,1152]{4,3,1,2,0:T(8,128)(2,1)S(1)}, u32[]{:S(2)}, u32[]{:S(2)}) collective-permute-start(bf16[1,2,2,32,1152]{4,3,1,2,0:T(8,128)(2,1)} %constant_dynamic-slice_fusion.3), channel_id=1, source_target_pairs={{0,4},{2,6},{4,0},{6,2},{1,5},{3,7},{5,1},{7,3},{8,12},{10,14},{12... | collective-permute-start | bytes 884744 | tf_op jit(solution)/shard_map/ppermute | solution.py:49
  267.7 3.2 collective-permute-start.47
  270.8 8.6 %collective-permute-done.52 = bf16[1,2,2,32,1152]{4,3,1,2,0:T(8,128)(2,1)S(1)} collective-permute-done((bf16[1,2,2,32,1152]{4,3,1,2,0:T(8,128)(2,1)}, bf16[1,2,2,32,1152]{4,3,1,2,0:T(8,128)(2,1)S(1)}, u32[]{:S(2)}, u32[]{:S(2)}) %collective-permute-start.52) | collective-permute-done | bytes 294944 | tf_op jit(solution)/shard_map/ppermute | solution.py:49
  284.6 2.7 collective-permute-start.48
  292.9 13.9 %collective-permute-done.49 = bf16[80,768]{1,0:T(8,128)(2,1)S(1)} collective-permute-done((bf16[80,768]{1,0:T(8,128)(2,1)S(1)}, bf16[80,768]{1,0:T(8,128)(2,1)S(1)}, u32[]{:S(2)}, u32[]{:S(2)}) %collective-permute-start.49) | collective-permute-done | bytes 122912 | tf_op jit(solution)/shard_map/ppermute | solution.py:49
  312.6 4.5 %collective-permute-done.58 = bf16[32,2304]{1,0:T(8,128)(2,1)S(1)} collective-permute-done((bf16[32,2304]{1,0:T(8,128)(2,1)S(1)}, bf16[32,2304]{1,0:T(8,128)(2,1)S(1)}, u32[]{:S(2)}, u32[]{:S(2)}) %collective-permute-start.58) | collective-permute-done | bytes 147488 | tf_op jit(solution)/shard_map/ppermute | solution.py:45
  (336 shorter events, 96.4 us)
Async XLA Ops:
  13.8 15.0 %collective-permute-start.1 = (bf16[512,256]{1,0:T(8,128)(2,1)}, bf16[512,256]{1,0:T(8,128)(2,1)S(1)}, u32[]{:S(2)}, u32[]{:S(2)}) collective-permute-start(bf16[512,256]{1,0:T(8,128)(2,1)} %get-tuple-element.121), channel_id=1, source_target_pairs={{0,2},{2,0},{4,6},{6,4},{1,3},{3,1},{5,7},{7,5},{8,10},{10,8},{12,... | collective-permute-start | bytes 786440 | tf_op jit(solution)/shard_map/ppermute | solution.py:49
  16.5 21.7 %collective-permute-start.2 = (bf16[512,256]{1,0:T(8,128)(2,1)}, bf16[512,256]{1,0:T(8,128)(2,1)S(1)}, u32[]{:S(2)}, u32[]{:S(2)}) collective-permute-start(bf16[512,256]{1,0:T(8,128)(2,1)} %get-tuple-element.122), channel_id=1, source_target_pairs={{0,4},{2,6},{4,0},{6,2},{1,5},{3,7},{5,1},{7,3},{8,12},{10,14},{12... | collective-permute-start | bytes 786440 | tf_op jit(solution)/shard_map/ppermute | solution.py:49
  19.1 19.9 %collective-permute-start.3 = (bf16[512,256]{1,0:T(8,128)(2,1)}, bf16[512,256]{1,0:T(8,128)(2,1)S(1)}, u32[]{:S(2)}, u32[]{:S(2)}) collective-permute-start(bf16[512,256]{1,0:T(8,128)(2,1)} %get-tuple-element.123), channel_id=1, source_target_pairs={{0,6},{2,4},{4,2},{6,0},{1,7},{3,5},{5,3},{7,1},{8,14},{10,12},{12... | collective-permute-start | bytes 786440 | tf_op jit(solution)/shard_map/ppermute | solution.py:49
  70.3 15.6 %collective-permute-start.11 = (bf16[256,1024]{1,0:T(8,128)(2,1)S(1)}, bf16[256,1024]{1,0:T(8,128)(2,1)S(1)}, u32[]{:S(2)}, u32[]{:S(2)}) collective-permute-start(bf16[256,1024]{1,0:T(8,128)(2,1)S(1)} %copy-done.2), channel_id=1, source_target_pairs={{0,1},{1,0},{2,3},{3,2},{4,5},{5,4},{6,7},{7,6},{8,9},{9,8},{10,11... | collective-permute-start | bytes 1572872 | tf_op jit(solution)/shard_map/ppermute | solution.py:45
  70.8 30.3 %collective-permute-start.17 = (bf16[256,1024]{1,0:T(8,128)(2,1)S(1)}, bf16[256,1024]{1,0:T(8,128)(2,1)}, u32[]{:S(2)}, u32[]{:S(2)}) collective-permute-start(bf16[256,1024]{1,0:T(8,128)(2,1)S(1)} %copy-done.2), channel_id=1, source_target_pairs={{0,8},{8,0},{1,9},{9,1},{2,10},{10,2},{3,11},{11,3},{4,12},{12,4},... | collective-permute-start | bytes 1572872 | tf_op jit(solution)/shard_map/ppermute | solution.py:45
  79.9 21.7 %collective-permute-start.12 = (bf16[256,1024]{1,0:T(8,128)(2,1)}, bf16[256,1024]{1,0:T(8,128)(2,1)}, u32[]{:S(2)}, u32[]{:S(2)}) collective-permute-start(bf16[256,1024]{1,0:T(8,128)(2,1)} %get-tuple-element.137.ho_ref), channel_id=1, source_target_pairs={{0,8},{8,0},{1,9},{9,1},{2,10},{10,2},{3,11},{11,3},{4,12},{12,4},... | collective-permute-start | bytes 1572872 | tf_op jit(solution)/shard_map/ppermute | solution.py:45
  80.6 20.9 %collective-permute-start.13 = (bf16[256,1024]{1,0:T(8,128)(2,1)S(1)}, bf16[256,1024]{1,0:T(8,128)(2,1)S(1)}, u32[]{:S(2)}, u32[]{:S(2)}) collective-permute-start(bf16[256,1024]{1,0:T(8,128)(2,1)S(1)} %copy-done.43), channel_id=1, source_target_pairs={{0,2},{2,4},{4,6},{1,3},{3,5},{5,7},{8,10},{10,12},{12,14},{9,11},... | collective-permute-start | bytes 1572872 | tf_op jit(solution)/shard_map/ppermute | solution.py:54
  84.5 17.1 %collective-permute-start.14 = (bf16[256,1024]{1,0:T(8,128)(2,1)S(1)}, bf16[256,1024]{1,0:T(8,128)(2,1)S(1)}, u32[]{:S(2)}, u32[]{:S(2)}) collective-permute-start(bf16[256,1024]{1,0:T(8,128)(2,1)S(1)} %copy-done.43), channel_id=1, source_target_pairs={{2,0},{4,2},{6,4},{3,1},{5,3},{7,5},{10,8},{12,10},{14,12},{11,9},... | collective-permute-start | bytes 1572872 | tf_op jit(solution)/shard_map/ppermute | solution.py:55
  103.3 29.4 %collective-permute-start.19 = (bf16[256,1024]{1,0:T(8,128)(2,1)}, bf16[256,1024]{1,0:T(8,128)(2,1)}, u32[]{:S(2)}, u32[]{:S(2)}) collective-permute-start(bf16[256,1024]{1,0:T(8,128)(2,1)} %copy-done.52), channel_id=1, source_target_pairs={{0,2},{2,4},{4,6},{1,3},{3,5},{5,7},{8,10},{10,12},{12,14},{9,11},... | collective-permute-start | bytes 1572872 | tf_op jit(solution)/shard_map/ppermute | solution.py:54
  108.6 24.1 %collective-permute-start.20 = (bf16[256,1024]{1,0:T(8,128)(2,1)}, bf16[256,1024]{1,0:T(8,128)(2,1)}, u32[]{:S(2)}, u32[]{:S(2)}) collective-permute-start(bf16[256,1024]{1,0:T(8,128)(2,1)} %copy-done.54), channel_id=1, source_target_pairs={{2,0},{4,2},{6,4},{3,1},{5,3},{7,5},{10,8},{12,10},{14,12},{11,9},... | collective-permute-start | bytes 1572872 | tf_op jit(solution)/shard_map/ppermute | solution.py:55
  133.2 33.8 %collective-permute-start.29 = (bf16[4,144,1024]{2,1,0:T(8,128)(2,1)}, bf16[4,144,1024]{2,1,0:T(8,128)(2,1)}, u32[]{:S(2)}, u32[]{:S(2)}) collective-permute-start(bf16[4,144,1024]{2,1,0:T(8,128)(2,1)} %dynamic-slice_bitcast_fusion.2), channel_id=1, source_target_pairs={{0,16},{16,0},{1,17},{17,1},{2,18},{18,2},{3,19},{19,3},{4,20},{20... | collective-permute-start | bytes 3538952 | tf_op jit(solution)/shard_map/ppermute | solution.py:45
  134.7 21.9 %collective-permute-start.25 = (bf16[256,1024]{1,0:T(8,128)(2,1)}, bf16[256,1024]{1,0:T(8,128)(2,1)S(1)}, u32[]{:S(2)}, u32[]{:S(2)}) collective-permute-start(bf16[256,1024]{1,0:T(8,128)(2,1)} %collective-permute-done.19), channel_id=1, source_target_pairs={{0,2},{2,4},{4,6},{1,3},{3,5},{5,7},{8,10},{10,12},{12,14},{9,11},... | collective-permute-start | bytes 1572872 | tf_op jit(solution)/shard_map/ppermute | solution.py:54
  139.3 17.3 %collective-permute-start.26 = (bf16[256,1024]{1,0:T(8,128)(2,1)}, bf16[256,1024]{1,0:T(8,128)(2,1)S(1)}, u32[]{:S(2)}, u32[]{:S(2)}) collective-permute-start(bf16[256,1024]{1,0:T(8,128)(2,1)} %collective-permute-done.20), channel_id=1, source_target_pairs={{2,0},{4,2},{6,4},{3,1},{5,3},{7,5},{10,8},{12,10},{14,12},{11,9},... | collective-permute-start | bytes 1572872 | tf_op jit(solution)/shard_map/ppermute | solution.py:55
  152.2 49.9 %collective-permute-start.37 = (bf16[2,4,2,32,1152]{4,3,2,1,0:T(8,128)(2,1)}, bf16[2,4,2,32,1152]{4,3,2,1,0:T(8,128)(2,1)}, u32[]{:S(2)}, u32[]{:S(2)}) collective-permute-start(bf16[2,4,2,32,1152]{4,3,2,1,0:T(8,128)(2,1)} %dynamic-slice_bitcast_fusion.1), channel_id=1, source_target_pairs={{0,16},{16,0},{1,17},{17,1},{2,18},{18,2},{3,19},{19,3},{4,20},{20... | collective-permute-start | bytes 3538952 | tf_op jit(solution)/shard_map/ppermute | solution.py:45
  182.6 23.4 %collective-permute-start.21 = (bf16[256,1024]{1,0:T(8,128)(2,1)S(1)}, bf16[256,1024]{1,0:T(8,128)(2,1)S(1)}, u32[]{:S(2)}, u32[]{:S(2)}) collective-permute-start(bf16[256,1024]{1,0:T(8,128)(2,1)S(1)} %copy-done.68), channel_id=1, source_target_pairs={{0,1},{1,0},{2,3},{3,2},{4,5},{5,4},{6,7},{7,6},{8,9},{9,8},{10,11... | collective-permute-start | bytes 1572872 | tf_op jit(solution)/shard_map/ppermute | solution.py:45
  184.7 19.8 %collective-permute-start.27 = (bf16[256,1024]{1,0:T(8,128)(2,1)S(1)}, bf16[256,1024]{1,0:T(8,128)(2,1)S(1)}, u32[]{:S(2)}, u32[]{:S(2)}) collective-permute-start(bf16[256,1024]{1,0:T(8,128)(2,1)S(1)} %copy-done.46), channel_id=1, source_target_pairs={{0,8},{8,0},{1,9},{9,1},{2,10},{10,2},{3,11},{11,3},{4,12},{12,4},... | collective-permute-start | bytes 1572872 | tf_op jit(solution)/shard_map/ppermute | solution.py:45
  186.1 52.4 %collective-permute-start.41 = (bf16[2,4,2,32,1152]{4,3,2,1,0:T(8,128)(2,1)}, bf16[2,4,2,32,1152]{4,3,2,1,0:T(8,128)(2,1)}, u32[]{:S(2)}, u32[]{:S(2)}) collective-permute-start(bf16[2,4,2,32,1152]{4,3,2,1,0:T(8,128)(2,1)} %dynamic-slice_bitcast_fusion), channel_id=1, source_target_pairs={{0,16},{16,0},{1,17},{17,1},{2,18},{18,2},{3,19},{19,3},{4,20},{20... | collective-permute-start | bytes 3538952 | tf_op jit(solution)/shard_map/ppermute | solution.py:45
  186.7 29.0 %collective-permute-start.36 = (bf16[2,144,1024]{2,1,0:T(8,128)(2,1)S(1)}, bf16[2,144,1024]{2,1,0:T(8,128)(2,1)S(1)}, u32[]{:S(2)}, u32[]{:S(2)}) collective-permute-start(bf16[2,144,1024]{2,1,0:T(8,128)(2,1)S(1)} %dynamic-slice_bitcast_fusion.3), channel_id=1, source_target_pairs={{0,2},{2,0},{4,6},{6,4},{1,3},{3,1},{5,7},{7,5},{8,10},{10,8},{12,... | collective-permute-start | bytes 1769480 | tf_op jit(solution)/shard_map/ppermute | solution.py:49
  205.4 25.7 %collective-permute-start.40 = (bf16[2,2,2,32,1152]{4,3,1,2,0:T(8,128)(2,1)}, bf16[2,2,2,32,1152]{4,3,1,2,0:T(8,128)(2,1)}, u32[]{:S(2)}, u32[]{:S(2)}) collective-permute-start(bf16[2,2,2,32,1152]{4,3,1,2,0:T(8,128)(2,1)} %bitcast.123), channel_id=1, source_target_pairs={{0,2},{2,0},{4,6},{6,4},{1,3},{3,1},{5,7},{7,5},{8,10},{10,8},{12,... | collective-permute-start | bytes 1769480 | tf_op jit(solution)/shard_map/ppermute | solution.py:49
  215.9 15.1 %collective-permute-start.39 = (bf16[1,144,1024]{2,1,0:T(8,128)(2,1)S(1)}, bf16[1,144,1024]{2,1,0:T(8,128)(2,1)S(1)}, u32[]{:S(2)}, u32[]{:S(2)}) collective-permute-start(bf16[1,144,1024]{2,1,0:T(8,128)(2,1)S(1)} %constant_dynamic-slice_fusion.6), channel_id=1, source_target_pairs={{0,4},{2,6},{4,0},{6,2},{1,5},{3,7},{5,1},{7,3},{8,12},{10,14},{12... | collective-permute-start | bytes 884744 | tf_op jit(solution)/shard_map/ppermute | solution.py:49
  233.4 21.5 %collective-permute-start.43 = (bf16[512,256]{1,0:T(8,128)(2,1)S(1)}, bf16[512,256]{1,0:T(8,128)(2,1)}, u32[]{:S(2)}, u32[]{:S(2)}) collective-permute-start(bf16[512,256]{1,0:T(8,128)(2,1)S(1)} %copy-done.70), channel_id=1, source_target_pairs={{0,4},{2,6},{4,0},{6,2},{1,5},{3,7},{5,1},{7,3},{8,12},{10,14},{12... | collective-permute-start | bytes 786440 | tf_op jit(solution)/shard_map/ppermute | solution.py:49
  235.1 19.7 %collective-permute-start.44 = (bf16[512,256]{1,0:T(8,128)(2,1)S(1)}, bf16[512,256]{1,0:T(8,128)(2,1)}, u32[]{:S(2)}, u32[]{:S(2)}) collective-permute-start(bf16[512,256]{1,0:T(8,128)(2,1)S(1)} %copy-done.69), channel_id=1, source_target_pairs={{0,6},{2,4},{4,2},{6,0},{1,7},{3,5},{5,3},{7,1},{8,14},{10,12},{12... | collective-permute-start | bytes 786440 | tf_op jit(solution)/shard_map/ppermute | solution.py:49
  237.0 28.9 %collective-permute-start.46 = (bf16[560,256]{1,0:T(8,128)(2,1)S(1)}, bf16[560,256]{1,0:T(8,128)(2,1)}, u32[]{:S(2)}, u32[]{:S(2)}) collective-permute-start(bf16[560,256]{1,0:T(8,128)(2,1)S(1)} %pad_maximum_fusion), channel_id=1, source_target_pairs={{0,8},{8,0},{1,9},{9,1},{2,10},{10,2},{3,11},{11,3},{4,12},{12,4},... | collective-permute-start | bytes 860168 | tf_op jit(solution)/shard_map/ppermute | solution.py:45
  240.1 40.3 %collective-permute-start.55 = (bf16[2,2,2,32,1152]{4,3,1,2,0:T(8,128)(2,1)S(1)}, bf16[2,2,2,32,1152]{4,3,1,2,0:T(8,128)(2,1)S(1)}, u32[]{:S(2)}, u32[]{:S(2)}) collective-permute-start(bf16[2,2,2,32,1152]{4,3,1,2,0:T(8,128)(2,1)S(1)} %bitcast.148), channel_id=1, source_target_pairs={{0,2},{2,0},{4,6},{6,4},{1,3},{3,1},{5,7},{7,5},{8,10},{10,8},{12,... | collective-permute-start | bytes 1769480 | tf_op jit(solution)/shard_map/ppermute | solution.py:49
  260.7 26.7 %collective-permute-start.45 = (bf16[256,1024]{1,0:T(8,128)(2,1)}, bf16[256,1024]{1,0:T(8,128)(2,1)S(1)}, u32[]{:S(2)}, u32[]{:S(2)}) collective-permute-start(bf16[256,1024]{1,0:T(8,128)(2,1)} %get-tuple-element.214), channel_id=1, source_target_pairs={{0,1},{1,0},{2,3},{3,2},{4,5},{5,4},{6,7},{7,6},{8,9},{9,8},{10,11... | collective-permute-start | bytes 1572872 | tf_op jit(solution)/shard_map/ppermute | solution.py:45
  260.9 18.5 %collective-permute-start.52 = (bf16[1,2,2,32,1152]{4,3,1,2,0:T(8,128)(2,1)}, bf16[1,2,2,32,1152]{4,3,1,2,0:T(8,128)(2,1)S(1)}, u32[]{:S(2)}, u32[]{:S(2)}) collective-permute-start(bf16[1,2,2,32,1152]{4,3,1,2,0:T(8,128)(2,1)} %constant_dynamic-slice_fusion.3), channel_id=1, source_target_pairs={{0,4},{2,6},{4,0},{6,2},{1,5},{3,7},{5,1},{7,3},{8,12},{10,14},{12... | collective-permute-start | bytes 884744 | tf_op jit(solution)/shard_map/ppermute | solution.py:49
  265.2 14.4 %collective-permute-start.59 = (bf16[144,1024]{1,0:T(8,128)(2,1)S(1)}, bf16[144,1024]{1,0:T(8,128)(2,1)S(1)}, u32[]{:S(2)}, u32[]{:S(2)}) collective-permute-start(bf16[144,1024]{1,0:T(8,128)(2,1)S(1)} %bitcast.151), channel_id=1, source_target_pairs={{0,0},{1,8},{2,2},{3,10},{4,4},{5,12},{6,6},{7,14},{8,16},{9,24},{... | collective-permute-start | bytes 884744 | tf_op jit(solution)/shard_map/ppermute | solution.py:773
  267.7 14.9 %collective-permute-start.47 = (bf16[272,768]{1,0:T(8,128)(2,1)S(1)}, bf16[272,768]{1,0:T(8,128)(2,1)S(1)}, u32[]{:S(2)}, u32[]{:S(2)}) collective-permute-start(bf16[272,768]{1,0:T(8,128)(2,1)S(1)} %maximum_maximum_fusion), channel_id=1, source_target_pairs={{0,16},{16,0},{1,17},{17,1},{2,18},{18,2},{3,19},{19,3},{4,20},{20... | collective-permute-start | bytes 1253384 | tf_op jit(solution)/shard_map/ppermute | solution.py:45
  280.6 27.5 %collective-permute-start.56 = (bf16[1,2,2,32,1152]{4,3,1,2,0:T(8,128)(2,1)S(1)}, bf16[1,2,2,32,1152]{4,3,1,2,0:T(8,128)(2,1)S(1)}, u32[]{:S(2)}, u32[]{:S(2)}) collective-permute-start(bf16[1,2,2,32,1152]{4,3,1,2,0:T(8,128)(2,1)S(1)} %constant_dynamic-slice_fusion), channel_id=1, source_target_pairs={{0,4},{2,6},{4,0},{6,2},{1,5},{3,7},{5,1},{7,3},{8,12},{10,14},{12... | collective-permute-start | bytes 884744 | tf_op jit(solution)/shard_map/ppermute | solution.py:49
  284.5 22.3 %collective-permute-start.49 = (bf16[80,768]{1,0:T(8,128)(2,1)S(1)}, bf16[80,768]{1,0:T(8,128)(2,1)S(1)}, u32[]{:S(2)}, u32[]{:S(2)}) collective-permute-start(bf16[80,768]{1,0:T(8,128)(2,1)S(1)} %get-tuple-element.254), channel_id=1, source_target_pairs={{0,4},{2,6},{4,0},{6,2},{1,5},{3,7},{5,1},{7,3},{8,12},{10,14},{12... | collective-permute-start | bytes 368648 | tf_op jit(solution)/shard_map/ppermute | solution.py:49
  284.6 22.2 %collective-permute-start.48 = (bf16[80,768]{1,0:T(8,128)(2,1)S(1)}, bf16[80,768]{1,0:T(8,128)(2,1)S(1)}, u32[]{:S(2)}, u32[]{:S(2)}) collective-permute-start(bf16[80,768]{1,0:T(8,128)(2,1)S(1)} %get-tuple-element.253), channel_id=1, source_target_pairs={{0,2},{2,0},{4,6},{6,4},{1,3},{3,1},{5,7},{7,5},{8,10},{10,8},{12,... | collective-permute-start | bytes 368648 | tf_op jit(solution)/shard_map/ppermute | solution.py:49
  287.4 19.8 %collective-permute-start.54 = (bf16[32,2304]{1,0:T(8,128)(2,1)S(1)}, bf16[32,2304]{1,0:T(8,128)(2,1)S(1)}, u32[]{:S(2)}, u32[]{:S(2)}) collective-permute-start(bf16[32,2304]{1,0:T(8,128)(2,1)S(1)} %fusion.11), channel_id=1, source_target_pairs={{0,8},{8,0},{1,9},{9,1},{2,10},{10,2},{3,11},{11,3},{4,12},{12,4},... | collective-permute-start | bytes 442376 | tf_op jit(solution)/shard_map/ppermute | solution.py:45
  (100 other events, 781.3 us)

commit v4 on v3

--- a/solution.py
+++ b/solution.py
@@ -82,14 +82,15 @@
         kept = pick(parts, bit, 1)
         if needed:
             sent = after(sent, *needed)
-        self.sent = sent
-        self.parts = kept + crossed(sent, self.step, self.count)
+        self.sent, self.kept = sent, kept
+        self.got = crossed(sent, self.step, self.count)
+        self.parts = kept + self.got
         self.step = self.step * 2
 
-    def finish(self):
+    def finish(self, *needed):
         while self.step < self.count:
             self.advance()
-        return self.parts[0]
+        return after(self.parts, *needed)[0] if needed else self.parts[0]
 
 
 def in_order(index, own, other, axis):
@@ -128,6 +129,9 @@
     return pl.BlockSpec((rows, cols), lambda i, ids: (0, ids[CORE]))
 
 
+IN_HBM = pl.BlockSpec(memory_space=pltpu.HBM)
+
+
 def shaped(*shape, dtype=BF16):
     return jax.ShapeDtypeStruct(shape, dtype)
 
@@ -141,10 +145,17 @@
         (lanes & 63) < 32, pltpu.roll(field, LANES - 32, 1), pltpu.roll(field, 32, 1))
 
 
+def low_sum(field, lanes):
+    return jnp.sum(jnp.where(lanes < 64, field, 0.0), axis=1, keepdims=True)
+
+
 def half_sums(field, lanes):
-    low = jnp.sum(jnp.where(lanes < 64, field, 0.0), axis=1, keepdims=True)
     high = jnp.sum(jnp.where(lanes < 64, 0.0, field), axis=1, keepdims=True)
-    return jnp.where(lanes < 64, low, high)
+    return jnp.where(lanes < 64, low_sum(field, lanes), high)
+
+
+def twice(row):
+    return jnp.concatenate([row, row], axis=1)
 
 
 def tables(ids, slots, first_row, rows, freq):
@@ -184,15 +195,17 @@
         unit = raw * lax.rsqrt(half_sums(raw * raw, lanes) * (1.0 / head_size) + EPSILON) * gain
         return unit * cosine + half_swap(unit, lanes) * sine
 
+    q_scale = twice(qg_ref[...]) * (math.log2(math.e) / math.sqrt(head_size))
+    k_scale = twice(kg_ref[...])
     q_raw = dot_nn(h, wq_ref[...])
     k_raw = dot_nn(h, wk_ref[...])
     v_raw = dot_nn(h, wv_ref[...])
     for head in range(heads):
         span = slice(head * LANES, (head + 1) * LANES)
-        packed[head, :, 0:LANES] = turned(q_raw[:, span], qg_ref[...]).astype(BF16)
+        packed[head, :, 0:LANES] = turned(q_raw[:, span], q_scale).astype(BF16)
     for pair in range(heads // 2):
         span = slice(pair * LANES, (pair + 1) * LANES)
-        keys = turned(k_raw[:, span], kg_ref[...])
+        keys = turned(k_raw[:, span], k_scale)
         values = v_raw[:, span]
         even = jnp.where(lanes < 64, keys, pltpu.roll(values, 64, 1))
         odd = jnp.where(lanes < 64, pltpu.roll(keys, 64, 1), values)
@@ -207,12 +220,12 @@
     rows, width = x_own.shape
     block = pl.BlockSpec((rows, 2 * LANES), lambda i, ids: (jnp.bitwise_xor(i, ids[CORE]), 0))
     part = whole((rows, width))
-    row = whole((1, LANES))
+    row, gains = whole((1, LANES)), whole((1, head_size))
     return run_kernel(
         functools.partial(project_kernel, head_size, slots), "project", ids,
         (x_own, x_other, gain, w_query, w_key, w_value, freq, qg, kg),
         [part, part, whole((1, width)), of_core(width, w_query.shape[1] // 2),
-         of_core(width, w_key.shape[1] // 2), of_core(width, w_value.shape[1] // 2), row, row, row],
+         of_core(width, w_key.shape[1] // 2), of_core(width, w_value.shape[1] // 2), row, gains, gains],
         [shaped(rows, width)] * 2 + [shaped(2 * rows, 2 * LANES)] * heads,
         [part, part] + [block] * heads,
         grid=(2,), scratch=[pltpu.VMEM((heads, rows, 2 * LANES), BF16)], vmem=58,
@@ -239,10 +252,14 @@
 
 
 def attend_kernel(slots, ids, *refs):
-    count = (len(refs) - 4) // 2
-    arrived, sent = refs[:count], refs[count : 2 * count]
-    wide_ref, qaug_ref, kaug_ref, vaug_ref = refs[2 * count :]
-    block = arrived[0].shape[0]
+    count = (len(refs) - 6) // 2
+    sources, sent = refs[:count], refs[count : 2 * count]
+    wide_ref, qaug_ref, kaug_ref, vaug_ref, arrived, arrivals = refs[2 * count :]
+    block = arrived.shape[1]
+    copies = [pltpu.make_async_copy(source, arrived.at[k], arrivals.at[k])
+              for k, source in enumerate(sources)]
+    for copy in copies:
+        copy.start()
     mark = 64 + slots
     lanes = lane_ids(block)
     plane = ids[PLANE]
@@ -260,8 +277,9 @@
             edge = stop
         segq = jnp.where(inside, 1.0, 0.0)
         segk = jnp.where(ones_lane, 1.0, jnp.where(slot_lane & jnp.logical_not(inside), -FAR, 0.0))
-        pair = arrived[step][:, 0:LANES].astype(F32)
-        keyval = arrived[step][:, LANES:].astype(F32)
+        copies[step].wait()
+        pair = arrived[step, :, 0:LANES].astype(F32)
+        keyval = arrived[step, :, LANES:].astype(F32)
         qaug_ref[0, span, :] = jnp.where(lanes < 64, pair, segq).astype(BF16)
         qaug_ref[1, span, :] = jnp.where(lanes < 64, pltpu.roll(pair, 64, 1), segq).astype(BF16)
         kaug_ref[span, :] = jnp.where(lanes < 64, keyval, segk).astype(BF16)
@@ -297,68 +315,77 @@
         shaped(rows, LANES)]
     return run_kernel(
         functools.partial(attend_kernel, slots), "attend", ids, arrived,
-        [whole(a.shape) for a in arrived], outs, [whole(o.shape) for o in outs], vmem=40,
+        [IN_HBM] * count, outs, [whole(o.shape) for o in outs],
+        scratch=[pltpu.VMEM((count, block, 2 * LANES), BF16), pltpu.SemaphoreType.DMA((count,))],
+        vmem=40,
         micros=9)
 
 
 def middle_kernel(count, ids, *refs):
-    own, other = refs[:count], refs[count : 2 * count]
-    xo_ref, xt_ref, w_ref, gain_ref, y_ref, ho_ref, ht_ref, o_ref = refs[2 * count :]
-    turn = pl.program_id(0)
-    for core, blocks in ((ids[CORE], own), (1 - ids[CORE], other)):
+    blocks = refs[: 2 * count]
+    xo_ref, xt_ref, w_ref, gain_ref, y_ref, ho_ref, ht_ref, o_ref, arrivals = refs[2 * count :]
+    rows = xo_ref.shape[0]
+    copies = []
+    for twin in range(2):
+        core = jnp.bitwise_xor(ids[CORE], twin)
         for step in range(count):
             head = core * count + jnp.bitwise_xor(ids[PLANE], step)
-            o_ref[:, pl.ds(pl.multiple_of(head * LANES, LANES), LANES)] = blocks[step][...]
-    y = jnp.where(turn == 0, xo_ref[...], xt_ref[...]).astype(F32)
-    y = y + dot_nn(o_ref[...], w_ref[...])
-    h = (y * lax.rsqrt(jnp.mean(y * y, axis=1, keepdims=True) + EPSILON) * gain_ref[...]).astype(
-        BF16)
-
-    @pl.when(turn == 0)
-    def _():
-        y_ref[...] = y
-        ho_ref[...] = h
-
-    @pl.when(turn == 1)
-    def _():
-        ht_ref[...] = h
+            span = pl.ds(pl.multiple_of(head * LANES, LANES), LANES)
+            for half in range(2):
+                spot = pl.multiple_of(jnp.bitwise_xor(ids[CORE], half) * rows, rows)
+                copies.append(pltpu.make_async_copy(
+                    blocks[twin * count + step].at[pl.ds(spot, rows), :],
+                    o_ref.at[half * rows : (half + 1) * rows, span],
+                    arrivals.at[len(copies)]))
+                copies[-1].start()
+    for copy in copies:
+        copy.wait()
+    for half, x_ref, h_ref in ((0, xo_ref, ho_ref), (1, xt_ref, ht_ref)):
+        y = x_ref[...].astype(F32) + dot_nn(o_ref[half * rows : (half + 1) * rows, :], w_ref[...])
+        if half == 0:
+            y_ref[...] = y
+        scale = lax.rsqrt(jnp.mean(y * y, axis=1, keepdims=True) + EPSILON)
+        h_ref[...] = (y * scale * gain_ref[...]).astype(BF16)
 
 
 def middle(ids, own, other, x_own, x_other, w_out, gain):
     rows, width = x_own.shape
     count = len(own)
-    block = pl.BlockSpec((rows, LANES), lambda i, ids: (jnp.bitwise_xor(i, ids[CORE]), 0))
     part = whole((rows, width))
     return run_kernel(
         functools.partial(middle_kernel, count), "middle", ids,
         (*own, *other, x_own, x_other, w_out, gain),
-        [block] * (2 * count) + [part, part, whole(w_out.shape), whole((1, width))],
+        [IN_HBM] * (2 * count) + [part, part, whole(w_out.shape), whole((1, width))],
         [shaped(rows, width, dtype=F32), shaped(rows, width), shaped(rows, width),
          shaped(2 * rows, width)],
-        [part, part, part, pl.BlockSpec((rows, width), lambda i, ids: (i, 0))],
-        grid=(2,), vmem=58, micros=4)
-
-
-def feed_kernel(ids, ho_ref, ht_ref, co_ref, ct_ref, wg_all, wu_all, wd_all, *refs):
+        [part, part, part, whole((2 * rows, width))],
+        scratch=[pltpu.SemaphoreType.DMA((4 * count,))], vmem=32, micros=4)
+
+
+def feed_kernel(ids, ho_all, ht_all, co_all, ct_all, wg_all, wu_all, wd_all, *refs):
     m_ref, dg_ref, du_ref, ha_ref, ca_ref, do_ref, dt_ref, yo_ref, yt_ref = refs[-13:-4]
     wg_ref, wu_ref, wd_ref, arrivals = refs[-4:]
-    rows = ho_ref.shape[0]
+    rows = ho_all.shape[0]
     units = wg_ref.shape[1]
     mine = pl.ds(pl.multiple_of((2 * ids[2] + ids[CORE]) * units, LANES), units)
     gates = pltpu.make_async_copy(wg_all.at[:, mine], wg_ref, arrivals.at[0])
     ups = pltpu.make_async_copy(wu_all.at[:, mine], wu_ref, arrivals.at[1])
     downs = pltpu.make_async_copy(wd_all.at[mine, :], wd_ref, arrivals.at[2])
-    gates.start()
-    ups.start()
-    downs.start()
-    ha_ref[0:rows, :] = ho_ref[...]
-    ha_ref[rows:, :] = ht_ref[...]
-    ca_ref[0:rows, :] = co_ref[...]
-    ca_ref[rows:, :] = ct_ref[...]
+    blocks = [
+        pltpu.make_async_copy(source, target.at[half * rows : (half + 1) * rows, :],
+                              arrivals.at[3 + k])
+        for k, (source, target, half) in enumerate((
+            (ho_all, ha_ref, 0), (ht_all, ha_ref, 1), (co_all, ca_ref, 0), (ct_all, ca_ref, 1)))]
+    for copy in (*blocks[:2], gates, ups, *blocks[2:], downs):
+        copy.start()
+    blocks[0].wait()
+    blocks[1].wait()
     gates.wait()
     gate = dot_nn(ha_ref[...], wg_ref[...])
     ups.wait()
     up = dot_nn(ha_ref[...], wu_ref[...])
+    blocks[2].wait()
+    blocks[3].wait()
     downs.wait()
     sig = jax.nn.sigmoid(gate)
     silu = gate * sig
@@ -383,11 +410,11 @@
     cols = [units] * 3 + [width] * 2
     return run_kernel(
         feed_kernel, "feed", ids, (h_own, h_other, c_own, c_other, w_gate, w_up, w_down, *earlier),
-        [part] * 4 + [anywhere] * (3 + len(earlier)),
+        [IN_HBM] * 4 + [anywhere] * (3 + len(earlier)),
         [shaped(4 * rows, n) for n in cols] + [shaped(rows, width)] * 4,
         [kept(n) for n in cols] + [part] * 4,
         scratch=[pltpu.VMEM((width, units), BF16)] * 2
-        + [pltpu.VMEM((units, width), BF16), pltpu.SemaphoreType.DMA((3,))],
+        + [pltpu.VMEM((units, width), BF16), pltpu.SemaphoreType.DMA((7,))],
         vmem=58, micros=12, aliases={8 + k: k for k in range(len(earlier))})
 
 
@@ -431,7 +458,7 @@
         [part, part, whole(w_out.shape)],
         [shaped(2 * rows, width // 2)] + [shaped(2 * rows, LANES)] * count,
         [pl.BlockSpec((rows, width // 2), lambda i, ids: (i, 0))] + [block] * count,
-        grid=(2,), vmem=58, micros=2)
+        grid=(2,), vmem=24, micros=2)
 
 
 def attend_back_kernel(ids, qaug_ref, kaug_ref, vaug_ref, wide_ref, *refs):
@@ -509,14 +536,15 @@
         wk_ref[...].astype(F32), wv_ref[...].astype(F32), odd, lane_ids(width)).astype(BF16)
     wq = wq_ref[...]
 
-    def undo(raw, grad, gain, cosine, sine):
-        scale = lax.rsqrt(half_sums(raw * raw, lanes) * (1.0 / head_size) + EPSILON)
+    def undo(raw, grad, gain, cosine, sine, sums):
+        scale = lax.rsqrt(sums(raw * raw, lanes) * (1.0 / head_size) + EPSILON)
         unit = raw * scale
         back = grad * cosine - half_swap(grad, lanes) * sine
         scaled = back * gain
-        mean = half_sums(scaled * unit, lanes) * (1.0 / head_size)
+        mean = sums(scaled * unit, lanes) * (1.0 / head_size)
         return scale * (scaled - unit * mean), jnp.sum(back * unit, axis=0, keepdims=True)
 
+    q_scale, k_scale = twice(qg_ref[...]), twice(kg_ref[...])
     q_gain = jnp.zeros((1, LANES), F32)
     k_gain = jnp.zeros((1, LANES), F32)
     for step in range(count):
@@ -528,9 +556,10 @@
             span = pl.ds(first, rows)
             cosine, sine = cos_ref[span, :], sin_ref[span, :]
             dkv = dkv_ref[span, :]
-            dqr, add_q = undo(dot_nn(h, wq), dq_ref[span, :], qg_ref[...], cosine, sine)
+            dqr, add_q = undo(
+                dot_nn(h, wq), dq_ref[span, :], q_scale, cosine, sine, half_sums)
             dkr, add_k = undo(
-                dot_nn(h, wkv), jnp.where(lanes < 64, dkv, 0.0), kg_ref[...], cosine, sine)
+                dot_nn(h, wkv), jnp.where(lanes < 64, dkv, 0.0), k_scale, cosine, sine, low_sum)
             q_gain = q_gain + add_q
             k_gain = k_gain + add_k
             dqr = dqr.astype(BF16)
@@ -554,7 +583,7 @@
     count = len(blocks) // 2
     head = lambda ids: ids[CORE] * heads + ids[PLANE]
     pair = pl.BlockSpec((width, LANES), lambda i, ids: (0, head(ids) // 2))
-    row = whole((1, LANES))
+    row = whole((1, head_size))
     outs = [shaped(2 * rows, 2 * LANES)] * count + [
         shaped(width, 2 * LANES), shaped(1, width, dtype=F32), shaped(8, LANES, dtype=F32)]
     return run_kernel(
@@ -564,7 +593,7 @@
         + [pl.BlockSpec((width, LANES), lambda i, ids: (0, head(ids))), pair, pair,
            whole(cosine.shape), whole(sine.shape), row, row, whole(dq.shape), whole(dkv.shape)],
         outs, [whole(o.shape) for o in outs],
-        scratch=[pltpu.VMEM((2 * LANES, width), F32)], vmem=58, micros=7)
+        scratch=[pltpu.VMEM((2 * LANES, width), F32)], vmem=40, micros=7)
 
 
 def back_kernel(ids, *refs):
@@ -593,7 +622,7 @@
         back_kernel, "to_tokens", ids, (*arrived, w_query, w_key, w_value),
         [whole(a.shape) for a in arrived]
         + [of_core(width, w.shape[1] // 2) for w in (w_query, w_key, w_value)],
-        [shaped(rows, width)] * 2, [whole((rows, width))] * 2, vmem=58, micros=4)
+        [shaped(rows, width)] * 2, [whole((rows, width))] * 2, vmem=24, micros=4)
 
 
 def last_kernel(ids, mine_ref, twin_ref, x_ref, dy_ref, gain_ref, out_ref):
@@ -657,15 +686,13 @@
     lane = np.arange(LANES)
     freq = jnp.asarray(
         (ROPE_BASE ** (-2.0 * (lane % (head_size // 2)) / head_size)).astype(np.float32))[None, :]
-    to_exp2 = math.log2(math.e) / math.sqrt(head_size)
-    qg = jnp.tile(query_gain, 2)[None, :]
-    kg = jnp.tile(key_gain, 2)[None, :]
+    qg, kg = query_gain[None, :], key_gain[None, :]
     a_gain, f_gain = attn_gain[None, :], ffn_gain[None, :]
     steps = range(1, n_z)
 
     x_other = swap(tokens, "c")
     h_own, h_other, *packed = project(
-        ids, tokens, x_other, a_gain, w_query, w_key, w_value, freq, qg * to_exp2, kg, head_size,
+        ids, tokens, x_other, a_gain, w_query, w_key, w_value, freq, qg, kg, head_size,
         slots, heads)
     arrived = [packed[0]] + [crossed(packed[s], s, n_z) for s in steps]
 
@@ -747,40 +774,18 @@
         ids, qaug, kaug, vaug, wide, after(do_arrived, *blocks[3::2]))
     mixed = (y_mine + (y_near + after(y_home, dq).astype(F32))).astype(BF16)
 
-    out_parts = out_parts.finish(dq)
     gate = Halving(jnp.moveaxis(gate.finish(dq), 1, 0), i_z)
     down.advance(dq)
     gate.advance()
     *back, grad_head, gain_attn, gains = unturn(
         ids, blocks, w_query, w_key, w_value, cosine, sine, qg, kg,
-        after(dq, down.sent, gate.sent, out_parts, mixed), dkv, head_size, heads)
+        after(dq, down.sent, gate.sent, mixed), dkv, head_size, heads)
     up = Halving(jnp.moveaxis(up.finish(back[0]), 1, 0), i_z)
     back = after(back, down.parts, gate.parts, up.parts)
     back_arrived = [back[0]] + [crossed(back[s], s, n_z) for s in steps]
     late = tuple(back_arrived[1:])
+    gain_attn, gains = after((gain_attn, gains), back_arrived[1])
     up.advance()
-    dh_own, dh_other = to_tokens(ids, back_arrived, w_query, w_key, w_value)
-    gate.advance(back_arrived[1])
-    grad_tokens = last(ids, dh_own, swap(dh_other, "c"), tokens, dy, a_gain)
-
-    owners = []
-    for y in range(n_y):
-        for x in range(2):
-            for z in range(n_z):
-                for c in range(2):
-                    source = ((y * 2 + x) * n_z + z) * 2 + c
-                    owners.append((source, n_y * n_z * (2 * x + c) + z * n_y + y))
-    share_down = lax.ppermute(after(down.finish(), *late), ALL, owners).astype(F32)
-
-    def spread(parts):
-        got = swap(pick(parts, 1 - i_c, 1), "c")
-        cols = in_order(i_c, pick(parts, i_c, 1), got, 2)
-        got = swap(pick(cols, 1 - i_x), "x")
-        return in_order(i_x, pick(cols, i_x), got, 1).astype(F32)
-
-    share_gate = spread(gate.finish())
-    share_up = spread(up.finish())
-
     half = width // 2
     sums = jnp.concatenate(
         [gain_attn / a_gain, gain_ffn, gains[0:1, :head_size] + gains[0:1, head_size:],
@@ -794,9 +799,12 @@
     got = swap(jnp.concatenate([pick(parts, 1 - i_x), *split_up(sums)], axis=0), "x")
     count = kept_x.shape[0]
     sums = sums + sum(got[count + k * depth :][:depth].astype(F32) for k in range(3))
-    parts = jnp.concatenate([out_parts.reshape(-1, half), kept_x + got[:count]], axis=1)
+    parts = jnp.concatenate(
+        [out_parts.finish(back[0]).reshape(-1, half), kept_x + got[:count]], axis=1)
     parts = parts.reshape(n_y, n_z * 2 * row_block, half + 2 * LANES)
 
+    dh_own, dh_other = to_tokens(ids, after(back_arrived, parts), w_query, w_key, w_value)
+    gate.advance(back_arrived[1])
     def joined(rows_sent, vector):
         beside = jnp.concatenate(split_up(vector), axis=1)
         wider = rows_sent.shape[1] - beside.shape[1]
@@ -813,6 +821,29 @@
     else:
         parts = lax.psum_scatter(parts, "y", scatter_dimension=0, tiled=False)
         sums = lax.psum(sums, "y")
+    up.advance()
+    grad_tokens = last(
+        ids, dh_own, after(swap(dh_other, "c"), parts, up.sent), tokens, dy, a_gain)
+
+    owners = []
+    for y in range(n_y):
+        for x in range(2):
+            for z in range(n_z):
+                for c in range(2):
+                    source = ((y * 2 + x) * n_z + z) * 2 + c
+                    owners.append((source, n_y * n_z * (2 * x + c) + z * n_y + y))
+    share_down = lax.ppermute(after(down.finish(), *late), ALL, owners)
+    share_down = after(share_down, grad_tokens, up.sent).astype(F32)
+
+    def spread(parts):
+        got = swap(pick(parts, 1 - i_c, 1), "c")
+        cols = in_order(i_c, pick(parts, i_c, 1), got, 2)
+        got = swap(pick(cols, 1 - i_x), "x")
+        return in_order(i_x, pick(cols, i_x), got, 1).astype(F32)
+
+    share_gate = spread(gate.finish(grad_tokens))
+    share_up = spread(up.finish())
+
     parts = parts.reshape(n_z, 2 * row_block, half + 2 * LANES)
     kept_z, sums_z = pick(parts, i_z), sums
     out_sum, by_step = kept_z[:, :half].astype(F32), [kept_z[:, half:]]

time: 322 us -> 299 us (0.929)
  Pallas kernels: 93.6 us -> 79.4 us
  local copies, waits for them, and re-layouts: 24.4 us -> 18.9 us
  starting transfers between devices: 71.8 us -> 75.8 us
    pallas_call x12, Pallas kernels: 93.6 us -> 79.4 us  [run_kernel(): pl.pallas_call(kernel, grid_spec=pltpu.PrefetchScalarGridSpec(num_scalar_...]
    ppermute x32, waiting for transfers between devices: 15.8 us -> 5.72 us  [swap(): return lax.ppermute(field, axis_name, [(0, 1), (1, 0)])]
    ppermute x21, waiting for transfers between devices: 67.7 us -> 75.4 us  [crossed(): return lax.ppermute(field, 'z', [(k, k ^ step) for k in range(count)])]
    unnamed x151 -> x135, local copies, waits for them, and re-layouts: 14.3 us -> 9.76 us
  transfers between devices with their start and end apart: 60 -> 60, of which waited for: 15 -> 20; matrix products, arithmetic and copies ran while one was open for 16% -> 15% of each run, Pallas kernels for 24% -> 21%
where the time goes in v4:
time: 299 us; the launch traced here: 296 us
  waiting for transfers between devices  81.2 us (27%)
  Pallas kernels  79.4 us (27%)
  starting transfers between devices  75.8 us (25%)
  other arithmetic  24 us (8%)
  local copies, waits for them, and re-layouts  18.9 us (6%)
  matrix products  12.1 us (4%)
  between operations  4.1 us (1%)
    pallas_call x12, Pallas kernels, run_kernel(): pl.pallas_call(kernel, grid_spec=pltpu.PrefetchScalarGridSpec(num_scalar_...  79.4 us
    ppermute x21, waiting for transfers between devices, crossed(): return lax.ppermute(field, 'z', [(k, k ^ step) for k in range(count)])  75.4 us
    ppermute x21, starting transfers between devices, crossed(): return lax.ppermute(field, 'z', [(k, k ^ step) for k in range(count)])  37.1 us
    ppermute x32, starting transfers between devices, swap(): return lax.ppermute(field, axis_name, [(0, 1), (1, 0)])  19.1 us
    ppermute x3, starting transfers between devices, along(): lax.ppermute(to_right, 'z', [(k, k + 1) for k in pairs])  14.6 us
    dot_general x4, matrix products, dot_tn(): lax.dot_general(left, right, (((0,), (0,)), ((), ())), preferred_element_...  12.1 us
    unnamed x135, local copies, waits for them, and re-layouts  9.76 us
    squeeze x13, local copies, waits for them, and re-layouts, pick(): return lax.dynamic_index_in_dim(field, index, axis, keepdims=False)  6.2 us
  transfers between devices with their start and end apart: 60, of which 20 were waited for; matrix products, arithmetic and copies ran while one was open for 15% of the time, Pallas kernels for 21%

profile of v4, /device:TPU:0, one launch (start us, length us, event | category | flops | bytes accessed | tf_op | source)
XLA Modules:
  0.0 295.5 jit_solution(8822244854490876581)
XLA Ops:
  3.7 8.1 %project.1 = (bf16[256,1024]{1,0:T(8,128)(2,1)}, bf16[256,1024]{1,0:T(8,128)(2,1)}, bf16[512,256]{1,0:T(8,128)(2,1)}, bf16[512,256]{1,0:T(8,128)(2,1)}, bf16[512...) custom-call(s32[8]{0:T(128)} %concatenate.58.ids, bf16[256,1024]{1,0:T(8,128)(2,1)} %x_ref.1, bf16[256,1024]{1,0:T(8,128)(2,1)} %copy-done.13, ...), custom_call_target="tpu_custom_call" | custom-call | flops 500000 | bytes 1024 | tf_op jit(solution)/shard_map/project/pallas_call | solution.py:110
  11.8 3.0 %collective-permute-start.1 = (bf16[512,256]{1,0:T(8,128)(2,1)}, bf16[512,256]{1,0:T(8,128)(2,1)S(1)}, u32[]{:S(2)}, u32[]{:S(2)}) collective-permute-start(bf16[512,256]{1,0:T(8,128)(2,1)} %get-tuple-element.130), channel_id=1, source_target_pairs={{0,2},{2,0},{4,6},{6,4},{1,3},{3,1},{5,7},{7,5},{8,10},{10,8},{12,... | collective-permute-start | bytes 786440 | tf_op jit(solution)/shard_map/ppermute | solution.py:49
  14.8 2.6 collective-permute-start.2
  17.4 9.2 %collective-permute-done.1.refs_1_ = bf16[512,256]{1,0:T(8,128)(2,1)S(1)} collective-permute-done((bf16[512,256]{1,0:T(8,128)(2,1)}, bf16[512,256]{1,0:T(8,128)(2,1)S(1)}, u32[]{:S(2)}, u32[]{:S(2)}) %collective-permute-start.1) | collective-permute-done | bytes 262176 | tf_op jit(solution)/shard_map/ppermute | solution.py:49
  29.9 5.6 %fusion = (f32[2048,128]{1,0:T(8,128)}, f32[2048,128]{1,0:T(8,128)}) fusion(f32[128]{0:T(128)S(1)} %copy-done.62, f32[128]{0:T(128)S(1)} %copy-done.63, f32[2048]{0:T(1024)S(1)} %subtract_convert_fusion.4), kind=kLoop, calls=%fused_computation.15 | loop fusion | flops 524288 | bytes 2106368 | tf_op jit(solution)/shard_map/mul | solution.py:708
  37.4 10.0 %attend.1 = (bf16[512,128]{1,0:T(8,128)(2,1)S(1)}, bf16[512,128]{1,0:T(8,128)(2,1)S(1)}, bf16[512,128]{1,0:T(8,128)(2,1)S(1)}, bf16[512,128]{1,0:T(8,128)(2,1)S(...) custom-call(s32[8]{0:T(128)S(1)} %copy-done.34, ...), custom_call_target="tpu_custom_call" | custom-call | flops 900000 | bytes 1024 | tf_op jit(solution)/shard_map/attend/pallas_call | solution.py:110
  47.5 5.2 %collective-permute-start.4 = (bf16[512,128]{1,0:T(8,128)(2,1)S(1)}, bf16[512,128]{1,0:T(8,128)(2,1)S(1)}, u32[]{:S(2)}, u32[]{:S(2)}) collective-permute-start(bf16[512,128]{1,0:T(8,128)(2,1)S(1)} %get-tuple-element.139), channel_id=1, source_target_pairs={{0,2},{2,0},{4,6},{6,4},{1,3},{3,1},{5,7},{7,5},{8,10},{10,8},{12,... | collective-permute-start | bytes 393224 | tf_op jit(solution)/shard_map/ppermute | solution.py:49
  56.9 7.9 %collective-permute-done.5.refs_2_ = bf16[512,128]{1,0:T(8,128)(2,1)S(1)} collective-permute-done((bf16[512,128]{1,0:T(8,128)(2,1)S(1)}, bf16[512,128]{1,0:T(8,128)(2,1)S(1)}, u32[]{:S(2)}, u32[]{:S(2)}) %collective-permute-start.5) | collective-permute-done | bytes 131104 | tf_op jit(solution)/shard_map/ppermute | solution.py:49
  68.4 2.5 middle.1
  73.6 4.7 %collective-permute-start.13 = (bf16[256,1024]{1,0:T(8,128)(2,1)S(1)}, bf16[256,1024]{1,0:T(8,128)(2,1)}, u32[]{:S(2)}, u32[]{:S(2)}) collective-permute-start(bf16[256,1024]{1,0:T(8,128)(2,1)S(1)} %copy-done.23), channel_id=1, source_target_pairs={{0,2},{2,4},{4,6},{1,3},{3,5},{5,7},{8,10},{10,12},{12,14},{9,11},... | collective-permute-start | bytes 1572872 | tf_op jit(solution)/shard_map/ppermute | solution.py:54
  80.5 13.2 %feed.2 = (bf16[1024,1152]{1,0:T(8,128)(2,1)}, bf16[1024,1152]{1,0:T(8,128)(2,1)}, bf16[1024,1152]{1,0:T(8,128)(2,1)}, bf16[1024,1024]{1,0:T(8,128)(2,1)}, bf16[...) custom-call(s32[8]{0:T(128)} %concatenate.58.ids, ...), custom_call_target="tpu_custom_call" | custom-call | flops 1200000 | bytes 1024 | tf_op jit(solution)/shard_map/feed/pallas_call | solution.py:110
  94.5 5.3 %collective-permute-start.19 = (bf16[256,1024]{1,0:T(8,128)(2,1)}, bf16[256,1024]{1,0:T(8,128)(2,1)}, u32[]{:S(2)}, u32[]{:S(2)}) collective-permute-start(bf16[256,1024]{1,0:T(8,128)(2,1)} %collective-permute-done.13), channel_id=1, source_target_pairs={{0,2},{2,4},{4,6},{1,3},{3,5},{5,7},{8,10},{10,12},{12,14},{9,11},... | collective-permute-start | bytes 1572872 | tf_op jit(solution)/shard_map/ppermute | solution.py:54
  102.1 13.1 %feed.3 = (bf16[1024,1152]{1,0:T(8,128)(2,1)}, bf16[1024,1152]{1,0:T(8,128)(2,1)}, bf16[1024,1152]{1,0:T(8,128)(2,1)}, bf16[1024,1024]{1,0:T(8,128)(2,1)}, bf16[...) custom-call(s32[8]{0:T(128)} %concatenate.58.ids, ...), custom_call_target="tpu_custom_call", output_to_operand_aliasing={{0}: (8, {}), {1}: (9, {}), {2}: (10, {}), {3}: (11, {}), {... | custom-call | flops 1200000 | bytes 1024 | tf_op jit(solution)/shard_map/feed/pallas_call | solution.py:110
  115.2 4.9 %convolution_convert_fusion.2 = bf16[1152,1024]{1,0:T(8,128)(2,1)S(1)} fusion(bf16[1024,1152]{1,0:T(8,128)(2,1)} %get-tuple-element.165, bf16[1024,1024]{1,0:T(8,128)(2,1)} %get-tuple-element.166), kind=kOutput, calls=%fused_computation.2 | convolution fusion | flops 2417098752 | bytes 6815744 | tf_op jit(solution)/shard_map/dot_general | solution.py:33
  124.8 4.6 %collective-permute-start.25 = (bf16[256,1024]{1,0:T(8,128)(2,1)}, bf16[256,1024]{1,0:T(8,128)(2,1)S(1)}, u32[]{:S(2)}, u32[]{:S(2)}) collective-permute-start(bf16[256,1024]{1,0:T(8,128)(2,1)} %collective-permute-done.19), channel_id=1, source_target_pairs={{0,2},{2,4},{4,6},{1,3},{3,5},{5,7},{8,10},{10,12},{12,14},{9,11},... | collective-permute-start | bytes 1572872 | tf_op jit(solution)/shard_map/ppermute | solution.py:54
  136.5 3.2 %convolution_convert_fusion.1 = bf16[1024,1152]{1,0:T(8,128)(2,1)S(1)} fusion(bf16[1024,1024]{1,0:T(8,128)(2,1)S(1)} %copy-done.50, bf16[1024,1152]{1,0:T(8,128)(2,1)S(1)} %copy-done.43), kind=kOutput, calls=%fused_computation.1 | convolution fusion | flops 2417098752 | bytes 6815744 | tf_op jit(solution)/shard_map/dot_general | solution.py:33
  141.9 3.2 %convolution_convert_fusion = bf16[1024,1152]{1,0:T(8,128)(2,1)S(1)} fusion(bf16[1024,1024]{1,0:T(8,128)(2,1)S(1)} %copy-done.50, bf16[1024,1152]{1,0:T(8,128)(2,1)S(1)} %copy-done.44), kind=kOutput, calls=%fused_computation | convolution fusion | flops 2417098752 | bytes 6815744 | tf_op jit(solution)/shard_map/dot_general | solution.py:33
  152.1 2.5 to_heads.1
  154.6 2.4 collective-permute-start.30
  161.6 7.9 %collective-permute-done.31.refs_2_ = bf16[512,128]{1,0:T(8,128)(2,1)S(1)} collective-permute-done((bf16[512,128]{1,0:T(8,128)(2,1)S(1)}, bf16[512,128]{1,0:T(8,128)(2,1)S(1)}, u32[]{:S(2)}, u32[]{:S(2)}) %collective-permute-start.31) | collective-permute-done | bytes 131104 | tf_op jit(solution)/shard_map/ppermute | solution.py:49
  174.4 13.5 %attend_back.1 = (f32[2048,128]{1,0:T(8,128)S(1)}, f32[2048,128]{1,0:T(8,128)S(1)}) custom-call(s32[8]{0:T(128)S(1)} %copy-done.35, bf16[2,2048,128]{2,1,0:T(8,128)(2,1)S(1)} %copy-done.20, bf16[2048,128]{1,0:T(8,128)(2,1)S(1)} %copy-done.27, bf16[2048,128]{1,0:T(8,128)(2,1)S(1)} %copy-done.29, f32[2048,128]{1,0:T(8,128)S(1)} %copy-done.18, ...), custom_call_target="tpu_custom_call" | custom-call | flops 1300000 | bytes 1024 | tf_op jit(solution)/shard_map/attend_back/pallas_call | solution.py:110
  194.9 7.7 %unturn.1 = (bf16[512,256]{1,0:T(8,128)(2,1)S(1)}, bf16[512,256]{1,0:T(8,128)(2,1)S(1)}, bf16[512,256]{1,0:T(8,128)(2,1)}, bf16[512,256]{1,0:T(8,128)(2,1)}, bf1...) custom-call(s32[8]{0:T(128)S(1)} %copy-done.35, bf16[256,1024]{1,0:T(8,128)(2,1)S(1)} %copy-done.24, ...), custom_call_target="tpu_custom_call" | custom-call | flops 700000 | bytes 1024 | tf_op jit(solution)/shard_map/unturn/pallas_call | solution.py:110
  202.6 7.5 %collective-permute-done.38 = bf16[1,144,1024]{2,1,0:T(8,128)(2,1)S(1)} collective-permute-done((bf16[1,144,1024]{2,1,0:T(8,128)(2,1)S(1)}, bf16[1,144,1024]{2,1,0:T(8,128)(2,1)S(1)}, u32[]{:S(2)}, u32[]{:S(2)}) %collective-permute-start.38) | collective-permute-done | bytes 294944 | tf_op jit(solution)/shard_map/ppermute | solution.py:49
  218.3 5.3 %collective-permute-done.41.refs_1_ = bf16[512,256]{1,0:T(8,128)(2,1)S(1)} collective-permute-done((bf16[512,256]{1,0:T(8,128)(2,1)S(1)}, bf16[512,256]{1,0:T(8,128)(2,1)S(1)}, u32[]{:S(2)}, u32[]{:S(2)}) %collective-permute-start.41) | collective-permute-done | bytes 262176 | tf_op jit(solution)/shard_map/ppermute | solution.py:49
  229.0 5.9 %collective-permute-done.42.refs_2_ = bf16[512,256]{1,0:T(8,128)(2,1)} collective-permute-done((bf16[512,256]{1,0:T(8,128)(2,1)}, bf16[512,256]{1,0:T(8,128)(2,1)}, u32[]{:S(2)}, u32[]{:S(2)}) %collective-permute-start.42) | collective-permute-done | bytes 262176 | tf_op jit(solution)/shard_map/ppermute | solution.py:49
  234.9 4.1 %to_tokens.1 = (bf16[256,1024]{1,0:T(8,128)(2,1)S(1)}, bf16[256,1024]{1,0:T(8,128)(2,1)S(1)}) custom-call(s32[8]{0:T(128)S(1)} %copy-done.35, bf16[512,256]{1,0:T(8,128)(2,1)S(1)} %get-tuple-element.229.refs_0_, bf16[512,256]{1,0:T(8,128)(2,1)S(1)} %copy-done.33, bf16[512,256]{1,0:T(8,128)(2,1)} %collective-permute-done.42.refs_2_, ...), custom_call_target="tpu_custom_call" | custom-call | flops 400000 | bytes 1024 | tf_op jit(solution)/shard_map/to_tokens/pallas_call | solution.py:110
  239.1 5.5 %collective-permute-start.53 = (bf16[1,2,2,32,1152]{4,3,1,2,0:T(8,128)(2,1)S(1)}, bf16[1,2,2,32,1152]{4,3,1,2,0:T(8,128)(2,1)S(1)}, u32[]{:S(2)}, u32[]{:S(2)}) collective-permute-start(bf16[1,2,2,32,1152]{4,3,1,2,0:T(8,128)(2,1)S(1)} %copy-done.60), channel_id=1, source_target_pairs={{0,4},{2,6},{4,0},{6,2},{1,5},{3,7},{5,1},{7,3},{8,12},{10,14},{12... | collective-permute-start | bytes 884744 | tf_op jit(solution)/shard_map/ppermute | solution.py:49
  245.7 3.1 %collective-permute-start.47 = (bf16[272,768]{1,0:T(8,128)(2,1)S(1)}, bf16[272,768]{1,0:T(8,128)(2,1)S(1)}, u32[]{:S(2)}, u32[]{:S(2)}) collective-permute-start(bf16[272,768]{1,0:T(8,128)(2,1)S(1)} %maximum_maximum_fusion), channel_id=1, source_target_pairs={{0,16},{16,0},{1,17},{17,1},{2,18},{18,2},{3,19},{19,3},{4,20},{20... | collective-permute-start | bytes 1253384 | tf_op jit(solution)/shard_map/ppermute | solution.py:45
  249.3 15.9 %collective-permute-done.53 = bf16[1,2,2,32,1152]{4,3,1,2,0:T(8,128)(2,1)S(1)} collective-permute-done((bf16[1,2,2,32,1152]{4,3,1,2,0:T(8,128)(2,1)S(1)}, bf16[1,2,2,32,1152]{4,3,1,2,0:T(8,128)(2,1)S(1)}, u32[]{:S(2)}, u32[]{:S(2)}) %collective-permute-start.53) | collective-permute-done | bytes 294944 | tf_op jit(solution)/shard_map/ppermute | solution.py:49
  265.2 6.0 %collective-permute-done.56 = bf16[1,2,2,32,1152]{4,3,1,2,0:T(8,128)(2,1)S(1)} collective-permute-done((bf16[1,2,2,32,1152]{4,3,1,2,0:T(8,128)(2,1)S(1)}, bf16[1,2,2,32,1152]{4,3,1,2,0:T(8,128)(2,1)S(1)}, u32[]{:S(2)}, u32[]{:S(2)}) %collective-permute-start.56) | collective-permute-done | bytes 294944 | tf_op jit(solution)/shard_map/ppermute | solution.py:49
  273.0 3.1 %collective-permute-start.49 = (bf16[80,768]{1,0:T(8,128)(2,1)S(1)}, bf16[80,768]{1,0:T(8,128)(2,1)S(1)}, u32[]{:S(2)}, u32[]{:S(2)}) collective-permute-start(bf16[80,768]{1,0:T(8,128)(2,1)S(1)} %get-tuple-element.271), channel_id=1, source_target_pairs={{0,2},{2,0},{4,6},{6,4},{1,3},{3,1},{5,7},{7,5},{8,10},{10,8},{12,... | collective-permute-start | bytes 368648 | tf_op jit(solution)/shard_map/ppermute | solution.py:49
  279.8 4.8 %collective-permute-done.50 = bf16[80,768]{1,0:T(8,128)(2,1)S(1)} collective-permute-done((bf16[80,768]{1,0:T(8,128)(2,1)S(1)}, bf16[80,768]{1,0:T(8,128)(2,1)S(1)}, u32[]{:S(2)}, u32[]{:S(2)}) %collective-permute-start.50) | collective-permute-done | bytes 122912 | tf_op jit(solution)/shard_map/ppermute | solution.py:49
  (315 shorter events, 89.9 us)
Async XLA Ops:
  11.8 14.8 %collective-permute-start.1 = (bf16[512,256]{1,0:T(8,128)(2,1)}, bf16[512,256]{1,0:T(8,128)(2,1)S(1)}, u32[]{:S(2)}, u32[]{:S(2)}) collective-permute-start(bf16[512,256]{1,0:T(8,128)(2,1)} %get-tuple-element.130), channel_id=1, source_target_pairs={{0,2},{2,0},{4,6},{6,4},{1,3},{3,1},{5,7},{7,5},{8,10},{10,8},{12,... | collective-permute-start | bytes 786440 | tf_op jit(solution)/shard_map/ppermute | solution.py:49
  14.8 21.6 %collective-permute-start.2 = (bf16[512,256]{1,0:T(8,128)(2,1)}, bf16[512,256]{1,0:T(8,128)(2,1)}, u32[]{:S(2)}, u32[]{:S(2)}) collective-permute-start(bf16[512,256]{1,0:T(8,128)(2,1)} %get-tuple-element.131), channel_id=1, source_target_pairs={{0,4},{2,6},{4,0},{6,2},{1,5},{3,7},{5,1},{7,3},{8,12},{10,14},{12... | collective-permute-start | bytes 786440 | tf_op jit(solution)/shard_map/ppermute | solution.py:49
  17.4 19.1 %collective-permute-start.3 = (bf16[512,256]{1,0:T(8,128)(2,1)}, bf16[512,256]{1,0:T(8,128)(2,1)}, u32[]{:S(2)}, u32[]{:S(2)}) collective-permute-start(bf16[512,256]{1,0:T(8,128)(2,1)} %get-tuple-element.132), channel_id=1, source_target_pairs={{0,6},{2,4},{4,2},{6,0},{1,7},{3,5},{5,3},{7,1},{8,14},{10,12},{12... | collective-permute-start | bytes 786440 | tf_op jit(solution)/shard_map/ppermute | solution.py:49
  65.3 14.4 %collective-permute-start.11 = (bf16[256,1024]{1,0:T(8,128)(2,1)S(1)}, bf16[256,1024]{1,0:T(8,128)(2,1)S(1)}, u32[]{:S(2)}, u32[]{:S(2)}) collective-permute-start(bf16[256,1024]{1,0:T(8,128)(2,1)S(1)} %copy-done.11), channel_id=1, source_target_pairs={{0,1},{1,0},{2,3},{3,2},{4,5},{5,4},{6,7},{7,6},{8,9},{9,8},{10,11... | collective-permute-start | bytes 1572872 | tf_op jit(solution)/shard_map/ppermute | solution.py:45
  65.8 28.0 %collective-permute-start.17 = (bf16[256,1024]{1,0:T(8,128)(2,1)S(1)}, bf16[256,1024]{1,0:T(8,128)(2,1)}, u32[]{:S(2)}, u32[]{:S(2)}) collective-permute-start(bf16[256,1024]{1,0:T(8,128)(2,1)S(1)} %copy-done.11), channel_id=1, source_target_pairs={{0,8},{8,0},{1,9},{9,1},{2,10},{10,2},{3,11},{11,3},{4,12},{12,4},... | collective-permute-start | bytes 1572872 | tf_op jit(solution)/shard_map/ppermute | solution.py:45
  72.8 21.6 %collective-permute-start.12 = (bf16[256,1024]{1,0:T(8,128)(2,1)S(1)}, bf16[256,1024]{1,0:T(8,128)(2,1)}, u32[]{:S(2)}, u32[]{:S(2)}) collective-permute-start(bf16[256,1024]{1,0:T(8,128)(2,1)S(1)} %get-tuple-element.146.ho_all), channel_id=1, source_target_pairs={{0,8},{8,0},{1,9},{9,1},{2,10},{10,2},{3,11},{11,3},{4,12},{12,4},... | collective-permute-start | bytes 1572872 | tf_op jit(solution)/shard_map/ppermute | solution.py:45
  73.6 20.8 %collective-permute-start.13 = (bf16[256,1024]{1,0:T(8,128)(2,1)S(1)}, bf16[256,1024]{1,0:T(8,128)(2,1)}, u32[]{:S(2)}, u32[]{:S(2)}) collective-permute-start(bf16[256,1024]{1,0:T(8,128)(2,1)S(1)} %copy-done.23), channel_id=1, source_target_pairs={{0,2},{2,4},{4,6},{1,3},{3,5},{5,7},{8,10},{10,12},{12,14},{9,11},... | collective-permute-start | bytes 1572872 | tf_op jit(solution)/shard_map/ppermute | solution.py:54
  78.3 16.1 %collective-permute-start.14 = (bf16[256,1024]{1,0:T(8,128)(2,1)S(1)}, bf16[256,1024]{1,0:T(8,128)(2,1)}, u32[]{:S(2)}, u32[]{:S(2)}) collective-permute-start(bf16[256,1024]{1,0:T(8,128)(2,1)S(1)} %copy-done.23), channel_id=1, source_target_pairs={{2,0},{4,2},{6,4},{3,1},{5,3},{7,5},{10,8},{12,10},{14,12},{11,9},... | collective-permute-start | bytes 1572872 | tf_op jit(solution)/shard_map/ppermute | solution.py:55
  94.5 28.3 %collective-permute-start.19 = (bf16[256,1024]{1,0:T(8,128)(2,1)}, bf16[256,1024]{1,0:T(8,128)(2,1)}, u32[]{:S(2)}, u32[]{:S(2)}) collective-permute-start(bf16[256,1024]{1,0:T(8,128)(2,1)} %collective-permute-done.13), channel_id=1, source_target_pairs={{0,2},{2,4},{4,6},{1,3},{3,5},{5,7},{8,10},{10,12},{12,14},{9,11},... | collective-permute-start | bytes 1572872 | tf_op jit(solution)/shard_map/ppermute | solution.py:54
  99.8 23.0 %collective-permute-start.20 = (bf16[256,1024]{1,0:T(8,128)(2,1)}, bf16[256,1024]{1,0:T(8,128)(2,1)}, u32[]{:S(2)}, u32[]{:S(2)}) collective-permute-start(bf16[256,1024]{1,0:T(8,128)(2,1)} %collective-permute-done.14), channel_id=1, source_target_pairs={{2,0},{4,2},{6,4},{3,1},{5,3},{7,5},{10,8},{12,10},{14,12},{11,9},... | collective-permute-start | bytes 1572872 | tf_op jit(solution)/shard_map/ppermute | solution.py:55
  123.3 31.3 %collective-permute-start.29 = (bf16[4,144,1024]{2,1,0:T(8,128)(2,1)}, bf16[4,144,1024]{2,1,0:T(8,128)(2,1)S(1)}, u32[]{:S(2)}, u32[]{:S(2)}) collective-permute-start(bf16[4,144,1024]{2,1,0:T(8,128)(2,1)} %dynamic-slice_bitcast_fusion.2), channel_id=1, source_target_pairs={{0,16},{16,0},{1,17},{17,1},{2,18},{18,2},{3,19},{19,3},{4,20},{20... | collective-permute-start | bytes 3538952 | tf_op jit(solution)/shard_map/ppermute | solution.py:45
  124.8 20.3 %collective-permute-start.25 = (bf16[256,1024]{1,0:T(8,128)(2,1)}, bf16[256,1024]{1,0:T(8,128)(2,1)S(1)}, u32[]{:S(2)}, u32[]{:S(2)}) collective-permute-start(bf16[256,1024]{1,0:T(8,128)(2,1)} %collective-permute-done.19), channel_id=1, source_target_pairs={{0,2},{2,4},{4,6},{1,3},{3,5},{5,7},{8,10},{10,12},{12,14},{9,11},... | collective-permute-start | bytes 1572872 | tf_op jit(solution)/shard_map/ppermute | solution.py:54
  129.4 15.7 %collective-permute-start.26 = (bf16[256,1024]{1,0:T(8,128)(2,1)}, bf16[256,1024]{1,0:T(8,128)(2,1)S(1)}, u32[]{:S(2)}, u32[]{:S(2)}) collective-permute-start(bf16[256,1024]{1,0:T(8,128)(2,1)} %collective-permute-done.20), channel_id=1, source_target_pairs={{2,0},{4,2},{6,4},{3,1},{5,3},{7,5},{10,8},{12,10},{14,12},{11,9},... | collective-permute-start | bytes 1572872 | tf_op jit(solution)/shard_map/ppermute | solution.py:55
  133.2 13.5 %collective-permute-start.24 = (bf16[256,1024]{1,0:T(8,128)(2,1)S(1)}, bf16[256,1024]{1,0:T(8,128)(2,1)S(1)}, u32[]{:S(2)}, u32[]{:S(2)}) collective-permute-start(bf16[256,1024]{1,0:T(8,128)(2,1)S(1)} %add.230), channel_id=1, source_target_pairs={{0,8},{8,0},{1,9},{9,1},{2,10},{10,2},{3,11},{11,3},{4,12},{12,4},... | collective-permute-start | bytes 1572872 | tf_op jit(solution)/shard_map/ppermute | solution.py:45
  141.0 47.8 %collective-permute-start.37 = (bf16[2,4,2,32,1152]{4,3,2,1,0:T(8,128)(2,1)}, bf16[2,4,2,32,1152]{4,3,2,1,0:T(8,128)(2,1)}, u32[]{:S(2)}, u32[]{:S(2)}) collective-permute-start(bf16[2,4,2,32,1152]{4,3,2,1,0:T(8,128)(2,1)} %dynamic-slice_bitcast_fusion.1), channel_id=1, source_target_pairs={{0,16},{16,0},{1,17},{17,1},{2,18},{18,2},{3,19},{19,3},{4,20},{20... | collective-permute-start | bytes 3538952 | tf_op jit(solution)/shard_map/ppermute | solution.py:45
  150.8 37.1 %collective-permute-start.27 = (bf16[256,1024]{1,0:T(8,128)(2,1)}, bf16[256,1024]{1,0:T(8,128)(2,1)}, u32[]{:S(2)}, u32[]{:S(2)}) collective-permute-start(bf16[256,1024]{1,0:T(8,128)(2,1)} %add.229), channel_id=1, source_target_pairs={{0,8},{8,0},{1,9},{9,1},{2,10},{10,2},{3,11},{11,3},{4,12},{12,4},... | collective-permute-start | bytes 1572872 | tf_op jit(solution)/shard_map/ppermute | solution.py:45
  171.1 21.3 %collective-permute-start.21 = (bf16[256,1024]{1,0:T(8,128)(2,1)}, bf16[256,1024]{1,0:T(8,128)(2,1)}, u32[]{:S(2)}, u32[]{:S(2)}) collective-permute-start(bf16[256,1024]{1,0:T(8,128)(2,1)} %get-tuple-element.167), channel_id=1, source_target_pairs={{0,1},{1,0},{2,3},{3,2},{4,5},{5,4},{6,7},{7,6},{8,9},{9,8},{10,11... | collective-permute-start | bytes 1572872 | tf_op jit(solution)/shard_map/ppermute | solution.py:45
  171.5 46.9 %collective-permute-start.40 = (bf16[2,4,2,32,1152]{4,3,2,1,0:T(8,128)(2,1)}, bf16[2,4,2,32,1152]{4,3,2,1,0:T(8,128)(2,1)}, u32[]{:S(2)}, u32[]{:S(2)}) collective-permute-start(bf16[2,4,2,32,1152]{4,3,2,1,0:T(8,128)(2,1)} %dynamic-slice_bitcast_fusion), channel_id=1, source_target_pairs={{0,16},{16,0},{1,17},{17,1},{2,18},{18,2},{3,19},{19,3},{4,20},{20... | collective-permute-start | bytes 3538952 | tf_op jit(solution)/shard_map/ppermute | solution.py:45
  172.2 18.6 %collective-permute-start.36 = (bf16[2,144,1024]{2,1,0:T(8,128)(2,1)S(1)}, bf16[2,144,1024]{2,1,0:T(8,128)(2,1)S(1)}, u32[]{:S(2)}, u32[]{:S(2)}) collective-permute-start(bf16[2,144,1024]{2,1,0:T(8,128)(2,1)S(1)} %dynamic-slice_bitcast_fusion.3), channel_id=1, source_target_pairs={{0,2},{2,0},{4,6},{6,4},{1,3},{3,1},{5,7},{7,5},{8,10},{10,8},{12,... | collective-permute-start | bytes 1769480 | tf_op jit(solution)/shard_map/ppermute | solution.py:49
  187.9 29.6 %collective-permute-start.44 = (bf16[2,4,2,32,512]{4,3,2,1,0:T(8,128)(2,1)}, bf16[2,4,2,32,512]{4,3,2,1,0:T(8,128)(2,1)S(1)}, u32[]{:S(2)}, u32[]{:S(2)}) collective-permute-start(bf16[2,4,2,32,512]{4,3,2,1,0:T(8,128)(2,1)} %dynamic-slice_bitcast_fusion.4), channel_id=1, source_target_pairs={{0,8},{8,0},{1,9},{9,1},{2,10},{10,2},{3,11},{11,3},{4,12},{12,4},... | collective-permute-start | bytes 1572872 | tf_op jit(solution)/shard_map/ppermute | solution.py:45
  190.4 20.9 %collective-permute-start.39 = (bf16[2,2,2,32,1152]{4,3,1,2,0:T(8,128)(2,1)S(1)}, bf16[2,2,2,32,1152]{4,3,1,2,0:T(8,128)(2,1)S(1)}, u32[]{:S(2)}, u32[]{:S(2)}) collective-permute-start(bf16[2,2,2,32,1152]{4,3,1,2,0:T(8,128)(2,1)S(1)} %bitcast.156), channel_id=1, source_target_pairs={{0,2},{2,0},{4,6},{6,4},{1,3},{3,1},{5,7},{7,5},{8,10},{10,8},{12,... | collective-permute-start | bytes 1769480 | tf_op jit(solution)/shard_map/ppermute | solution.py:49
  190.9 19.1 %collective-permute-start.38 = (bf16[1,144,1024]{2,1,0:T(8,128)(2,1)S(1)}, bf16[1,144,1024]{2,1,0:T(8,128)(2,1)S(1)}, u32[]{:S(2)}, u32[]{:S(2)}) collective-permute-start(bf16[1,144,1024]{2,1,0:T(8,128)(2,1)S(1)} %constant_dynamic-slice_fusion.6), channel_id=1, source_target_pairs={{0,4},{2,6},{4,0},{6,2},{1,5},{3,7},{5,1},{7,3},{8,12},{10,14},{12... | collective-permute-start | bytes 884744 | tf_op jit(solution)/shard_map/ppermute | solution.py:49
  213.2 21.7 %collective-permute-start.42 = (bf16[512,256]{1,0:T(8,128)(2,1)}, bf16[512,256]{1,0:T(8,128)(2,1)}, u32[]{:S(2)}, u32[]{:S(2)}) collective-permute-start(bf16[512,256]{1,0:T(8,128)(2,1)} %get-tuple-element.215), channel_id=1, source_target_pairs={{0,4},{2,6},{4,0},{6,2},{1,5},{3,7},{5,1},{7,3},{8,12},{10,14},{12... | collective-permute-start | bytes 786440 | tf_op jit(solution)/shard_map/ppermute | solution.py:49
  214.5 20.5 %collective-permute-start.43 = (bf16[512,256]{1,0:T(8,128)(2,1)}, bf16[512,256]{1,0:T(8,128)(2,1)}, u32[]{:S(2)}, u32[]{:S(2)}) collective-permute-start(bf16[512,256]{1,0:T(8,128)(2,1)} %get-tuple-element.216), channel_id=1, source_target_pairs={{0,6},{2,4},{4,2},{6,0},{1,7},{3,5},{5,3},{7,1},{8,14},{10,12},{12... | collective-permute-start | bytes 786440 | tf_op jit(solution)/shard_map/ppermute | solution.py:49
  225.6 19.9 %collective-permute-start.45 = (bf16[560,256]{1,0:T(8,128)(2,1)S(1)}, bf16[560,256]{1,0:T(8,128)(2,1)S(1)}, u32[]{:S(2)}, u32[]{:S(2)}) collective-permute-start(bf16[560,256]{1,0:T(8,128)(2,1)S(1)} %pad_maximum_fusion.1), channel_id=1, source_target_pairs={{0,8},{8,0},{1,9},{9,1},{2,10},{10,2},{3,11},{11,3},{4,12},{12,4},... | collective-permute-start | bytes 860168 | tf_op jit(solution)/shard_map/ppermute | solution.py:45
  229.0 19.9 %collective-permute-start.48 = (bf16[2,2,2,32,1152]{4,3,1,2,0:T(8,128)(2,1)S(1)}, bf16[2,2,2,32,1152]{4,3,1,2,0:T(8,128)(2,1)S(1)}, u32[]{:S(2)}, u32[]{:S(2)}) collective-permute-start(bf16[2,2,2,32,1152]{4,3,1,2,0:T(8,128)(2,1)S(1)} %bitcast.155), channel_id=1, source_target_pairs={{0,2},{2,0},{4,6},{6,4},{1,3},{3,1},{5,7},{7,5},{8,10},{10,8},{12,... | collective-permute-start | bytes 1769480 | tf_op jit(solution)/shard_map/ppermute | solution.py:49
  239.0 32.5 %collective-permute-start.46 = (bf16[256,1024]{1,0:T(8,128)(2,1)S(1)}, bf16[256,1024]{1,0:T(8,128)(2,1)S(1)}, u32[]{:S(2)}, u32[]{:S(2)}) collective-permute-start(bf16[256,1024]{1,0:T(8,128)(2,1)S(1)} %get-tuple-element.234), channel_id=1, source_target_pairs={{0,1},{1,0},{2,3},{3,2},{4,5},{5,4},{6,7},{7,6},{8,9},{9,8},{10,11... | collective-permute-start | bytes 1572872 | tf_op jit(solution)/shard_map/ppermute | solution.py:45
  239.1 26.0 %collective-permute-start.53 = (bf16[1,2,2,32,1152]{4,3,1,2,0:T(8,128)(2,1)S(1)}, bf16[1,2,2,32,1152]{4,3,1,2,0:T(8,128)(2,1)S(1)}, u32[]{:S(2)}, u32[]{:S(2)}) collective-permute-start(bf16[1,2,2,32,1152]{4,3,1,2,0:T(8,128)(2,1)S(1)} %copy-done.60), channel_id=1, source_target_pairs={{0,4},{2,6},{4,0},{6,2},{1,5},{3,7},{5,1},{7,3},{8,12},{10,14},{12... | collective-permute-start | bytes 884744 | tf_op jit(solution)/shard_map/ppermute | solution.py:49
  244.7 33.5 %collective-permute-start.59 = (bf16[144,1024]{1,0:T(8,128)(2,1)S(1)}, bf16[144,1024]{1,0:T(8,128)(2,1)S(1)}, u32[]{:S(2)}, u32[]{:S(2)}) collective-permute-start(bf16[144,1024]{1,0:T(8,128)(2,1)S(1)} %bitcast.158), channel_id=1, source_target_pairs={{0,0},{1,8},{2,2},{3,10},{4,4},{5,12},{6,6},{7,14},{8,16},{9,24},{... | collective-permute-start | bytes 884744 | tf_op jit(solution)/shard_map/ppermute | solution.py:835
  245.7 25.6 %collective-permute-start.47 = (bf16[272,768]{1,0:T(8,128)(2,1)S(1)}, bf16[272,768]{1,0:T(8,128)(2,1)S(1)}, u32[]{:S(2)}, u32[]{:S(2)}) collective-permute-start(bf16[272,768]{1,0:T(8,128)(2,1)S(1)} %maximum_maximum_fusion), channel_id=1, source_target_pairs={{0,16},{16,0},{1,17},{17,1},{2,18},{18,2},{3,19},{19,3},{4,20},{20... | collective-permute-start | bytes 1253384 | tf_op jit(solution)/shard_map/ppermute | solution.py:45
  248.9 22.3 %collective-permute-start.56 = (bf16[1,2,2,32,1152]{4,3,1,2,0:T(8,128)(2,1)S(1)}, bf16[1,2,2,32,1152]{4,3,1,2,0:T(8,128)(2,1)S(1)}, u32[]{:S(2)}, u32[]{:S(2)}) collective-permute-start(bf16[1,2,2,32,1152]{4,3,1,2,0:T(8,128)(2,1)S(1)} %constant_dynamic-slice_fusion.1), channel_id=1, source_target_pairs={{0,4},{2,6},{4,0},{6,2},{1,5},{3,7},{5,1},{7,3},{8,12},{10,14},{12... | collective-permute-start | bytes 884744 | tf_op jit(solution)/shard_map/ppermute | solution.py:49
  271.3 13.6 %collective-permute-start.57 = (bf16[2,32,1152]{2,1,0:T(8,128)(2,1)S(1)}, bf16[2,32,1152]{2,1,0:T(8,128)(2,1)S(1)}, u32[]{:S(2)}, u32[]{:S(2)}) collective-permute-start(bf16[2,32,1152]{2,1,0:T(8,128)(2,1)S(1)} %dynamic-slice_bitcast_fusion.6), channel_id=1, source_target_pairs={{0,1},{1,0},{2,3},{3,2},{4,5},{5,4},{6,7},{7,6},{8,9},{9,8},{10,11... | collective-permute-start | bytes 442376 | tf_op jit(solution)/shard_map/ppermute | solution.py:45
  (92 other events, 994.9 us)
